TPU v7x, 256 devices: a whole 4x4x8 slice. The times are simulated.
256 devices in a mesh: row: 8 (over x, core), col: 32 (over y, z).
Axes of the slice: x: 4, y: 4, z: 8, core: 2. Of those that a mesh axis runs over, the one named last changes fastest.
Arguments:
- grad: bfloat16 [1024, 73728], P('row', 'col'), may hold values from -180 to 180
- weight: bfloat16 [1024, 73728], P('row', 'col'), may hold values from -6 to 6
- residual: bfloat16 [1024, 73728], P('row', 'col'), may hold values from -0.0038909912 to 0.0038909912
- row_state: float32 [1024], P('row'), may hold values from 0.01 to 0.5
- col_state: float32 [73728], P('col'), may hold values from 0.01 to 0.5
- out_grad: bfloat16 [2048, 73728], P('col'), may hold values from -0.0234375 to 0.0234375
Outputs:
- new_weight: bfloat16 [1024, 73728], P('row', 'col')
- row_out: float32 [1024], P('row')
- col_out: float32 [73728], P('col')
- input_grad: bfloat16 [2048, 1024], P('col', 'row')
All inputs are finite; a program needn't handle non-finite values.
Results may differ from a plain program's by a relative error of at most 0.0014.
The roundings to bfloat16 on the way count: a program that leaves them out, or rounds other values in their place, can miss the bound.
Values may be sent and summed in bfloat16 or wider, within the bound.
No kernel may reach another device: no remote copies, remote signals or barrier semaphores. Data moves between devices by JAX's collectives and lax.ppermute only.
A program may use at most 128 MiB of HBM per device.

v0:
```python
import jax
import jax.numpy as jnp
from jax import lax
from jax.sharding import PartitionSpec as P

decay_rate = 0.9
step_size = 0.05
clip_level = 1.0
tiny_square = 1e-30


def body(grad, weight, residual, row_state, col_state, out_grad):
    grad_full = grad.astype(jnp.float32)
    squares = grad_full * grad_full + tiny_square
    col_total = lax.psum(jnp.sum(squares, axis=0), "row")
    all_rows = grad.shape[0] * lax.axis_size("row")
    all_cols = grad.shape[1] * lax.axis_size("col")
    col_out = decay_rate * col_state + (1.0 - decay_rate) * col_total / all_rows
    row_part = jnp.sum(squares, axis=1)
    row_total = lax.psum(row_part, "col")
    row_out = decay_rate * row_state + (1.0 - decay_rate) * row_total / all_cols
    scaled = grad_full * lax.rsqrt(row_out[:, None] * col_out[None, :])
    master = weight.astype(jnp.float32) + residual.astype(jnp.float32)
    upd_square, w_square = lax.psum(
        (jnp.sum(scaled * scaled), jnp.sum(master * master)), ("row", "col")
    )
    entries = all_rows * all_cols
    upd_rms = jnp.sqrt(upd_square / entries)
    w_rms = jnp.sqrt(w_square / entries)
    factor = step_size * w_rms / jnp.maximum(1.0, upd_rms / clip_level)
    full = master - factor * scaled
    new_weight = full.astype(jnp.bfloat16)
    summed = lax.dot_general(
        out_grad,
        lax.all_gather(new_weight, "col", axis=1, tiled=True),
        (((1,), (1,)), ((), ())),
        preferred_element_type=jnp.float32,
    )
    input_grad = summed.astype(jnp.bfloat16)
    return (new_weight, row_out, col_out, input_grad)


def solution(mesh):
    in_specs = (
        P("row", "col"),
        P("row", "col"),
        P("row", "col"),
        P("row"),
        P("col"),
        P("col", None),
    )
    out_specs = (P("row", "col"), P("row"), P("col"), P("col", "row"))
    return jax.shard_map(body, mesh=mesh, in_specs=in_specs, out_specs=out_specs, check_vma=False)
```

profile of v0, /device:TPU:1, one launch (start us, length us, event | category | flops | bytes accessed | tf_op | source)
XLA Modules:
  0.0 354.0 jit_solution(14071920591395877674)
XLA Ops:
  7.2 0.0 copy-start
  7.2 0.0 copy-start.1
  7.2 0.0 copy-start.2
  7.2 0.0 copy-start.6
  7.2 0.0 copy-start.4
  7.2 0.0 all-gather.2.cloned.1.call-start
  7.3 1.4 fusion.2
  8.7 64.6 %psum.29 = f32[128]{0:T(128)S(1)} all-reduce(f32[128]{0:T(128)S(1)} %get-tuple-element.4), channel_id=1, replica_groups=mesh['row'=8,'col'=32] {'col'}, use_global_device_ids=true, to_apply=%region_3.0 | all-reduce | flops 128 | bytes 1024 | tf_op jit(solution)/shard_map/psum | solution.py:20
  73.3 34.8 %psum.30 = f32[2304]{0:T(1024)S(1)} all-reduce(f32[2304]{0:T(1024)S(1)} %get-tuple-element.5), channel_id=1, replica_groups=mesh['row'=8,'col'=32] {'row'}, use_global_device_ids=true, to_apply=%region_5.0 | all-reduce | flops 2304 | bytes 18432 | tf_op jit(solution)/shard_map/psum | solution.py:15
  108.1 2.2 multiply_reduce_fusion.1
  110.3 0.0 copy-done.6
  110.3 0.0 copy-done.4
  110.3 0.0 copy-start.5
  110.3 0.0 copy-done
  110.3 0.0 copy-start.3
  110.4 1.1 multiply_reduce_fusion
  111.5 74.0 %all-reduce = (f32[]{:T(128)}, f32[]{:T(128)}) all-reduce(f32[]{:T(128)} %multiply_reduce_fusion.1, f32[]{:T(128)} %multiply_reduce_fusion), channel_id=1, replica_groups=mesh['row'=8,'col'=32] {'row','col'}, use_global_device_ids=true, to_apply=%region_1.0 | all-reduce | flops 2 | bytes 16 | tf_op jit(solution)/shard_map/psum | solution.py:24
  186.9 0.0 copy-done.1
  186.9 0.0 copy-done.2
  187.0 1.2 subtract_convert_fusion
  188.2 0.0 copy-done.5
  188.2 0.0 all-gather.2.cloned.1.call-update
  188.2 145.9 %all-gather.2.cloned.1.call-done = bf16[128,73728]{1,0:T(8,128)(2,1)} async-done(((bf16[128,2304]{1,0:T(8,128)(2,1)}), bf16[128,73728]{1,0:T(8,128)(2,1)}) %all-gather.2.cloned.1.call-update) | async-done | bytes 18874384 | tf_op jit(solution)/shard_map/all_gather | solution.py:35
  334.1 13.0 %fusion.3 = bf16[64,128]{1,0:T(8,128)(2,1)} fusion(bf16[128,73728]{1,0:T(8,128)(2,1)} %all-gather.2.cloned.1.call-done, bf16[64,73728]{1,0:T(8,128)(2,1)} %param.11), kind=kOutput, calls=%fused_computation.10 | convolution fusion | flops 1207967744 | bytes 28327936 | tf_op jit(solution)/shard_map/dot_general | solution.py:33
  (3 shorter events, 0.0 us)
Async XLA Ops:
  7.2 103.2 %copy-start = (bf16[128,2304]{1,0:T(8,128)(2,1)S(1)}, bf16[128,2304]{1,0:T(8,128)(2,1)}, u32[]{:S(2)}) copy-start(bf16[128,2304]{1,0:T(8,128)(2,1)} %param.6) | copy-start | bytes 1769476
  7.2 179.8 %copy-start.1 = (bf16[128,2304]{1,0:T(8,128)(2,1)S(1)}, bf16[128,2304]{1,0:T(8,128)(2,1)}, u32[]{:S(2)}) copy-start(bf16[128,2304]{1,0:T(8,128)(2,1)} %param.8) | copy-start | bytes 1769476
  7.2 179.8 %copy-start.2 = (bf16[128,2304]{1,0:T(8,128)(2,1)S(1)}, bf16[128,2304]{1,0:T(8,128)(2,1)}, u32[]{:S(2)}) copy-start(bf16[128,2304]{1,0:T(8,128)(2,1)} %param.7) | copy-start | bytes 1769476
  7.2 103.1 %copy-start.6 = (f32[128]{0:T(128)S(1)}, f32[128]{0:T(128)}, u32[]{:S(2)}) copy-start(f32[128]{0:T(128)} %param.9) | copy-start | bytes 1540
  7.2 103.1 %copy-start.4 = (f32[2304]{0:T(1024)S(1)}, f32[2304]{0:T(1024)}, u32[]{:S(2)}) copy-start(f32[2304]{0:T(1024)} %param.10) | copy-start | bytes 27652
  7.2 326.9 %all-gather.2.cloned.1.call-start = ((), (), s32[]{:S(2)}) async-start(), calls=%async_computation | async-start | bytes 19464192 | tf_op jit(solution)/shard_map/all_gather | solution.py:35
  110.3 77.9 %copy-start.5 = (f32[128]{0:T(128)}, f32[128]{0:T(128)S(1)}, u32[]{:S(2)}) copy-start(f32[128]{0:T(128)S(1)} %multiply_add_fusion.1) | copy-start | bytes 1540
  110.3 77.8 %copy-start.3 = (f32[2304]{0:T(1024)}, f32[2304]{0:T(1024)S(1)}, u32[]{:S(2)}) copy-start(f32[2304]{0:T(1024)S(1)} %multiply_add_fusion) | copy-start | bytes 27652
Sparse Core Ops, SparseCore 0:
  188.3 145.6 all-gather.1
where the time goes:
time: 354 us
  blocking collectives  173 us (49%)
  waiting for transfers between devices  146 us (41%)
  between operations  15.5 us (4%)
  matrix products  13 us (4%)
  other arithmetic  5.96 us (2%)
    all_gather x1, waiting for transfers between devices, body(): lax.all_gather(new_weight, 'col', axis=1, tiled=True)  146 us
    psum x1, blocking collectives, body(): lax.psum((jnp.sum(scaled * scaled), jnp.sum(master * master)), ('row', 'c...  74 us
    psum x1, blocking collectives, body(): row_total = lax.psum(row_part, 'col')  64.6 us
    psum x1, blocking collectives, body(): col_total = lax.psum(jnp.sum(squares, axis=0), 'row')  34.8 us
    dot_general x1, matrix products, body(): lax.dot_general(out_grad, lax.all_gather(new_weight, 'col', axis=1, tiled...  13 us
  transfers between devices with their start and end apart: 1, of which 1 were waited for; matrix products, arithmetic and copies ran while one was open for 0% of the time, Pallas kernels for 0%

commit v1 on v0

v1 whole, which is shorter than its diff:
```python
import jax
import jax.numpy as jnp
from jax import lax
from jax.sharding import Mesh, PartitionSpec as P

decay_rate = 0.9
step_size = 0.05
clip_level = 1.0
tiny_square = 1e-30
ROW = ("x", "core")
COL = ("y", "z")


def spread_sum(value, axes, count):
    copies = jnp.broadcast_to(value[None], (count,) + value.shape)
    return jnp.sum(lax.all_to_all(copies, axes, 0, 0, tiled=True), axis=0)


def body(grad, weight, residual, row_state, col_state, out_grad):
    rows, cols = grad.shape
    tokens = out_grad.shape[0]
    n_row, n_y, n_z = lax.axis_size(ROW), lax.axis_size("y"), lax.axis_size("z")
    n_col = n_y * n_z
    all_rows, all_cols = rows * n_row, cols * n_col
    part = tokens // n_row

    me = lax.axis_index(ROW)
    share = lax.dynamic_slice_in_dim(out_grad, me * part, part, 0)
    share = share.reshape(part, n_y, n_z, cols).transpose(2, 1, 0, 3)
    share = lax.all_to_all(share, "z", 0, 0, tiled=True)
    tokens_in = lax.all_gather(share, ROW, axis=0)

    grad_full = grad.astype(jnp.float32)
    squares = grad_full * grad_full + tiny_square
    col_part = jnp.sum(squares, axis=0).reshape(cols // 128, 128)
    col_total = spread_sum(col_part, ROW, n_row).reshape(cols)
    col_out = decay_rate * col_state + (1.0 - decay_rate) * col_total / all_rows
    master = weight.astype(jnp.float32) + residual.astype(jnp.float32)
    row_part = jnp.sum(squares, axis=1)
    scaled_part = jnp.sum(grad_full * grad_full * (1.0 / col_out)[None, :], axis=1)
    w_part = jnp.sum(master * master, axis=1)
    sums = jnp.concatenate([row_part[None], scaled_part[None], w_part[None], jnp.zeros((5, rows), jnp.float32)])
    sums = spread_sum(sums, COL, n_col)
    row_out = decay_rate * row_state + (1.0 - decay_rate) * sums[0] / all_cols
    upd_part = jnp.sum(sums[1] / row_out)
    w_part = jnp.sum(sums[2])
    pair = jnp.concatenate([jnp.full((4, 128), upd_part), jnp.full((4, 128), w_part)])
    pair = spread_sum(pair, ROW, n_row)
    entries = all_rows * all_cols
    upd_rms = jnp.sqrt(pair[0, 0] / entries)
    w_rms = jnp.sqrt(pair[4, 0] / entries)
    factor = step_size * w_rms / jnp.maximum(1.0, upd_rms / clip_level)
    scaled = grad_full * lax.rsqrt(row_out[:, None] * col_out[None, :])
    new_weight = (master - factor * scaled).astype(jnp.bfloat16)
    around = lax.all_gather(new_weight, "y", axis=0)

    total = 0.0
    for i in range(n_y):
        total += lax.dot_general(tokens_in[:, :, i], around[i], (((3,), (1,)), ((), ())), preferred_element_type=jnp.float32)
    total = total.transpose(1, 0, 2, 3).reshape(n_z, tokens, rows)
    total = lax.all_to_all(total, "z", 0, 0, tiled=True)
    input_grad = jnp.sum(total, axis=0).astype(jnp.bfloat16)
    return (new_weight, row_out, col_out, input_grad)


def solution(mesh):
    fine = Mesh(mesh.devices.reshape(4, 2, 4, 8), ("x", "core", "y", "z"))
    in_specs = (P(ROW, COL), P(ROW, COL), P(ROW, COL), P(ROW), P(COL), P(COL, None))
    out_specs = (P(ROW, COL), P(ROW), P(COL), P(COL, ROW))
    return jax.shard_map(body, mesh=fine, in_specs=in_specs, out_specs=out_specs, check_vma=False)
```

time: 354 us -> 178 us (0.50)
  waiting for transfers between devices: 146 us -> 48.2 us
  blocking collectives: 173 us -> 79.5 us
  local copies, waits for them, and re-layouts: 0.04 us -> 12.8 us
  starting transfers between devices: 0.04 us -> 6.44 us
    psum x3 -> x0, blocking collectives: 173 us -> none  [the longest x1 74 us: body(): lax.psum((jnp.sum(scaled * scaled), jnp.sum(master * master)), ('row', 'c...]
    all_gather x1 -> x2, waiting for transfers between devices: 146 us -> 43.6 us  [the longest x1 29.9 us: body(): around = lax.all_gather(new_weight, 'y', axis=0)]
    all_to_all x0 -> x4, blocking collectives: none -> 79.5 us  [the longest x1 39.4 us: body(): share = lax.all_to_all(share, 'z', 0, 0, tiled=True)]
    all_gather x0 -> x1, local copies, waits for them, and re-layouts: none -> 7.94 us  [body(): tokens_in = lax.all_gather(share, ROW, axis=0)]
    all_to_all x0 -> x1, starting transfers between devices: none -> 6.4 us  [spread_sum(): return jnp.sum(lax.all_to_all(copies, axes, 0, 0, tiled=True), axis=0)]
    all_to_all x0 -> x1, waiting for transfers between devices: none -> 4.59 us  [spread_sum(): return jnp.sum(lax.all_to_all(copies, axes, 0, 0, tiled=True), axis=0)]
    dot_general x1 -> x4, matrix products: 13 us -> 10.1 us  [body(): lax.dot_general(tokens_in[:, :, i], around[i], (((3,), (1,)), ((), ())),...]
  transfers between devices with their start and end apart: 1 -> 3, of which waited for: 1 -> 3; matrix products, arithmetic and copies ran while one was open for 0% -> 8% of each run, Pallas kernels for 0% -> 0%
where the time goes in v1:
time: 178 us; the launch traced here: 177 us
  blocking collectives  79.5 us (45%)
  waiting for transfers between devices  48.2 us (27%)
  between operations  15.6 us (9%)
  local copies, waits for them, and re-layouts  12.8 us (7%)
  matrix products  10.1 us (6%)
  starting transfers between devices  6.44 us (4%)
  other arithmetic  3.99 us (2%)
    all_to_all x1, blocking collectives, body(): share = lax.all_to_all(share, 'z', 0, 0, tiled=True)  39.4 us
    all_gather x1, waiting for transfers between devices, body(): around = lax.all_gather(new_weight, 'y', axis=0)  29.9 us
    all_to_all x2, blocking collectives, spread_sum(): return jnp.sum(lax.all_to_all(copies, axes, 0, 0, tiled=True), axis=0)  23.1 us
    all_to_all x1, blocking collectives, body(): total = lax.all_to_all(total, 'z', 0, 0, tiled=True)  17 us
    all_gather x1, waiting for transfers between devices, body(): tokens_in = lax.all_gather(share, ROW, axis=0)  13.7 us
    dot_general x4, matrix products, body(): lax.dot_general(tokens_in[:, :, i], around[i], (((3,), (1,)), ((), ())),...  10.1 us
    all_gather x1, local copies, waits for them, and re-layouts, body(): tokens_in = lax.all_gather(share, ROW, axis=0)  7.94 us
    all_to_all x1, starting transfers between devices, spread_sum(): return jnp.sum(lax.all_to_all(copies, axes, 0, 0, tiled=True), axis=0)  6.4 us
  transfers between devices with their start and end apart: 3, of which 3 were waited for; matrix products, arithmetic and copies ran while one was open for 8% of the time, Pallas kernels for 0%

profile of v1, /device:TPU:1, one launch (start us, length us, event | category | flops | bytes accessed | tf_op | source)
XLA Modules:
  0.0 176.7 jit_solution(16184037126099846003)
XLA Ops:
  7.2 1.4 constant_dynamic-slice_fusion
  8.8 0.7 copy.23
  9.5 39.4 %all_to_all.25 = bf16[8,4,8,2304]{3,2,1,0:T(8,128)(2,1)} all-to-all(bf16[8,4,8,2304]{3,2,1,0:T(8,128)(2,1)S(1)} %copy.23), channel_id=1, replica_groups=mesh['x'=4,'core'=2,'y'=4,'z'=8] {'z'}, dimensions={0} | all-to-all | bytes 2359296 | tf_op jit(solution)/shard_map/all_to_all | solution.py:30
  49.2 0.6 broadcast_in_dim.40
  49.9 6.4 %all-to-all-start = ((f32[8,18,128]{2,1,0:T(8,128)}), f32[8,18,128]{2,1,0:T(8,128)S(1)}, u32[]{:S(2)}, u32[]{:S(2)}) async-start(f32[8,18,128]{2,1,0:T(8,128)} %broadcast_in_dim.40), calls=%async_computation | async-start | bytes 196608 | tf_op jit(solution)/shard_map/all_to_all | solution.py:16
  56.3 0.3 multiply_reduce_fusion
  56.7 4.6 %all-to-all-done = f32[8,18,128]{2,1,0:T(8,128)S(1)} async-done(((f32[8,18,128]{2,1,0:T(8,128)}), f32[8,18,128]{2,1,0:T(8,128)S(1)}, u32[]{:S(2)}, u32[]{:S(2)}) %all-to-all-start) | async-done | bytes 73760 | tf_op jit(solution)/shard_map/all_to_all | solution.py:16
  61.6 13.5 %all_to_all.26 = f32[32,8,128]{2,1,0:T(8,128)S(1)} all-to-all(f32[32,8,128]{2,1,0:T(8,128)S(1)} %broadcast_in_dim.44), channel_id=1, replica_groups=mesh['x'=4,'core'=2,'y'=4,'z'=8] {'y','z'}, dimensions={0} | all-to-all | bytes 262144 | tf_op jit(solution)/shard_map/all_to_all | solution.py:16
  75.2 0.6 slice_reduce_fusion
  75.8 0.6 fusion.16
  76.4 0.6 broadcast_in_dim.45
  77.1 0.7 concatenate.7
  77.8 9.6 %all_to_all.27 = f32[8,8,128]{2,1,0:T(8,128)S(1)} all-to-all(f32[8,8,128]{2,1,0:T(8,128)S(1)} %broadcast_in_dim.46), channel_id=1, replica_groups=mesh['x'=4,'core'=2,'y'=4,'z'=8] {'x','core'}, dimensions={0} | all-to-all | bytes 65536 | tf_op jit(solution)/shard_map/all_to_all | solution.py:16
  87.4 0.5 fusion.17
  89.3 1.2 fusion.11
  90.6 13.7 %all-gather.5.cloned.1.call-done = bf16[64,4,8,2304]{3,2,1,0:T(8,128)(2,1)} async-done(((bf16[8,4,8,2304]{3,2,1,0:T(8,128)(2,1)}), bf16[64,4,8,2304]{3,2,1,0:T(8,128)(2,1)}) %all-gather.5.cloned.1.call-update) | async-done | bytes 9437200 | tf_op jit(solution)/shard_map/all_gather | solution.py:31
  104.3 7.9 %copy.24 = bf16[64,4,8,2304]{3,2,0,1:T(8,128)(2,1)} copy(bf16[64,4,8,2304]{3,2,1,0:T(8,128)(2,1)} %all-gather.5.cloned.1.call-done) | data formatting | bytes 18874368 | tf_op jit(solution)/shard_map/all_gather | solution.py:31
  112.2 29.9 %all-gather.7.cloned.1.call-done = bf16[512,2304]{1,0:T(8,128)(2,1)} async-done(((bf16[128,2304]{1,0:T(8,128)(2,1)}), bf16[512,2304]{1,0:T(8,128)(2,1)}) %all-gather.7.cloned.1.call-update) | async-done | bytes 2359312 | tf_op jit(solution)/shard_map/all_gather | solution.py:55
  142.2 2.7 %fusion.2 = f32[8,8,8,128]{3,2,1,0:T(8,128)S(1)} fusion(bf16[8,8,4,8,2304]{4,3,1,0,2:T(8,128)(2,1)} %bitcast.69, bf16[512,2304]{1,0:T(8,128)(2,1)} %all-gather.7.cloned.1.call-done), kind=kOutput, calls=%fused_computation.5 | convolution fusion | flops 301989888 | bytes 3211264 | tf_op jit(solution)/shard_map/dot_general | solution.py:59
  144.9 2.5 %fusion.12 = f32[8,8,8,128]{3,2,1,0:T(8,128)S(1)} fusion(f32[8,8,8,128]{3,2,1,0:T(8,128)S(1)} %fusion.2, bf16[8,8,4,8,2304]{4,3,1,0,2:T(8,128)(2,1)} %bitcast.70, bf16[512,2304]{1,0:T(8,128)(2,1)S(1)} %copy-done.7), kind=kOutput, calls=%fused_computation.21 | convolution fusion | flops 302055424 | bytes 3473408 | tf_op jit(solution)/shard_map/dot_general | solution.py:59
  147.3 2.5 %fusion.13 = f32[8,8,8,128]{3,2,1,0:T(8,128)S(1)} fusion(f32[8,8,8,128]{3,2,1,0:T(8,128)S(1)} %fusion.12, bf16[8,8,4,8,2304]{4,3,1,0,2:T(8,128)(2,1)} %bitcast.71, bf16[512,2304]{1,0:T(8,128)(2,1)S(1)} %copy-done.7), kind=kOutput, calls=%fused_computation.22 | convolution fusion | flops 302055424 | bytes 3473408 | tf_op jit(solution)/shard_map/dot_general | solution.py:59
  149.8 2.5 %fusion.15 = f32[8,8,8,128]{3,2,0,1:T(8,128)S(1)} fusion(f32[8,8,8,128]{3,2,1,0:T(8,128)S(1)} %fusion.13, bf16[8,8,4,8,2304]{4,3,1,0,2:T(8,128)(2,1)} %bitcast.72, bf16[512,2304]{1,0:T(8,128)(2,1)S(1)} %copy-done.7), kind=kOutput, calls=%fused_computation.24 | convolution fusion | flops 302055424 | bytes 3473408 | tf_op jit(solution)/shard_map/dot_general | solution.py:59
  152.3 17.0 %all_to_all.28 = f32[8,64,128]{2,1,0:T(8,128)S(1)} all-to-all(f32[8,64,128]{2,1,0:T(8,128)S(1)} %bitcast.75), channel_id=1, replica_groups=mesh['x'=4,'core'=2,'y'=4,'z'=8] {'z'}, dimensions={0} | all-to-all | bytes 524288 | tf_op jit(solution)/shard_map/all_to_all | solution.py:61
  169.3 0.6 reduce_sum.99
  (33 shorter events, 1.1 us)
Async XLA Ops:
  7.2 97.1 %all-gather.5.cloned.1.call-start = ((), (), s32[]{:S(2)}) async-start(), calls=%async_computation.5 | async-start | bytes 10616832 | tf_op jit(solution)/shard_map/all_gather | solution.py:31
  9.4 39.5 %copy-start = (bf16[128,2304]{1,0:T(8,128)(2,1)S(1)}, bf16[128,2304]{1,0:T(8,128)(2,1)}, u32[]{:S(2)}) copy-start(bf16[128,2304]{1,0:T(8,128)(2,1)} %param.6) | copy-start | bytes 1769476
  9.4 46.8 %copy-start.1 = (bf16[128,2304]{1,0:T(8,128)(2,1)S(1)}, bf16[128,2304]{1,0:T(8,128)(2,1)}, u32[]{:S(2)}) copy-start(bf16[128,2304]{1,0:T(8,128)(2,1)} %param.8) | copy-start | bytes 1769476
  9.5 46.8 %copy-start.2 = (bf16[128,2304]{1,0:T(8,128)(2,1)S(1)}, bf16[128,2304]{1,0:T(8,128)(2,1)}, u32[]{:S(2)}) copy-start(bf16[128,2304]{1,0:T(8,128)(2,1)} %param.7) | copy-start | bytes 1769476
  9.5 51.8 %copy-start.4 = (f32[2304]{0:T(1024)S(1)}, f32[2304]{0:T(1024)}, u32[]{:S(2)}) copy-start(f32[2304]{0:T(1024)} %param.10) | copy-start | bytes 27652
  48.9 26.9 %copy-start.6 = (f32[128]{0:T(128)S(1)}, f32[128]{0:T(128)}, u32[]{:S(2)}) copy-start(f32[128]{0:T(128)} %param.9) | copy-start | bytes 1540
  49.9 11.4 %all-to-all-start = ((f32[8,18,128]{2,1,0:T(8,128)}), f32[8,18,128]{2,1,0:T(8,128)S(1)}, u32[]{:S(2)}, u32[]{:S(2)}) async-start(f32[8,18,128]{2,1,0:T(8,128)} %broadcast_in_dim.40), calls=%async_computation | async-start | bytes 196608 | tf_op jit(solution)/shard_map/all_to_all | solution.py:16
  56.3 85.9 %all-gather.7.cloned.1.call-start = ((), (), s32[]{:S(2)}) async-start(), calls=%async_computation.6 | async-start | bytes 2949120 | tf_op jit(solution)/shard_map/all_gather | solution.py:55
  61.3 50.9 %copy-start.3 = (f32[2304]{0:T(1024)}, f32[2304]{0:T(1024)S(1)}, u32[]{:S(2)}) copy-start(f32[2304]{0:T(1024)S(1)} %get-tuple-element.9) | copy-start | bytes 27652
  76.4 35.8 %copy-start.5 = (f32[128]{0:T(128)}, f32[128]{0:T(128)S(1)}, u32[]{:S(2)}) copy-start(f32[128]{0:T(128)S(1)} %get-tuple-element.7) | copy-start | bytes 1540
  142.2 2.7 %copy-start.7 = (bf16[512,2304]{1,0:T(8,128)(2,1)S(1)}, bf16[512,2304]{1,0:T(8,128)(2,1)}, u32[]{:S(2)}) copy-start(bf16[512,2304]{1,0:T(8,128)(2,1)} %all-gather.7.cloned.1.call-done) | copy-start | bytes 7077892
Sparse Core Ops, SparseCore 0:
  49.1 55.1 all-gather.4
  106.7 35.4 all-gather.6

commit v2 on v1

v2 whole, which is shorter than its diff:
```python
import functools
import jax
import jax.numpy as jnp
from jax import lax
from jax.experimental import pallas as pl
from jax.experimental.pallas import tpu as pltpu
from jax.sharding import Mesh, PartitionSpec as P

decay_rate = 0.9
step_size = 0.05
clip_level = 1.0
tiny_square = 1e-30
ROW = ("x", "core")
COL = ("y", "z")


def shift(value, axis, by):
    n = lax.axis_size(axis)
    return lax.ppermute(value, axis, [(i, (i + by) % n) for i in range(n)])


def pair_sum(value, axis, bit):
    n = lax.axis_size(axis)
    return value + lax.ppermute(value, axis, [(i, i ^ bit) for i in range(n)])


def spread_sum(value, axis):
    copies = jnp.broadcast_to(value[None], (lax.axis_size(axis),) + value.shape)
    return jnp.sum(lax.all_to_all(copies, axis, 0, 0, tiled=True), axis=0)


def gather4(value, axis):
    return shift(value, axis, 1), shift(value, axis, -1)


def share_kernel(n_core, place, source, target, done):
    n_z, n_y, part, half = target.shape
    top = pl.multiple_of(place[0] * part, part)
    copies = []
    for j in range(n_y):
        for i in range(n_z):
            block = (place[2] + j) % n_y * n_z + i
            left = pl.multiple_of((block * n_core + place[1]) * half, 128)
            copy = pltpu.make_async_copy(source.at[pl.ds(top, part), pl.ds(left, half)], target.at[i, j], done.at[i, j])
            copy.start()
            copies.append(copy)
    for copy in copies:
        copy.wait()


def share_out(place, out_grad, n_z, n_y, part, half, n_core):
    shape = (n_z, n_y, part, half)
    return pl.pallas_call(
        functools.partial(share_kernel, n_core),
        out_shape=jax.ShapeDtypeStruct(shape, out_grad.dtype),
        grid_spec=pltpu.PrefetchScalarGridSpec(
            num_scalar_prefetch=1,
            grid=(1,),
            in_specs=[pl.BlockSpec(memory_space=pl.ANY)],
            out_specs=pl.BlockSpec(shape, lambda i, place: (0, 0, 0, 0)),
            scratch_shapes=[pltpu.SemaphoreType.DMA((n_z, n_y))],
        ),
        compiler_params=pltpu.CompilerParams(vmem_limit_bytes=56 * 1024 * 1024),
        cost_estimate=pl.CostEstimate(flops=0, bytes_accessed=4 * n_z * n_y * part * half, transcendentals=0),
    )(place, out_grad)


def update_kernel(entries, entry_cols, place, sums, state, col_out, grad, weight, residual, new_weight, row_out, kept, given):
    rows, half = kept.shape
    rows_out = decay_rate * state[...] + (1.0 - decay_rate) * sums[0:8] / entry_cols
    upd = jnp.sum(jnp.sum(sums[8:16] / rows_out, axis=0, keepdims=True), axis=1, keepdims=True)
    upd_rms = jnp.sqrt(upd / entries)
    w_rms = jnp.sqrt(jnp.sum(sums[16:17], axis=1, keepdims=True) / entries)
    factor = step_size * w_rms / jnp.maximum(1.0, upd_rms / clip_level)
    row_out[...] = rows_out[0:1]
    scale = factor * lax.rsqrt(jnp.transpose(jnp.broadcast_to(rows_out[0:1], (8, rows)))[:, :1])
    for target, at in ((kept, place[1]), (given, 1 - place[1])):
        part = pl.ds(pl.multiple_of(at * half, 128), half)
        master = weight[:, part].astype(jnp.float32) + residual[:, part].astype(jnp.float32)
        delta = grad[:, part].astype(jnp.float32) * (scale * lax.rsqrt(col_out[:, part]))
        new = (master - delta).astype(jnp.bfloat16)
        target[...] = new
        new_weight[:, part] = new


def update(place, entries, entry_cols, sums, state, col_out, arrays, half):
    rows, cols = arrays[0].shape
    whole = lambda shape: pl.BlockSpec(shape, lambda i, place: (0,) * len(shape))
    return pl.pallas_call(
        functools.partial(update_kernel, entries, entry_cols),
        out_shape=(
            jax.ShapeDtypeStruct((rows, cols), jnp.bfloat16),
            jax.ShapeDtypeStruct((1, rows), jnp.float32),
            jax.ShapeDtypeStruct((rows, half), jnp.bfloat16),
            jax.ShapeDtypeStruct((rows, half), jnp.bfloat16),
        ),
        grid_spec=pltpu.PrefetchScalarGridSpec(
            num_scalar_prefetch=1,
            grid=(1,),
            in_specs=[whole(sums.shape), whole(state.shape), whole((1, cols))] + [whole((rows, cols))] * 3,
            out_specs=[whole((rows, cols)), whole((1, rows)), whole((rows, half)), whole((rows, half))],
        ),
        compiler_params=pltpu.CompilerParams(vmem_limit_bytes=16 * 1024 * 1024),
    )(place, sums, state, col_out, *arrays)


def product_kernel(*refs):
    weights, tokens, (mine, other) = refs[:8], refs[8:-2], refs[-2:]
    n_z, _, part, rows = mine.shape
    n_y, half = tokens[0].shape[1], tokens[0].shape[3]
    total = 0.0
    for j in range(n_y):
        weight = jnp.concatenate([weights[2 * j][...], weights[2 * j + 1][...]], axis=0)
        wide = jnp.concatenate([ref[:, j].reshape(ref.shape[0] * part, half) for ref in tokens], axis=0)
        total += lax.dot_general(wide, weight, (((1,), (1,)), ((), ())), preferred_element_type=jnp.float32)
    total = total.reshape(-1, n_z, part, 2 * rows)
    for n in range(total.shape[0]):
        mine[:, n] = total[n, :, :, :rows]
        other[:, n] = total[n, :, :, rows:]


def products(weights, n_z, *tokens):
    n_y, part, half = tokens[0].shape[1:]
    count = sum(t.shape[0] for t in tokens) // n_z
    rows = weights[0].shape[0]
    out = jax.ShapeDtypeStruct((n_z, count, part, rows), jnp.float32)
    return pl.pallas_call(
        product_kernel,
        out_shape=(out, out),
        in_specs=[pl.BlockSpec(memory_space=pltpu.VMEM)] * (8 + len(tokens)),
        out_specs=(pl.BlockSpec(memory_space=pltpu.VMEM),) * 2,
        compiler_params=pltpu.CompilerParams(vmem_limit_bytes=40 * 1024 * 1024),
        cost_estimate=pl.CostEstimate(
            flops=4 * n_z * count * part * rows * n_y * half,
            bytes_accessed=4 * n_y * rows * half + 2 * sum(t.size for t in tokens) + 8 * n_z * count * part * rows,
            transcendentals=0,
        ),
    )(*weights, *tokens)


def body(grad, weight, residual, row_state, col_state, out_grad):
    rows, cols = grad.shape
    tokens = out_grad.shape[0]
    n_x, n_core, n_y, n_z = (lax.axis_size(a) for a in ("x", "core", "y", "z"))
    x, core, y = (lax.axis_index(a) for a in ("x", "core", "y"))
    all_rows, all_cols = rows * n_x * n_core, cols * n_y * n_z
    part, half = tokens // n_x, cols // n_core

    place = jnp.stack([x, core, y]).astype(jnp.int32)
    share = share_out(place, out_grad, n_z, n_y, part, half, n_core)
    share = lax.all_to_all(share, "z", 0, 0, tiled=True)

    grad_full = grad.astype(jnp.float32)
    squares = grad_full * grad_full + tiny_square
    col_part = jnp.sum(squares, axis=0).reshape(cols // 128, 128)
    col_total = pair_sum(col_part, "core", 1)
    col_total = col_total + shift(col_total, "x", 1) + shift(col_total, "x", 2) + shift(col_total, "x", 3)
    col_out = decay_rate * col_state + (1.0 - decay_rate) * col_total.reshape(cols) / all_rows
    master = weight.astype(jnp.float32) + residual.astype(jnp.float32)
    row_part = jnp.sum(squares, axis=1)
    scaled_part = jnp.sum(grad_full * grad_full * (1.0 / col_out)[None, :], axis=1)
    w_part = jnp.sum(master * master, axis=1)
    four = jnp.stack([row_part, scaled_part, w_part, row_state])
    two = jnp.stack([four, shift(four, "core", 1)], axis=1)
    parts = jnp.concatenate([two, shift(two, "x", 1), shift(two, "x", 2), shift(two, "x", 3)], axis=1)
    w_sum = jnp.sum(parts[2], axis=0, keepdims=True)
    sums = jnp.concatenate([parts[0], parts[1], w_sum, jnp.zeros((7, rows), jnp.float32)])
    sums = pair_sum(pair_sum(sums, "y", 1), "y", 2)
    sums, share = lax.optimization_barrier((sums, share))
    before, after = gather4(share, "x")
    sums = pair_sum(pair_sum(pair_sum(sums, "z", 1), "z", 2), "z", 4)

    new_weight, row_out, kept, given = update(
        place, all_rows * all_cols, all_cols, sums, parts[3], col_out[None], (grad, weight, residual), half
    )
    taken = shift(given, "core", 1)
    kept_before, kept_after = gather4(kept, "y")
    kept_before, kept_after, before, after = lax.optimization_barrier((kept_before, kept_after, before, after))
    far_low = shift(before[: n_z // 2], "x", 1)
    far_high = shift(after[n_z // 2 :], "x", -1)
    taken_before, taken_after = gather4(taken, "y")
    kept_far = shift(kept_before, "y", 1)
    taken_far = shift(taken_after, "y", -1)
    weights = (kept, taken, kept_after, taken_after, kept_far, taken_far, kept_before, taken_before)
    first = products(weights, n_z, share, after, before)
    last = products(weights, n_z, far_low, far_high)
    total = jnp.concatenate([first[0] + shift(first[1], "core", 1), last[0] + shift(last[1], "core", 1)], axis=1)
    total = lax.all_to_all(total, "z", 0, 0, tiled=True)
    summed = jnp.sum(total, axis=0)
    summed = jnp.stack([summed[0], summed[1], summed[3], summed[2]])
    summed = lax.dynamic_slice_in_dim(jnp.concatenate([summed, summed]), (n_x - x) % n_x, n_x, 0)
    input_grad = summed.reshape(tokens, rows).astype(jnp.bfloat16)
    return (new_weight, row_out.reshape(rows), col_out, input_grad)


def solution(mesh):
    fine = Mesh(mesh.devices.reshape(4, 2, 4, 8), ("x", "core", "y", "z"))
    in_specs = (P(ROW, COL), P(ROW, COL), P(ROW, COL), P(ROW), P(COL), P(COL, None))
    out_specs = (P(ROW, COL), P(ROW), P(COL), P(COL, ROW))
    return jax.shard_map(body, mesh=fine, in_specs=in_specs, out_specs=out_specs, check_vma=False)
```

time: 178 us -> 120 us (0.67)
  blocking collectives: 79.5 us -> 0 us
  starting transfers between devices: 6.44 us -> 46 us
  between operations: 15.6 us -> 0.86 us
  waiting for transfers between devices: 48.2 us -> 62.5 us
  local copies, waits for them, and re-layouts: 12.8 us -> 0.91 us
  matrix products: 10.1 us -> 0 us
  Pallas kernels: 0 us -> 7.03 us
    all_to_all x4 -> x0, blocking collectives: 79.5 us -> none  [the longest x1 39.4 us: body(): share = lax.all_to_all(share, 'z', 0, 0, tiled=True)]
    all_gather x2 -> x0, waiting for transfers between devices: 43.6 us -> none  [the longest x1 29.9 us: body(): around = lax.all_gather(new_weight, 'y', axis=0)]
    ppermute x0 -> x26, waiting for transfers between devices: none -> 43.3 us  [the longest x20 26.7 us: shift(): return lax.ppermute(value, axis, [(i, (i + by) % n) for i in range(n)])]
    ppermute x0 -> x26, starting transfers between devices: none -> 33.5 us  [the longest x20 28.2 us: shift(): return lax.ppermute(value, axis, [(i, (i + by) % n) for i in range(n)])]
    all_to_all x1 -> x2, waiting for transfers between devices: 4.59 us -> 19.2 us  [the longest x1 12.3 us: body(): total = lax.all_to_all(total, 'z', 0, 0, tiled=True)]
    dot_general x4 -> x0, matrix products: 10.1 us -> none  [body(): lax.dot_general(tokens_in[:, :, i], around[i], (((3,), (1,)), ((), ())),...]
    all_gather x1 -> x0, local copies, waits for them, and re-layouts: 7.94 us -> none  [body(): tokens_in = lax.all_gather(share, ROW, axis=0)]
    pallas_call x0 -> x4, Pallas kernels: none -> 7.03 us  [the longest x1 3.24 us: share_out(): pl.pallas_call(functools.partial(share_kernel, n_core), out_shape=jax.Sha...]
  transfers between devices with their start and end apart: 3 -> 28, of which waited for: 3 -> 22; matrix products, arithmetic and copies ran while one was open for 8% -> 1% of each run, Pallas kernels for 0% -> 3%
where the time goes in v2:
time: 120 us
  waiting for transfers between devices  62.5 us (52%)
  starting transfers between devices  46 us (38%)
  Pallas kernels  7.03 us (6%)
  other arithmetic  2.38 us (2%)
    ppermute x20, starting transfers between devices, shift(): return lax.ppermute(value, axis, [(i, (i + by) % n) for i in range(n)])  28.2 us
    ppermute x20, waiting for transfers between devices, shift(): return lax.ppermute(value, axis, [(i, (i + by) % n) for i in range(n)])  26.7 us
    ppermute x6, waiting for transfers between devices, pair_sum(): return value + lax.ppermute(value, axis, [(i, i ^ bit) for i in range(n)])  16.5 us
    all_to_all x1, waiting for transfers between devices, body(): total = lax.all_to_all(total, 'z', 0, 0, tiled=True)  12.3 us
    all_to_all x1, starting transfers between devices, body(): share = lax.all_to_all(share, 'z', 0, 0, tiled=True)  9.16 us
    all_to_all x1, waiting for transfers between devices, body(): share = lax.all_to_all(share, 'z', 0, 0, tiled=True)  6.91 us
    ppermute x6, starting transfers between devices, pair_sum(): return value + lax.ppermute(value, axis, [(i, i ^ bit) for i in range(n)])  5.3 us
    all_to_all x1, starting transfers between devices, body(): total = lax.all_to_all(total, 'z', 0, 0, tiled=True)  3.41 us
  transfers between devices with their start and end apart: 28, of which 22 were waited for; matrix products, arithmetic and copies ran while one was open for 1% of the time, Pallas kernels for 3%

profile of v2, /device:TPU:1, one launch (start us, length us, event | category | flops | bytes accessed | tf_op | source)
XLA Modules:
  0.0 119.7 jit_solution(9652690271160092770)
XLA Ops:
  1.2 3.2 %shard_map.93 = bf16[8,4,16,1152]{3,2,1,0:T(8,128)(2,1)} custom-call(s32[3]{0:T(128)} %pad_add_fusion.place, bf16[64,73728]{1,0:T(8,128)(2,1)} %source.1), custom_call_target="tpu_custom_call" | custom-call | bytes 2359296 | tf_op jit(solution)/shard_map/pallas_call | solution.py:53
  4.5 9.2 %all-to-all-start = ((bf16[8,4,16,1152]{3,2,1,0:T(8,128)(2,1)}), bf16[8,4,16,1152]{3,2,1,0:T(8,128)(2,1)S(1)}, u32[]{:S(2)}, u32[]{:S(2)}) async-start(bf16[8,4,16,1152]{3,2,1,0:T(8,128)(2,1)} %shard_map.93), calls=%async_computation | async-start | bytes 2359296 | tf_op jit(solution)/shard_map/all_to_all | solution.py:151
  15.9 2.7 %collective-permute-start.2 = (f32[18,128]{1,0:T(8,128)S(1)}, f32[18,128]{1,0:T(8,128)S(1)}, u32[]{:S(2)}, u32[]{:S(2)}) collective-permute-start(f32[18,128]{1,0:T(8,128)S(1)} %bitcast_add_fusion.1), channel_id=1, source_target_pairs={{0,128},{64,192},{128,0},{192,64},{1,129},{65,193},{129,1},{193,65... | collective-permute-start | bytes 27656 | tf_op jit(solution)/shard_map/ppermute | solution.py:19
  21.4 2.1 %collective-permute-done.1 = f32[18,128]{1,0:T(8,128)S(1)} collective-permute-done((f32[18,128]{1,0:T(8,128)S(1)}, f32[18,128]{1,0:T(8,128)S(1)}, u32[]{:S(2)}, u32[]{:S(2)}) %collective-permute-start.1) | collective-permute-done | bytes 9248 | tf_op jit(solution)/shard_map/ppermute | solution.py:19
  23.8 1.8 %collective-permute-start.4 = (f32[4,128]{1,0:T(4,128)S(1)}, f32[4,128]{1,0:T(4,128)S(1)}, u32[]{:S(2)}, u32[]{:S(2)}) collective-permute-start(f32[4,128]{1,0:T(4,128)S(1)} %pad_maximum_fusion.2), channel_id=1, source_target_pairs={{0,32},{32,0},{1,33},{33,1},{2,34},{34,2},{3,35},{35,3},{4,36},{36... | collective-permute-start | bytes 6152 | tf_op jit(solution)/shard_map/ppermute | solution.py:19
  34.7 2.9 %collective-permute-start.9 = (f32[24,128]{1,0:T(8,128)S(1)}, f32[24,128]{1,0:T(8,128)S(1)}, u32[]{:S(2)}, u32[]{:S(2)}) collective-permute-start(f32[24,128]{1,0:T(8,128)S(1)} %fusion.3), channel_id=1, source_target_pairs={{0,16},{8,24},{16,0},{24,8},{1,17},{9,25},{17,1},{25,9},{2,18},{10... | collective-permute-start | bytes 36872 | tf_op jit(solution)/shard_map/ppermute | solution.py:24
  38.8 6.9 %all-to-all-done.refs_8_ = bf16[8,4,16,1152]{3,2,1,0:T(8,128)(2,1)S(1)} async-done(((bf16[8,4,16,1152]{3,2,1,0:T(8,128)(2,1)}), bf16[8,4,16,1152]{3,2,1,0:T(8,128)(2,1)S(1)}, u32[]{:S(2)}, u32[]{:S(2)}) %all-to-all-start) | async-done | bytes 1179680 | tf_op jit(solution)/shard_map/all_to_all | solution.py:151
  45.7 2.5 %collective-permute-start.17 = (bf16[8,4,16,1152]{3,2,1,0:T(8,128)(2,1)S(1)}, bf16[8,4,16,1152]{3,2,1,0:T(8,128)(2,1)S(1)}, u32[]{:S(2)}, u32[]{:S(2)}) collective-permute-start(bf16[8,4,16,1152]{3,2,1,0:T(8,128)(2,1)S(1)} %all-to-all-done.refs_8_), channel_id=1, source_target_pairs={{0,192},{64,0},{128,64},{192,128},{1,193},{65,1},{129,65},{193,129... | collective-permute-start | bytes 3538952 | tf_op jit(solution)/shard_map/ppermute | solution.py:19
  48.2 2.8 %collective-permute-done.10 = f32[24,128]{1,0:T(8,128)S(1)} collective-permute-done((f32[24,128]{1,0:T(8,128)S(1)}, f32[24,128]{1,0:T(8,128)S(1)}, u32[]{:S(2)}, u32[]{:S(2)}) %collective-permute-start.10) | collective-permute-done | bytes 12320 | tf_op jit(solution)/shard_map/ppermute | solution.py:24
  51.0 3.7 %collective-permute-done.11 = f32[24,128]{1,0:T(8,128)S(1)} collective-permute-done((f32[24,128]{1,0:T(8,128)S(1)}, f32[24,128]{1,0:T(8,128)S(1)}, u32[]{:S(2)}, u32[]{:S(2)}) %collective-permute-start.11) | collective-permute-done | bytes 12320 | tf_op jit(solution)/shard_map/ppermute | solution.py:24
  54.8 6.4 %collective-permute-done.12 = f32[24,128]{1,0:T(8,128)S(1)} collective-permute-done((f32[24,128]{1,0:T(8,128)S(1)}, f32[24,128]{1,0:T(8,128)S(1)}, u32[]{:S(2)}, u32[]{:S(2)}) %collective-permute-start.12) | collective-permute-done | bytes 12320 | tf_op jit(solution)/shard_map/ppermute | solution.py:24
  61.2 1.8 %shard_map.94 = (bf16[128,2304]{1,0:T(8,128)(2,1)}, f32[1,128]{1,0:T(1,128)}, bf16[128,1152]{1,0:T(8,128)(2,1)S(1)}, bf16[128,1152]{1,0:T(8,128)(2,1)S(1)}) custom-call(s32[3]{0:T(128)S(1)} %copy-done.3, f32[24,128]{1,0:T(8,128)S(1)} %add.64.sums, f32[8,128]{1,0:T(8,128)S(1)} %get-tuple-element.36.state, f32[1,2304]{1,0:T(1,128)S(1)} %broadcast_in_dim.12.col_out, ...), custom_call_target="tpu_custom_call" | custom-call | tf_op jit(solution)/shard_map/pallas_call | solution.py:89
  63.0 3.7 %collective-permute-start.13 = (bf16[128,1152]{1,0:T(8,128)(2,1)S(1)}, bf16[128,1152]{1,0:T(8,128)(2,1)S(1)}, u32[]{:S(2)}, u32[]{:S(2)}) collective-permute-start(bf16[128,1152]{1,0:T(8,128)(2,1)S(1)} %get-tuple-element.22), channel_id=1, source_target_pairs={{0,32},{32,0},{1,33},{33,1},{2,34},{34,2},{3,35},{35,3},{4,36},{36... | collective-permute-start | bytes 884744 | tf_op jit(solution)/shard_map/ppermute | solution.py:19
  66.8 2.7 %collective-permute-start.15 = (bf16[128,1152]{1,0:T(8,128)(2,1)S(1)}, bf16[128,1152]{1,0:T(8,128)(2,1)S(1)}, u32[]{:S(2)}, u32[]{:S(2)}) collective-permute-start(bf16[128,1152]{1,0:T(8,128)(2,1)S(1)} %get-tuple-element.21.refs_0_), channel_id=1, source_target_pairs={{0,24},{8,0},{16,8},{24,16},{1,25},{9,1},{17,9},{25,17},{2,26},{10... | collective-permute-start | bytes 884744 | tf_op jit(solution)/shard_map/ppermute | solution.py:19
  69.5 2.7 %collective-permute-start.18 = (bf16[128,1152]{1,0:T(8,128)(2,1)S(1)}, bf16[128,1152]{1,0:T(8,128)(2,1)S(1)}, u32[]{:S(2)}, u32[]{:S(2)}) collective-permute-start(bf16[128,1152]{1,0:T(8,128)(2,1)S(1)} %collective-permute-done.13.refs_1_), channel_id=1, source_target_pairs={{0,24},{8,0},{16,8},{24,16},{1,25},{9,1},{17,9},{25,17},{2,26},{10... | collective-permute-start | bytes 884744 | tf_op jit(solution)/shard_map/ppermute | solution.py:19
  72.2 3.7 %collective-permute-done.15.refs_2_ = bf16[128,1152]{1,0:T(8,128)(2,1)S(1)} collective-permute-done((bf16[128,1152]{1,0:T(8,128)(2,1)S(1)}, bf16[128,1152]{1,0:T(8,128)(2,1)S(1)}, u32[]{:S(2)}, u32[]{:S(2)}) %collective-permute-start.15) | collective-permute-done | bytes 294944 | tf_op jit(solution)/shard_map/ppermute | solution.py:19
  75.9 3.1 %collective-permute-done.14.refs_6_ = bf16[128,1152]{1,0:T(8,128)(2,1)S(1)} collective-permute-done((bf16[128,1152]{1,0:T(8,128)(2,1)S(1)}, bf16[128,1152]{1,0:T(8,128)(2,1)S(1)}, u32[]{:S(2)}, u32[]{:S(2)}) %collective-permute-start.14) | collective-permute-done | bytes 294944 | tf_op jit(solution)/shard_map/ppermute | solution.py:19
  79.1 3.0 %collective-permute-start.24 = (bf16[4,4,16,1152]{3,2,1,0:T(8,128)(2,1)S(1)}, bf16[4,4,16,1152]{3,2,1,0:T(8,128)(2,1)S(1)}, u32[]{:S(2)}, u32[]{:S(2)}) collective-permute-start(bf16[4,4,16,1152]{3,2,1,0:T(8,128)(2,1)S(1)} %slice.35), channel_id=1, source_target_pairs={{0,192},{64,0},{128,64},{192,128},{1,193},{65,1},{129,65},{193,129... | collective-permute-start | bytes 1769480 | tf_op jit(solution)/shard_map/ppermute | solution.py:19
  82.2 3.4 %collective-permute-start.20 = (bf16[128,1152]{1,0:T(8,128)(2,1)S(1)}, bf16[128,1152]{1,0:T(8,128)(2,1)S(1)}, u32[]{:S(2)}, u32[]{:S(2)}) collective-permute-start(bf16[128,1152]{1,0:T(8,128)(2,1)S(1)} %collective-permute-done.18.refs_3_), channel_id=1, source_target_pairs={{0,24},{8,0},{16,8},{24,16},{1,25},{9,1},{17,9},{25,17},{2,26},{10... | collective-permute-start | bytes 884744 | tf_op jit(solution)/shard_map/ppermute | solution.py:19
  85.6 4.8 %collective-permute-done.21.refs_7_ = bf16[128,1152]{1,0:T(8,128)(2,1)S(1)} collective-permute-done((bf16[128,1152]{1,0:T(8,128)(2,1)S(1)}, bf16[128,1152]{1,0:T(8,128)(2,1)S(1)}, u32[]{:S(2)}, u32[]{:S(2)}) %collective-permute-start.21) | collective-permute-done | bytes 294944 | tf_op jit(solution)/shard_map/ppermute | solution.py:19
  91.0 5.7 %collective-permute-done.19.refs_4_ = bf16[128,1152]{1,0:T(8,128)(2,1)S(1)} collective-permute-done((bf16[128,1152]{1,0:T(8,128)(2,1)S(1)}, bf16[128,1152]{1,0:T(8,128)(2,1)S(1)}, u32[]{:S(2)}, u32[]{:S(2)}) %collective-permute-start.19) | collective-permute-done | bytes 294944 | tf_op jit(solution)/shard_map/ppermute | solution.py:19
  97.9 2.4 %collective-permute-start.22 = (f32[8,3,16,128]{3,2,1,0:T(8,128)S(1)}, f32[8,3,16,128]{3,2,1,0:T(8,128)S(1)}, u32[]{:S(2)}, u32[]{:S(2)}) collective-permute-start(f32[8,3,16,128]{3,2,1,0:T(8,128)S(1)} %get-tuple-element.29), channel_id=1, source_target_pairs={{0,32},{32,0},{1,33},{33,1},{2,34},{34,2},{3,35},{35,3},{4,36},{36... | collective-permute-start | bytes 589832 | tf_op jit(solution)/shard_map/ppermute | solution.py:19
  103.3 3.4 %all-to-all-start.1 = ((f32[8,4,16,128]{3,2,1,0:T(8,128)}), f32[8,4,16,128]{3,2,1,0:T(8,128)S(1)}, u32[]{:S(2)}, u32[]{:S(2)}) async-start(f32[8,4,16,128]{3,2,1,0:T(8,128)} %pad_maximum_fusion), calls=%async_computation.1 | async-start | bytes 524288 | tf_op jit(solution)/shard_map/all_to_all | solution.py:188
  106.7 12.3 %all-to-all-done.1 = f32[8,4,16,128]{3,2,1,0:T(8,128)S(1)} async-done(((f32[8,4,16,128]{3,2,1,0:T(8,128)}), f32[8,4,16,128]{3,2,1,0:T(8,128)S(1)}, u32[]{:S(2)}, u32[]{:S(2)}) %all-to-all-start.1) | async-done | bytes 262176 | tf_op jit(solution)/shard_map/all_to_all | solution.py:188
  (82 shorter events, 21.7 us)
Async XLA Ops:
  4.5 41.2 %all-to-all-start = ((bf16[8,4,16,1152]{3,2,1,0:T(8,128)(2,1)}), bf16[8,4,16,1152]{3,2,1,0:T(8,128)(2,1)S(1)}, u32[]{:S(2)}, u32[]{:S(2)}) async-start(bf16[8,4,16,1152]{3,2,1,0:T(8,128)(2,1)} %shard_map.93), calls=%async_computation | async-start | bytes 2359296 | tf_op jit(solution)/shard_map/all_to_all | solution.py:151
  15.9 4.5 %collective-permute-start.2 = (f32[18,128]{1,0:T(8,128)S(1)}, f32[18,128]{1,0:T(8,128)S(1)}, u32[]{:S(2)}, u32[]{:S(2)}) collective-permute-start(f32[18,128]{1,0:T(8,128)S(1)} %bitcast_add_fusion.1), channel_id=1, source_target_pairs={{0,128},{64,192},{128,0},{192,64},{1,129},{65,193},{129,1},{193,65... | collective-permute-start | bytes 27656 | tf_op jit(solution)/shard_map/ppermute | solution.py:19
  18.6 2.8 %collective-permute-start.3 = (f32[18,128]{1,0:T(8,128)S(1)}, f32[18,128]{1,0:T(8,128)S(1)}, u32[]{:S(2)}, u32[]{:S(2)}) collective-permute-start(f32[18,128]{1,0:T(8,128)S(1)} %bitcast_add_fusion.1), channel_id=1, source_target_pairs={{0,192},{64,0},{128,64},{192,128},{1,193},{65,1},{129,65},{193,129... | collective-permute-start | bytes 27656 | tf_op jit(solution)/shard_map/ppermute | solution.py:19
  19.5 4.1 %collective-permute-start.1 = (f32[18,128]{1,0:T(8,128)S(1)}, f32[18,128]{1,0:T(8,128)S(1)}, u32[]{:S(2)}, u32[]{:S(2)}) collective-permute-start(f32[18,128]{1,0:T(8,128)S(1)} %bitcast_add_fusion.1), channel_id=1, source_target_pairs={{0,64},{64,128},{128,192},{192,0},{1,65},{65,129},{129,193},{193,1... | collective-permute-start | bytes 27656 | tf_op jit(solution)/shard_map/ppermute | solution.py:19
  26.5 4.3 %collective-permute-start.6 = (f32[4,2,128]{2,1,0:T(2,128)S(1)}, f32[4,2,128]{2,1,0:T(2,128)S(1)}, u32[]{:S(2)}, u32[]{:S(2)}) collective-permute-start(f32[4,2,128]{2,1,0:T(2,128)S(1)} %pad_maximum_fusion.1), channel_id=1, source_target_pairs={{0,128},{64,192},{128,0},{192,64},{1,129},{65,193},{129,1},{193,65... | collective-permute-start | bytes 12296 | tf_op jit(solution)/shard_map/ppermute | solution.py:19
  27.7 4.0 %collective-permute-start.5 = (f32[4,2,128]{2,1,0:T(2,128)S(1)}, f32[4,2,128]{2,1,0:T(2,128)S(1)}, u32[]{:S(2)}, u32[]{:S(2)}) collective-permute-start(f32[4,2,128]{2,1,0:T(2,128)S(1)} %pad_maximum_fusion.1), channel_id=1, source_target_pairs={{0,64},{64,128},{128,192},{192,0},{1,65},{65,129},{129,193},{193,1... | collective-permute-start | bytes 12296 | tf_op jit(solution)/shard_map/ppermute | solution.py:19
  31.8 2.9 %collective-permute-start.8 = (f32[24,128]{1,0:T(8,128)S(1)}, f32[24,128]{1,0:T(8,128)S(1)}, u32[]{:S(2)}, u32[]{:S(2)}) collective-permute-start(f32[24,128]{1,0:T(8,128)S(1)} %maximum_maximum_fusion), channel_id=1, source_target_pairs={{0,8},{8,0},{16,24},{24,16},{1,9},{9,1},{17,25},{25,17},{2,10},{10... | collective-permute-start | bytes 36872 | tf_op jit(solution)/shard_map/ppermute | solution.py:24
  34.7 4.1 %collective-permute-start.9 = (f32[24,128]{1,0:T(8,128)S(1)}, f32[24,128]{1,0:T(8,128)S(1)}, u32[]{:S(2)}, u32[]{:S(2)}) collective-permute-start(f32[24,128]{1,0:T(8,128)S(1)} %fusion.3), channel_id=1, source_target_pairs={{0,16},{8,24},{16,0},{24,8},{1,17},{9,25},{17,1},{25,9},{2,18},{10... | collective-permute-start | bytes 36872 | tf_op jit(solution)/shard_map/ppermute | solution.py:24
  45.7 33.3 %collective-permute-start.17 = (bf16[8,4,16,1152]{3,2,1,0:T(8,128)(2,1)S(1)}, bf16[8,4,16,1152]{3,2,1,0:T(8,128)(2,1)S(1)}, u32[]{:S(2)}, u32[]{:S(2)}) collective-permute-start(bf16[8,4,16,1152]{3,2,1,0:T(8,128)(2,1)S(1)} %all-to-all-done.refs_8_), channel_id=1, source_target_pairs={{0,192},{64,0},{128,64},{192,128},{1,193},{65,1},{129,65},{193,129... | collective-permute-start | bytes 3538952 | tf_op jit(solution)/shard_map/ppermute | solution.py:19
  48.2 30.8 %collective-permute-start.16 = (bf16[8,4,16,1152]{3,2,1,0:T(8,128)(2,1)S(1)}, bf16[8,4,16,1152]{3,2,1,0:T(8,128)(2,1)S(1)}, u32[]{:S(2)}, u32[]{:S(2)}) collective-permute-start(bf16[8,4,16,1152]{3,2,1,0:T(8,128)(2,1)S(1)} %all-to-all-done.refs_8_), channel_id=1, source_target_pairs={{0,64},{64,128},{128,192},{192,0},{1,65},{65,129},{129,193},{193,1... | collective-permute-start | bytes 3538952 | tf_op jit(solution)/shard_map/ppermute | solution.py:19
  48.2 2.8 %collective-permute-start.10 = (f32[24,128]{1,0:T(8,128)S(1)}, f32[24,128]{1,0:T(8,128)S(1)}, u32[]{:S(2)}, u32[]{:S(2)}) collective-permute-start(f32[24,128]{1,0:T(8,128)S(1)} %add.61), channel_id=1, source_target_pairs={{0,1},{1,0},{2,3},{3,2},{4,5},{5,4},{6,7},{7,6},{8,9},{9,8},{10,11... | collective-permute-start | bytes 36872 | tf_op jit(solution)/shard_map/ppermute | solution.py:24
  51.0 3.7 %collective-permute-start.11 = (f32[24,128]{1,0:T(8,128)S(1)}, f32[24,128]{1,0:T(8,128)S(1)}, u32[]{:S(2)}, u32[]{:S(2)}) collective-permute-start(f32[24,128]{1,0:T(8,128)S(1)} %add.62), channel_id=1, source_target_pairs={{0,2},{1,3},{2,0},{3,1},{4,6},{5,7},{6,4},{7,5},{8,10},{9,11},{10,... | collective-permute-start | bytes 36872 | tf_op jit(solution)/shard_map/ppermute | solution.py:24
  54.8 6.5 %collective-permute-start.12 = (f32[24,128]{1,0:T(8,128)S(1)}, f32[24,128]{1,0:T(8,128)S(1)}, u32[]{:S(2)}, u32[]{:S(2)}) collective-permute-start(f32[24,128]{1,0:T(8,128)S(1)} %add.63), channel_id=1, source_target_pairs={{0,4},{1,5},{2,6},{3,7},{4,0},{5,1},{6,2},{7,3},{8,12},{9,13},{10,... | collective-permute-start | bytes 36872 | tf_op jit(solution)/shard_map/ppermute | solution.py:24
  63.0 6.5 %collective-permute-start.13 = (bf16[128,1152]{1,0:T(8,128)(2,1)S(1)}, bf16[128,1152]{1,0:T(8,128)(2,1)S(1)}, u32[]{:S(2)}, u32[]{:S(2)}) collective-permute-start(bf16[128,1152]{1,0:T(8,128)(2,1)S(1)} %get-tuple-element.22), channel_id=1, source_target_pairs={{0,32},{32,0},{1,33},{33,1},{2,34},{34,2},{3,35},{35,3},{4,36},{36... | collective-permute-start | bytes 884744 | tf_op jit(solution)/shard_map/ppermute | solution.py:19
  66.8 9.1 %collective-permute-start.15 = (bf16[128,1152]{1,0:T(8,128)(2,1)S(1)}, bf16[128,1152]{1,0:T(8,128)(2,1)S(1)}, u32[]{:S(2)}, u32[]{:S(2)}) collective-permute-start(bf16[128,1152]{1,0:T(8,128)(2,1)S(1)} %get-tuple-element.21.refs_0_), channel_id=1, source_target_pairs={{0,24},{8,0},{16,8},{24,16},{1,25},{9,1},{17,9},{25,17},{2,26},{10... | collective-permute-start | bytes 884744 | tf_op jit(solution)/shard_map/ppermute | solution.py:19
  69.5 9.5 %collective-permute-start.14 = (bf16[128,1152]{1,0:T(8,128)(2,1)S(1)}, bf16[128,1152]{1,0:T(8,128)(2,1)S(1)}, u32[]{:S(2)}, u32[]{:S(2)}) collective-permute-start(bf16[128,1152]{1,0:T(8,128)(2,1)S(1)} %get-tuple-element.21.refs_0_), channel_id=1, source_target_pairs={{0,8},{8,16},{16,24},{24,0},{1,9},{9,17},{17,25},{25,1},{2,10},{10... | collective-permute-start | bytes 884744 | tf_op jit(solution)/shard_map/ppermute | solution.py:19
  69.5 12.7 %collective-permute-start.18 = (bf16[128,1152]{1,0:T(8,128)(2,1)S(1)}, bf16[128,1152]{1,0:T(8,128)(2,1)S(1)}, u32[]{:S(2)}, u32[]{:S(2)}) collective-permute-start(bf16[128,1152]{1,0:T(8,128)(2,1)S(1)} %collective-permute-done.13.refs_1_), channel_id=1, source_target_pairs={{0,24},{8,0},{16,8},{24,16},{1,25},{9,1},{17,9},{25,17},{2,26},{10... | collective-permute-start | bytes 884744 | tf_op jit(solution)/shard_map/ppermute | solution.py:19
  79.1 21.3 %collective-permute-start.24 = (bf16[4,4,16,1152]{3,2,1,0:T(8,128)(2,1)S(1)}, bf16[4,4,16,1152]{3,2,1,0:T(8,128)(2,1)S(1)}, u32[]{:S(2)}, u32[]{:S(2)}) collective-permute-start(bf16[4,4,16,1152]{3,2,1,0:T(8,128)(2,1)S(1)} %slice.35), channel_id=1, source_target_pairs={{0,192},{64,0},{128,64},{192,128},{1,193},{65,1},{129,65},{193,129... | collective-permute-start | bytes 1769480 | tf_op jit(solution)/shard_map/ppermute | solution.py:19
  82.1 18.2 %collective-permute-start.23 = (bf16[4,4,16,1152]{3,2,1,0:T(8,128)(2,1)S(1)}, bf16[4,4,16,1152]{3,2,1,0:T(8,128)(2,1)S(1)}, u32[]{:S(2)}, u32[]{:S(2)}) collective-permute-start(bf16[4,4,16,1152]{3,2,1,0:T(8,128)(2,1)S(1)} %slice.34), channel_id=1, source_target_pairs={{0,64},{64,128},{128,192},{192,0},{1,65},{65,129},{129,193},{193,1... | collective-permute-start | bytes 1769480 | tf_op jit(solution)/shard_map/ppermute | solution.py:19
  82.1 8.3 %collective-permute-start.21 = (bf16[128,1152]{1,0:T(8,128)(2,1)S(1)}, bf16[128,1152]{1,0:T(8,128)(2,1)S(1)}, u32[]{:S(2)}, u32[]{:S(2)}) collective-permute-start(bf16[128,1152]{1,0:T(8,128)(2,1)S(1)} %collective-permute-done.13.refs_1_), channel_id=1, source_target_pairs={{0,8},{8,16},{16,24},{24,0},{1,9},{9,17},{17,25},{25,1},{2,10},{10... | collective-permute-start | bytes 884744 | tf_op jit(solution)/shard_map/ppermute | solution.py:19
  82.2 8.8 %collective-permute-start.20 = (bf16[128,1152]{1,0:T(8,128)(2,1)S(1)}, bf16[128,1152]{1,0:T(8,128)(2,1)S(1)}, u32[]{:S(2)}, u32[]{:S(2)}) collective-permute-start(bf16[128,1152]{1,0:T(8,128)(2,1)S(1)} %collective-permute-done.18.refs_3_), channel_id=1, source_target_pairs={{0,24},{8,0},{16,8},{24,16},{1,25},{9,1},{17,9},{25,17},{2,26},{10... | collective-permute-start | bytes 884744 | tf_op jit(solution)/shard_map/ppermute | solution.py:19
  85.6 11.1 %collective-permute-start.19 = (bf16[128,1152]{1,0:T(8,128)(2,1)S(1)}, bf16[128,1152]{1,0:T(8,128)(2,1)S(1)}, u32[]{:S(2)}, u32[]{:S(2)}) collective-permute-start(bf16[128,1152]{1,0:T(8,128)(2,1)S(1)} %collective-permute-done.14.refs_6_), channel_id=1, source_target_pairs={{0,8},{8,16},{16,24},{24,0},{1,9},{9,17},{17,25},{25,1},{2,10},{10... | collective-permute-start | bytes 884744 | tf_op jit(solution)/shard_map/ppermute | solution.py:19
  97.9 3.5 %collective-permute-start.22 = (f32[8,3,16,128]{3,2,1,0:T(8,128)S(1)}, f32[8,3,16,128]{3,2,1,0:T(8,128)S(1)}, u32[]{:S(2)}, u32[]{:S(2)}) collective-permute-start(f32[8,3,16,128]{3,2,1,0:T(8,128)S(1)} %get-tuple-element.29), channel_id=1, source_target_pairs={{0,32},{32,0},{1,33},{33,1},{2,34},{34,2},{3,35},{35,3},{4,36},{36... | collective-permute-start | bytes 589832 | tf_op jit(solution)/shard_map/ppermute | solution.py:19
  103.3 15.7 %all-to-all-start.1 = ((f32[8,4,16,128]{3,2,1,0:T(8,128)}), f32[8,4,16,128]{3,2,1,0:T(8,128)S(1)}, u32[]{:S(2)}, u32[]{:S(2)}) async-start(f32[8,4,16,128]{3,2,1,0:T(8,128)} %pad_maximum_fusion), calls=%async_computation.1 | async-start | bytes 524288 | tf_op jit(solution)/shard_map/all_to_all | solution.py:188
  (11 other events, 155.8 us)

commit v3 on v2

--- a/solution.py
+++ b/solution.py
@@ -105,12 +105,12 @@
 
 
 def product_kernel(*refs):
-    weights, tokens, (mine, other) = refs[:8], refs[8:-2], refs[-2:]
+    weights, tokens, (mine, other) = refs[:5], refs[5:-2], refs[-2:]
     n_z, _, part, rows = mine.shape
     n_y, half = tokens[0].shape[1], tokens[0].shape[3]
+    own, after, far_low, far_high, before = (ref[...] for ref in weights)
     total = 0.0
-    for j in range(n_y):
-        weight = jnp.concatenate([weights[2 * j][...], weights[2 * j + 1][...]], axis=0)
+    for j, weight in enumerate((own, after, jnp.concatenate([far_low, far_high], axis=0), before)):
         wide = jnp.concatenate([ref[:, j].reshape(ref.shape[0] * part, half) for ref in tokens], axis=0)
         total += lax.dot_general(wide, weight, (((1,), (1,)), ((), ())), preferred_element_type=jnp.float32)
     total = total.reshape(-1, n_z, part, 2 * rows)
@@ -122,12 +122,12 @@
 def products(weights, n_z, *tokens):
     n_y, part, half = tokens[0].shape[1:]
     count = sum(t.shape[0] for t in tokens) // n_z
-    rows = weights[0].shape[0]
+    rows = weights[0].shape[0] // 2
     out = jax.ShapeDtypeStruct((n_z, count, part, rows), jnp.float32)
     return pl.pallas_call(
         product_kernel,
         out_shape=(out, out),
-        in_specs=[pl.BlockSpec(memory_space=pltpu.VMEM)] * (8 + len(tokens)),
+        in_specs=[pl.BlockSpec(memory_space=pltpu.VMEM)] * (5 + len(tokens)),
         out_specs=(pl.BlockSpec(memory_space=pltpu.VMEM),) * 2,
         compiler_params=pltpu.CompilerParams(vmem_limit_bytes=40 * 1024 * 1024),
         cost_estimate=pl.CostEstimate(
@@ -174,14 +174,14 @@
         place, all_rows * all_cols, all_cols, sums, parts[3], col_out[None], (grad, weight, residual), half
     )
     taken = shift(given, "core", 1)
-    kept_before, kept_after = gather4(kept, "y")
-    kept_before, kept_after, before, after = lax.optimization_barrier((kept_before, kept_after, before, after))
+    block = jnp.concatenate([kept, taken], axis=0)
+    w_before, w_after = gather4(block, "y")
     far_low = shift(before[: n_z // 2], "x", 1)
     far_high = shift(after[n_z // 2 :], "x", -1)
-    taken_before, taken_after = gather4(taken, "y")
-    kept_far = shift(kept_before, "y", 1)
-    taken_far = shift(taken_after, "y", -1)
-    weights = (kept, taken, kept_after, taken_after, kept_far, taken_far, kept_before, taken_before)
+    kept_far = shift(w_before[:rows], "y", 1)
+    taken_far = shift(w_after[rows:], "y", -1)
+    kept_far, taken_far, far_low, far_high = lax.optimization_barrier((kept_far, taken_far, far_low, far_high))
+    weights = (block, w_after, kept_far, taken_far, w_before)
     first = products(weights, n_z, share, after, before)
     last = products(weights, n_z, far_low, far_high)
     total = jnp.concatenate([first[0] + shift(first[1], "core", 1), last[0] + shift(last[1], "core", 1)], axis=1)

time: 120 us -> 116 us (0.967)
  starting transfers between devices: 46 us -> 43.3 us
  waiting for transfers between devices: 62.5 us -> 60.9 us
    ppermute x20 -> x18, starting transfers between devices: 28.2 us -> 25.5 us  [shift(): return lax.ppermute(value, axis, [(i, (i + by) % n) for i in range(n)])]
    ppermute x20 -> x18, waiting for transfers between devices: 26.7 us -> 25.2 us  [shift(): return lax.ppermute(value, axis, [(i, (i + by) % n) for i in range(n)])]
  transfers between devices with their start and end apart: 28 -> 26, of which waited for: 22 -> 19; matrix products, arithmetic and copies ran while one was open for 1% -> 1% of each run, Pallas kernels for 3% -> 2%
where the time goes in v3:
time: 116 us
  waiting for transfers between devices  60.9 us (52%)
  starting transfers between devices  43.3 us (37%)
  Pallas kernels  7.01 us (6%)
  other arithmetic  2.38 us (2%)
    ppermute x18, starting transfers between devices, shift(): return lax.ppermute(value, axis, [(i, (i + by) % n) for i in range(n)])  25.5 us
    ppermute x18, waiting for transfers between devices, shift(): return lax.ppermute(value, axis, [(i, (i + by) % n) for i in range(n)])  25.2 us
    ppermute x6, waiting for transfers between devices, pair_sum(): return value + lax.ppermute(value, axis, [(i, i ^ bit) for i in range(n)])  16.5 us
    all_to_all x1, waiting for transfers between devices, body(): total = lax.all_to_all(total, 'z', 0, 0, tiled=True)  12.3 us
    all_to_all x1, starting transfers between devices, body(): share = lax.all_to_all(share, 'z', 0, 0, tiled=True)  9.16 us
    all_to_all x1, waiting for transfers between devices, body(): share = lax.all_to_all(share, 'z', 0, 0, tiled=True)  6.91 us
    ppermute x6, starting transfers between devices, pair_sum(): return value + lax.ppermute(value, axis, [(i, i ^ bit) for i in range(n)])  5.3 us
    all_to_all x1, starting transfers between devices, body(): total = lax.all_to_all(total, 'z', 0, 0, tiled=True)  3.41 us
  transfers between devices with their start and end apart: 26, of which 19 were waited for; matrix products, arithmetic and copies ran while one was open for 1% of the time, Pallas kernels for 2%

profile of v3, /device:TPU:1, one launch (start us, length us, event | category | flops | bytes accessed | tf_op | source)
XLA Modules:
  0.0 115.5 jit_solution(832453535103131156)
XLA Ops:
  1.2 3.2 %shard_map.93 = bf16[8,4,16,1152]{3,2,1,0:T(8,128)(2,1)} custom-call(s32[3]{0:T(128)} %pad_add_fusion.place, bf16[64,73728]{1,0:T(8,128)(2,1)} %source.1), custom_call_target="tpu_custom_call" | custom-call | bytes 2359296 | tf_op jit(solution)/shard_map/pallas_call | solution.py:53
  4.5 9.2 %all-to-all-start = ((bf16[8,4,16,1152]{3,2,1,0:T(8,128)(2,1)}), bf16[8,4,16,1152]{3,2,1,0:T(8,128)(2,1)S(1)}, u32[]{:S(2)}, u32[]{:S(2)}) async-start(bf16[8,4,16,1152]{3,2,1,0:T(8,128)(2,1)} %shard_map.93), calls=%async_computation | async-start | bytes 2359296 | tf_op jit(solution)/shard_map/all_to_all | solution.py:151
  15.9 2.7 %collective-permute-start.2 = (f32[18,128]{1,0:T(8,128)S(1)}, f32[18,128]{1,0:T(8,128)S(1)}, u32[]{:S(2)}, u32[]{:S(2)}) collective-permute-start(f32[18,128]{1,0:T(8,128)S(1)} %bitcast_add_fusion.1), channel_id=1, source_target_pairs={{0,128},{64,192},{128,0},{192,64},{1,129},{65,193},{129,1},{193,65... | collective-permute-start | bytes 27656 | tf_op jit(solution)/shard_map/ppermute | solution.py:19
  21.4 2.1 %collective-permute-done.1 = f32[18,128]{1,0:T(8,128)S(1)} collective-permute-done((f32[18,128]{1,0:T(8,128)S(1)}, f32[18,128]{1,0:T(8,128)S(1)}, u32[]{:S(2)}, u32[]{:S(2)}) %collective-permute-start.1) | collective-permute-done | bytes 9248 | tf_op jit(solution)/shard_map/ppermute | solution.py:19
  23.8 1.8 %collective-permute-start.4 = (f32[4,128]{1,0:T(4,128)S(1)}, f32[4,128]{1,0:T(4,128)S(1)}, u32[]{:S(2)}, u32[]{:S(2)}) collective-permute-start(f32[4,128]{1,0:T(4,128)S(1)} %pad_maximum_fusion.2), channel_id=1, source_target_pairs={{0,32},{32,0},{1,33},{33,1},{2,34},{34,2},{3,35},{35,3},{4,36},{36... | collective-permute-start | bytes 6152 | tf_op jit(solution)/shard_map/ppermute | solution.py:19
  29.3 1.6 %collective-permute-done.6 = f32[4,2,128]{2,1,0:T(2,128)S(1)} collective-permute-done((f32[4,2,128]{2,1,0:T(2,128)S(1)}, f32[4,2,128]{2,1,0:T(2,128)S(1)}, u32[]{:S(2)}, u32[]{:S(2)}) %collective-permute-start.6) | collective-permute-done | bytes 4128 | tf_op jit(solution)/shard_map/ppermute | solution.py:19
  33.1 1.5 %collective-permute-done.8 = f32[24,128]{1,0:T(8,128)S(1)} collective-permute-done((f32[24,128]{1,0:T(8,128)S(1)}, f32[24,128]{1,0:T(8,128)S(1)}, u32[]{:S(2)}, u32[]{:S(2)}) %collective-permute-start.8) | collective-permute-done | bytes 12320 | tf_op jit(solution)/shard_map/ppermute | solution.py:24
  34.7 2.9 %collective-permute-start.9 = (f32[24,128]{1,0:T(8,128)S(1)}, f32[24,128]{1,0:T(8,128)S(1)}, u32[]{:S(2)}, u32[]{:S(2)}) collective-permute-start(f32[24,128]{1,0:T(8,128)S(1)} %fusion.3), channel_id=1, source_target_pairs={{0,16},{8,24},{16,0},{24,8},{1,17},{9,25},{17,1},{25,9},{2,18},{10... | collective-permute-start | bytes 36872 | tf_op jit(solution)/shard_map/ppermute | solution.py:24
  38.8 6.9 %all-to-all-done.refs_5_ = bf16[8,4,16,1152]{3,2,1,0:T(8,128)(2,1)S(1)} async-done(((bf16[8,4,16,1152]{3,2,1,0:T(8,128)(2,1)}), bf16[8,4,16,1152]{3,2,1,0:T(8,128)(2,1)S(1)}, u32[]{:S(2)}, u32[]{:S(2)}) %all-to-all-start) | async-done | bytes 1179680 | tf_op jit(solution)/shard_map/all_to_all | solution.py:151
  45.7 2.5 %collective-permute-start.20 = (bf16[8,4,16,1152]{3,2,1,0:T(8,128)(2,1)S(1)}, bf16[8,4,16,1152]{3,2,1,0:T(8,128)(2,1)S(1)}, u32[]{:S(2)}, u32[]{:S(2)}) collective-permute-start(bf16[8,4,16,1152]{3,2,1,0:T(8,128)(2,1)S(1)} %all-to-all-done.refs_5_), channel_id=1, source_target_pairs={{0,192},{64,0},{128,64},{192,128},{1,193},{65,1},{129,65},{193,129... | collective-permute-start | bytes 3538952 | tf_op jit(solution)/shard_map/ppermute | solution.py:19
  48.2 2.8 %collective-permute-done.10 = f32[24,128]{1,0:T(8,128)S(1)} collective-permute-done((f32[24,128]{1,0:T(8,128)S(1)}, f32[24,128]{1,0:T(8,128)S(1)}, u32[]{:S(2)}, u32[]{:S(2)}) %collective-permute-start.10) | collective-permute-done | bytes 12320 | tf_op jit(solution)/shard_map/ppermute | solution.py:24
  51.0 3.7 %collective-permute-done.11 = f32[24,128]{1,0:T(8,128)S(1)} collective-permute-done((f32[24,128]{1,0:T(8,128)S(1)}, f32[24,128]{1,0:T(8,128)S(1)}, u32[]{:S(2)}, u32[]{:S(2)}) %collective-permute-start.11) | collective-permute-done | bytes 12320 | tf_op jit(solution)/shard_map/ppermute | solution.py:24
  54.8 6.4 %collective-permute-done.12 = f32[24,128]{1,0:T(8,128)S(1)} collective-permute-done((f32[24,128]{1,0:T(8,128)S(1)}, f32[24,128]{1,0:T(8,128)S(1)}, u32[]{:S(2)}, u32[]{:S(2)}) %collective-permute-start.12) | collective-permute-done | bytes 12320 | tf_op jit(solution)/shard_map/ppermute | solution.py:24
  61.2 1.8 %shard_map.94 = (bf16[128,2304]{1,0:T(8,128)(2,1)}, f32[1,128]{1,0:T(1,128)}, bf16[128,1152]{1,0:T(8,128)(2,1)S(1)}, bf16[128,1152]{1,0:T(8,128)(2,1)S(1)}) custom-call(s32[3]{0:T(128)S(1)} %copy-done.3, f32[24,128]{1,0:T(8,128)S(1)} %add.64.sums, f32[8,128]{1,0:T(8,128)S(1)} %get-tuple-element.36.state, f32[1,2304]{1,0:T(1,128)S(1)} %broadcast_in_dim.12.col_out, ...), custom_call_target="tpu_custom_call" | custom-call | tf_op jit(solution)/shard_map/pallas_call | solution.py:89
  63.0 3.7 %collective-permute-start.13 = (bf16[128,1152]{1,0:T(8,128)(2,1)S(1)}, bf16[128,1152]{1,0:T(8,128)(2,1)S(1)}, u32[]{:S(2)}, u32[]{:S(2)}) collective-permute-start(bf16[128,1152]{1,0:T(8,128)(2,1)S(1)} %get-tuple-element.22), channel_id=1, source_target_pairs={{0,32},{32,0},{1,33},{33,1},{2,34},{34,2},{3,35},{35,3},{4,36},{36... | collective-permute-start | bytes 884744 | tf_op jit(solution)/shard_map/ppermute | solution.py:19
  68.0 1.6 %collective-permute-start.15 = (bf16[256,1152]{1,0:T(8,128)(2,1)S(1)}, bf16[256,1152]{1,0:T(8,128)(2,1)S(1)}, u32[]{:S(2)}, u32[]{:S(2)}) collective-permute-start(bf16[256,1152]{1,0:T(8,128)(2,1)S(1)} %constant_dynamic-update-slice_fusion.refs_0_), channel_id=1, source_target_pairs={{0,8},{8,16},{16,24},{24,0},{1,9},{9,17},{17,25},{25,1},{2,10},{10... | collective-permute-start | bytes 1769480 | tf_op jit(solution)/shard_map/ppermute | solution.py:19
  71.1 1.9 %collective-permute-done.20.refs_6_ = bf16[8,4,16,1152]{3,2,1,0:T(8,128)(2,1)S(1)} collective-permute-done((bf16[8,4,16,1152]{3,2,1,0:T(8,128)(2,1)S(1)}, bf16[8,4,16,1152]{3,2,1,0:T(8,128)(2,1)S(1)}, u32[]{:S(2)}, u32[]{:S(2)}) %collective-permute-start.20) | collective-permute-done | bytes 1179680 | tf_op jit(solution)/shard_map/ppermute | solution.py:19
  73.1 3.5 %collective-permute-start.21 = (bf16[4,4,16,1152]{3,2,1,0:T(8,128)(2,1)S(1)}, bf16[4,4,16,1152]{3,2,1,0:T(8,128)(2,1)S(1)}, u32[]{:S(2)}, u32[]{:S(2)}) collective-permute-start(bf16[4,4,16,1152]{3,2,1,0:T(8,128)(2,1)S(1)} %slice.54), channel_id=1, source_target_pairs={{0,192},{64,0},{128,64},{192,128},{1,193},{65,1},{129,65},{193,129... | collective-permute-start | bytes 1769480 | tf_op jit(solution)/shard_map/ppermute | solution.py:19
  76.7 7.4 %collective-permute-done.15.refs_4_ = bf16[256,1152]{1,0:T(8,128)(2,1)S(1)} collective-permute-done((bf16[256,1152]{1,0:T(8,128)(2,1)S(1)}, bf16[256,1152]{1,0:T(8,128)(2,1)S(1)}, u32[]{:S(2)}, u32[]{:S(2)}) %collective-permute-start.15) | collective-permute-done | bytes 589856 | tf_op jit(solution)/shard_map/ppermute | solution.py:19
  84.3 2.7 %collective-permute-start.17 = (bf16[128,1152]{1,0:T(8,128)(2,1)S(1)}, bf16[128,1152]{1,0:T(8,128)(2,1)S(1)}, u32[]{:S(2)}, u32[]{:S(2)}) collective-permute-start(bf16[128,1152]{1,0:T(8,128)(2,1)S(1)} %slice.52), channel_id=1, source_target_pairs={{0,24},{8,0},{16,8},{24,16},{1,25},{9,1},{17,9},{25,17},{2,26},{10... | collective-permute-start | bytes 884744 | tf_op jit(solution)/shard_map/ppermute | solution.py:19
  87.0 5.8 %collective-permute-done.16.refs_2_ = bf16[128,1152]{1,0:T(8,128)(2,1)S(1)} collective-permute-done((bf16[128,1152]{1,0:T(8,128)(2,1)S(1)}, bf16[128,1152]{1,0:T(8,128)(2,1)S(1)}, u32[]{:S(2)}, u32[]{:S(2)}) %collective-permute-start.16) | collective-permute-done | bytes 294944 | tf_op jit(solution)/shard_map/ppermute | solution.py:19
  94.0 2.2 %collective-permute-start.22 = (f32[8,3,16,128]{3,2,1,0:T(8,128)S(1)}, f32[8,3,16,128]{3,2,1,0:T(8,128)S(1)}, u32[]{:S(2)}, u32[]{:S(2)}) collective-permute-start(f32[8,3,16,128]{3,2,1,0:T(8,128)S(1)} %get-tuple-element.27), channel_id=1, source_target_pairs={{0,32},{32,0},{1,33},{33,1},{2,34},{34,2},{3,35},{35,3},{4,36},{36... | collective-permute-start | bytes 589832 | tf_op jit(solution)/shard_map/ppermute | solution.py:19
  99.1 3.4 %all-to-all-start.1 = ((f32[8,4,16,128]{3,2,1,0:T(8,128)}), f32[8,4,16,128]{3,2,1,0:T(8,128)S(1)}, u32[]{:S(2)}, u32[]{:S(2)}) async-start(f32[8,4,16,128]{3,2,1,0:T(8,128)} %pad_maximum_fusion), calls=%async_computation.1 | async-start | bytes 524288 | tf_op jit(solution)/shard_map/all_to_all | solution.py:188
  102.5 12.3 %all-to-all-done.1 = f32[8,4,16,128]{3,2,1,0:T(8,128)S(1)} async-done(((f32[8,4,16,128]{3,2,1,0:T(8,128)}), f32[8,4,16,128]{3,2,1,0:T(8,128)S(1)}, u32[]{:S(2)}, u32[]{:S(2)}) %all-to-all-start.1) | async-done | bytes 262176 | tf_op jit(solution)/shard_map/all_to_all | solution.py:188
  (82 shorter events, 20.8 us)
Async XLA Ops:
  4.5 41.2 %all-to-all-start = ((bf16[8,4,16,1152]{3,2,1,0:T(8,128)(2,1)}), bf16[8,4,16,1152]{3,2,1,0:T(8,128)(2,1)S(1)}, u32[]{:S(2)}, u32[]{:S(2)}) async-start(bf16[8,4,16,1152]{3,2,1,0:T(8,128)(2,1)} %shard_map.93), calls=%async_computation | async-start | bytes 2359296 | tf_op jit(solution)/shard_map/all_to_all | solution.py:151
  15.9 4.5 %collective-permute-start.2 = (f32[18,128]{1,0:T(8,128)S(1)}, f32[18,128]{1,0:T(8,128)S(1)}, u32[]{:S(2)}, u32[]{:S(2)}) collective-permute-start(f32[18,128]{1,0:T(8,128)S(1)} %bitcast_add_fusion.1), channel_id=1, source_target_pairs={{0,128},{64,192},{128,0},{192,64},{1,129},{65,193},{129,1},{193,65... | collective-permute-start | bytes 27656 | tf_op jit(solution)/shard_map/ppermute | solution.py:19
  18.6 2.8 %collective-permute-start.3 = (f32[18,128]{1,0:T(8,128)S(1)}, f32[18,128]{1,0:T(8,128)S(1)}, u32[]{:S(2)}, u32[]{:S(2)}) collective-permute-start(f32[18,128]{1,0:T(8,128)S(1)} %bitcast_add_fusion.1), channel_id=1, source_target_pairs={{0,192},{64,0},{128,64},{192,128},{1,193},{65,1},{129,65},{193,129... | collective-permute-start | bytes 27656 | tf_op jit(solution)/shard_map/ppermute | solution.py:19
  19.5 4.1 %collective-permute-start.1 = (f32[18,128]{1,0:T(8,128)S(1)}, f32[18,128]{1,0:T(8,128)S(1)}, u32[]{:S(2)}, u32[]{:S(2)}) collective-permute-start(f32[18,128]{1,0:T(8,128)S(1)} %bitcast_add_fusion.1), channel_id=1, source_target_pairs={{0,64},{64,128},{128,192},{192,0},{1,65},{65,129},{129,193},{193,1... | collective-permute-start | bytes 27656 | tf_op jit(solution)/shard_map/ppermute | solution.py:19
  23.8 2.7 %collective-permute-start.4 = (f32[4,128]{1,0:T(4,128)S(1)}, f32[4,128]{1,0:T(4,128)S(1)}, u32[]{:S(2)}, u32[]{:S(2)}) collective-permute-start(f32[4,128]{1,0:T(4,128)S(1)} %pad_maximum_fusion.2), channel_id=1, source_target_pairs={{0,32},{32,0},{1,33},{33,1},{2,34},{34,2},{3,35},{35,3},{4,36},{36... | collective-permute-start | bytes 6152 | tf_op jit(solution)/shard_map/ppermute | solution.py:19
  26.5 2.8 %collective-permute-start.7 = (f32[4,2,128]{2,1,0:T(2,128)S(1)}, f32[4,2,128]{2,1,0:T(2,128)S(1)}, u32[]{:S(2)}, u32[]{:S(2)}) collective-permute-start(f32[4,2,128]{2,1,0:T(2,128)S(1)} %pad_maximum_fusion.1), channel_id=1, source_target_pairs={{0,192},{64,0},{128,64},{192,128},{1,193},{65,1},{129,65},{193,129... | collective-permute-start | bytes 12296 | tf_op jit(solution)/shard_map/ppermute | solution.py:19
  26.5 4.3 %collective-permute-start.6 = (f32[4,2,128]{2,1,0:T(2,128)S(1)}, f32[4,2,128]{2,1,0:T(2,128)S(1)}, u32[]{:S(2)}, u32[]{:S(2)}) collective-permute-start(f32[4,2,128]{2,1,0:T(2,128)S(1)} %pad_maximum_fusion.1), channel_id=1, source_target_pairs={{0,128},{64,192},{128,0},{192,64},{1,129},{65,193},{129,1},{193,65... | collective-permute-start | bytes 12296 | tf_op jit(solution)/shard_map/ppermute | solution.py:19
  27.7 4.0 %collective-permute-start.5 = (f32[4,2,128]{2,1,0:T(2,128)S(1)}, f32[4,2,128]{2,1,0:T(2,128)S(1)}, u32[]{:S(2)}, u32[]{:S(2)}) collective-permute-start(f32[4,2,128]{2,1,0:T(2,128)S(1)} %pad_maximum_fusion.1), channel_id=1, source_target_pairs={{0,64},{64,128},{128,192},{192,0},{1,65},{65,129},{129,193},{193,1... | collective-permute-start | bytes 12296 | tf_op jit(solution)/shard_map/ppermute | solution.py:19
  31.8 2.9 %collective-permute-start.8 = (f32[24,128]{1,0:T(8,128)S(1)}, f32[24,128]{1,0:T(8,128)S(1)}, u32[]{:S(2)}, u32[]{:S(2)}) collective-permute-start(f32[24,128]{1,0:T(8,128)S(1)} %maximum_maximum_fusion), channel_id=1, source_target_pairs={{0,8},{8,0},{16,24},{24,16},{1,9},{9,1},{17,25},{25,17},{2,10},{10... | collective-permute-start | bytes 36872 | tf_op jit(solution)/shard_map/ppermute | solution.py:24
  34.7 4.1 %collective-permute-start.9 = (f32[24,128]{1,0:T(8,128)S(1)}, f32[24,128]{1,0:T(8,128)S(1)}, u32[]{:S(2)}, u32[]{:S(2)}) collective-permute-start(f32[24,128]{1,0:T(8,128)S(1)} %fusion.3), channel_id=1, source_target_pairs={{0,16},{8,24},{16,0},{24,8},{1,17},{9,25},{17,1},{25,9},{2,18},{10... | collective-permute-start | bytes 36872 | tf_op jit(solution)/shard_map/ppermute | solution.py:24
  45.7 27.3 %collective-permute-start.20 = (bf16[8,4,16,1152]{3,2,1,0:T(8,128)(2,1)S(1)}, bf16[8,4,16,1152]{3,2,1,0:T(8,128)(2,1)S(1)}, u32[]{:S(2)}, u32[]{:S(2)}) collective-permute-start(bf16[8,4,16,1152]{3,2,1,0:T(8,128)(2,1)S(1)} %all-to-all-done.refs_5_), channel_id=1, source_target_pairs={{0,192},{64,0},{128,64},{192,128},{1,193},{65,1},{129,65},{193,129... | collective-permute-start | bytes 3538952 | tf_op jit(solution)/shard_map/ppermute | solution.py:19
  48.2 28.4 %collective-permute-start.18 = (bf16[8,4,16,1152]{3,2,1,0:T(8,128)(2,1)S(1)}, bf16[8,4,16,1152]{3,2,1,0:T(8,128)(2,1)S(1)}, u32[]{:S(2)}, u32[]{:S(2)}) collective-permute-start(bf16[8,4,16,1152]{3,2,1,0:T(8,128)(2,1)S(1)} %all-to-all-done.refs_5_), channel_id=1, source_target_pairs={{0,64},{64,128},{128,192},{192,0},{1,65},{65,129},{129,193},{193,1... | collective-permute-start | bytes 3538952 | tf_op jit(solution)/shard_map/ppermute | solution.py:19
  48.2 2.8 %collective-permute-start.10 = (f32[24,128]{1,0:T(8,128)S(1)}, f32[24,128]{1,0:T(8,128)S(1)}, u32[]{:S(2)}, u32[]{:S(2)}) collective-permute-start(f32[24,128]{1,0:T(8,128)S(1)} %add.61), channel_id=1, source_target_pairs={{0,1},{1,0},{2,3},{3,2},{4,5},{5,4},{6,7},{7,6},{8,9},{9,8},{10,11... | collective-permute-start | bytes 36872 | tf_op jit(solution)/shard_map/ppermute | solution.py:24
  51.0 3.7 %collective-permute-start.11 = (f32[24,128]{1,0:T(8,128)S(1)}, f32[24,128]{1,0:T(8,128)S(1)}, u32[]{:S(2)}, u32[]{:S(2)}) collective-permute-start(f32[24,128]{1,0:T(8,128)S(1)} %add.62), channel_id=1, source_target_pairs={{0,2},{1,3},{2,0},{3,1},{4,6},{5,7},{6,4},{7,5},{8,10},{9,11},{10,... | collective-permute-start | bytes 36872 | tf_op jit(solution)/shard_map/ppermute | solution.py:24
  54.8 6.5 %collective-permute-start.12 = (f32[24,128]{1,0:T(8,128)S(1)}, f32[24,128]{1,0:T(8,128)S(1)}, u32[]{:S(2)}, u32[]{:S(2)}) collective-permute-start(f32[24,128]{1,0:T(8,128)S(1)} %add.63), channel_id=1, source_target_pairs={{0,4},{1,5},{2,6},{3,7},{4,0},{5,1},{6,2},{7,3},{8,12},{9,13},{10,... | collective-permute-start | bytes 36872 | tf_op jit(solution)/shard_map/ppermute | solution.py:24
  63.0 4.9 %collective-permute-start.13 = (bf16[128,1152]{1,0:T(8,128)(2,1)S(1)}, bf16[128,1152]{1,0:T(8,128)(2,1)S(1)}, u32[]{:S(2)}, u32[]{:S(2)}) collective-permute-start(bf16[128,1152]{1,0:T(8,128)(2,1)S(1)} %get-tuple-element.22), channel_id=1, source_target_pairs={{0,32},{32,0},{1,33},{33,1},{2,34},{34,2},{3,35},{35,3},{4,36},{36... | collective-permute-start | bytes 884744 | tf_op jit(solution)/shard_map/ppermute | solution.py:19
  68.0 16.1 %collective-permute-start.15 = (bf16[256,1152]{1,0:T(8,128)(2,1)S(1)}, bf16[256,1152]{1,0:T(8,128)(2,1)S(1)}, u32[]{:S(2)}, u32[]{:S(2)}) collective-permute-start(bf16[256,1152]{1,0:T(8,128)(2,1)S(1)} %constant_dynamic-update-slice_fusion.refs_0_), channel_id=1, source_target_pairs={{0,8},{8,16},{16,24},{24,0},{1,9},{9,17},{17,25},{25,1},{2,10},{10... | collective-permute-start | bytes 1769480 | tf_op jit(solution)/shard_map/ppermute | solution.py:19
  69.6 14.7 %collective-permute-start.14 = (bf16[256,1152]{1,0:T(8,128)(2,1)S(1)}, bf16[256,1152]{1,0:T(8,128)(2,1)S(1)}, u32[]{:S(2)}, u32[]{:S(2)}) collective-permute-start(bf16[256,1152]{1,0:T(8,128)(2,1)S(1)} %constant_dynamic-update-slice_fusion.refs_0_), channel_id=1, source_target_pairs={{0,24},{8,0},{16,8},{24,16},{1,25},{9,1},{17,9},{25,17},{2,26},{10... | collective-permute-start | bytes 1769480 | tf_op jit(solution)/shard_map/ppermute | solution.py:19
  73.1 19.8 %collective-permute-start.21 = (bf16[4,4,16,1152]{3,2,1,0:T(8,128)(2,1)S(1)}, bf16[4,4,16,1152]{3,2,1,0:T(8,128)(2,1)S(1)}, u32[]{:S(2)}, u32[]{:S(2)}) collective-permute-start(bf16[4,4,16,1152]{3,2,1,0:T(8,128)(2,1)S(1)} %slice.54), channel_id=1, source_target_pairs={{0,192},{64,0},{128,64},{192,128},{1,193},{65,1},{129,65},{193,129... | collective-permute-start | bytes 1769480 | tf_op jit(solution)/shard_map/ppermute | solution.py:19
  76.6 16.2 %collective-permute-start.19 = (bf16[4,4,16,1152]{3,2,1,0:T(8,128)(2,1)S(1)}, bf16[4,4,16,1152]{3,2,1,0:T(8,128)(2,1)S(1)}, u32[]{:S(2)}, u32[]{:S(2)}) collective-permute-start(bf16[4,4,16,1152]{3,2,1,0:T(8,128)(2,1)S(1)} %slice.53), channel_id=1, source_target_pairs={{0,64},{64,128},{128,192},{192,0},{1,65},{65,129},{129,193},{193,1... | collective-permute-start | bytes 1769480 | tf_op jit(solution)/shard_map/ppermute | solution.py:19
  84.2 8.7 %collective-permute-start.16 = (bf16[128,1152]{1,0:T(8,128)(2,1)S(1)}, bf16[128,1152]{1,0:T(8,128)(2,1)S(1)}, u32[]{:S(2)}, u32[]{:S(2)}) collective-permute-start(bf16[128,1152]{1,0:T(8,128)(2,1)S(1)} %slice.51), channel_id=1, source_target_pairs={{0,8},{8,16},{16,24},{24,0},{1,9},{9,17},{17,25},{25,1},{2,10},{10... | collective-permute-start | bytes 884744 | tf_op jit(solution)/shard_map/ppermute | solution.py:19
  84.3 8.5 %collective-permute-start.17 = (bf16[128,1152]{1,0:T(8,128)(2,1)S(1)}, bf16[128,1152]{1,0:T(8,128)(2,1)S(1)}, u32[]{:S(2)}, u32[]{:S(2)}) collective-permute-start(bf16[128,1152]{1,0:T(8,128)(2,1)S(1)} %slice.52), channel_id=1, source_target_pairs={{0,24},{8,0},{16,8},{24,16},{1,25},{9,1},{17,9},{25,17},{2,26},{10... | collective-permute-start | bytes 884744 | tf_op jit(solution)/shard_map/ppermute | solution.py:19
  94.0 4.3 %collective-permute-start.22 = (f32[8,3,16,128]{3,2,1,0:T(8,128)S(1)}, f32[8,3,16,128]{3,2,1,0:T(8,128)S(1)}, u32[]{:S(2)}, u32[]{:S(2)}) collective-permute-start(f32[8,3,16,128]{3,2,1,0:T(8,128)S(1)} %get-tuple-element.27), channel_id=1, source_target_pairs={{0,32},{32,0},{1,33},{33,1},{2,34},{34,2},{3,35},{35,3},{4,36},{36... | collective-permute-start | bytes 589832 | tf_op jit(solution)/shard_map/ppermute | solution.py:19
  99.1 15.7 %all-to-all-start.1 = ((f32[8,4,16,128]{3,2,1,0:T(8,128)}), f32[8,4,16,128]{3,2,1,0:T(8,128)S(1)}, u32[]{:S(2)}, u32[]{:S(2)}) async-start(f32[8,4,16,128]{3,2,1,0:T(8,128)} %pad_maximum_fusion), calls=%async_computation.1 | async-start | bytes 524288 | tf_op jit(solution)/shard_map/all_to_all | solution.py:188
  (9 other events, 150.3 us)

commit v4 on v2

v4 whole, which is shorter than its diff:
```python
import functools
import jax
import jax.numpy as jnp
from jax import lax
from jax.experimental import pallas as pl
from jax.experimental.pallas import tpu as pltpu
from jax.sharding import Mesh, PartitionSpec as P

decay_rate = 0.9
step_size = 0.05
clip_level = 1.0
tiny_square = 1e-30
ROW = ("x", "core")
COL = ("y", "z")


def shift(value, axis, by):
    n = lax.axis_size(axis)
    return lax.ppermute(value, axis, [(i, (i + by) % n) for i in range(n)])


def pair_sum(value, axis, bit):
    n = lax.axis_size(axis)
    return value + lax.ppermute(value, axis, [(i, i ^ bit) for i in range(n)])


def spread_sum(value, axis):
    copies = jnp.broadcast_to(value[None], (lax.axis_size(axis),) + value.shape)
    return jnp.sum(lax.all_to_all(copies, axis, 0, 0, tiled=True), axis=0)


def gather4(value, axis):
    return shift(value, axis, 1), shift(value, axis, -1)


def share_kernel(source, target, done):
    n_z, n_y, part, half = target.shape
    n_core = lax.axis_size("core")
    x, core, y = lax.axis_index("x"), lax.axis_index("core"), lax.axis_index("y")
    top = pl.multiple_of(x * part, part)
    copies = []
    for j in range(n_y):
        for i in range(n_z):
            block = (y + j) % n_y * n_z + i
            left = pl.multiple_of((block * n_core + core) * half, 128)
            copy = pltpu.make_async_copy(source.at[pl.ds(top, part), pl.ds(left, half)], target.at[i, j], done.at[i, j])
            copy.start()
            copies.append(copy)
    for copy in copies:
        copy.wait()


def share_out(out_grad, n_z, n_y, part, half):
    return pl.pallas_call(
        share_kernel,
        out_shape=jax.ShapeDtypeStruct((n_z, n_y, part, half), out_grad.dtype),
        in_specs=[pl.BlockSpec(memory_space=pltpu.HBM)],
        out_specs=pl.BlockSpec(memory_space=pltpu.VMEM),
        scratch_shapes=[pltpu.SemaphoreType.DMA((n_z, n_y))],
        compiler_params=pltpu.CompilerParams(vmem_limit_bytes=56 * 1024 * 1024),
        cost_estimate=pl.CostEstimate(flops=0, bytes_accessed=4 * n_z * n_y * part * half, transcendentals=0),
    )(out_grad)


def update_kernel(entries, entry_cols, sums, state, col_out, grad, weight, residual, new_weight, row_out, kept, given):
    rows, half = kept.shape
    rows_out = decay_rate * state[...] + (1.0 - decay_rate) * sums[0:8] / entry_cols
    upd = jnp.sum(jnp.sum(sums[8:16] / rows_out, axis=0, keepdims=True), axis=1, keepdims=True)
    upd_rms = jnp.sqrt(upd / entries)
    w_rms = jnp.sqrt(jnp.sum(sums[16:17], axis=1, keepdims=True) / entries)
    factor = step_size * w_rms / jnp.maximum(1.0, upd_rms / clip_level)
    row_out[...] = rows_out[0:1]
    scale = factor * lax.rsqrt(jnp.transpose(jnp.broadcast_to(rows_out[0:1], (8, rows)))[:, :1])
    core = lax.axis_index("core")
    for target, at in ((kept, core), (given, 1 - core)):
        part = pl.ds(pl.multiple_of(at * half, 128), half)
        master = weight[:, part].astype(jnp.float32) + residual[:, part].astype(jnp.float32)
        delta = grad[:, part].astype(jnp.float32) * (scale * lax.rsqrt(col_out[:, part]))
        new = (master - delta).astype(jnp.bfloat16)
        target[...] = new
        new_weight[:, part] = new


def update(entries, entry_cols, sums, state, col_out, arrays, half):
    rows, cols = arrays[0].shape
    vmem = pl.BlockSpec(memory_space=pltpu.VMEM)
    return pl.pallas_call(
        functools.partial(update_kernel, entries, entry_cols),
        out_shape=(
            jax.ShapeDtypeStruct((rows, cols), jnp.bfloat16),
            jax.ShapeDtypeStruct((1, rows), jnp.float32),
            jax.ShapeDtypeStruct((rows, half), jnp.bfloat16),
            jax.ShapeDtypeStruct((rows, half), jnp.bfloat16),
        ),
        in_specs=[vmem] * 6,
        out_specs=(vmem,) * 4,
        compiler_params=pltpu.CompilerParams(vmem_limit_bytes=16 * 1024 * 1024),
    )(sums, state, col_out, *arrays)


def joined(refs):
    return jnp.concatenate([ref[...] for ref in refs], axis=0)


def tokens_of(refs, j):
    return jnp.concatenate([ref[:, j].reshape(ref.shape[0] * ref.shape[2], ref.shape[3]) for ref in refs], axis=0)


def times(tokens, weights):
    return lax.dot_general(tokens, weights, (((1,), (1,)), ((), ())), preferred_element_type=jnp.float32)


def near_kernel(places, *refs):
    count = 2 * len(places)
    weights, tokens, total_ref = refs[:count], refs[count:-1], refs[-1]
    total = 0.0
    for n, j in enumerate(places):
        total += times(tokens_of(tokens, j), joined(weights[2 * n : 2 * n + 2]))
    total_ref[...] = total


def all_kernel(places, far, *refs):
    count = 2 * len(places)
    weights, far_weights, refs = refs[:count], refs[count : count + 2], refs[count + 2 :]
    tokens, far_tokens, partial, (mine, other) = refs[: len(places)], refs[len(places) : -3], refs[-3], refs[-2:]
    n_z, _, part, rows = mine.shape
    far_weight = joined(far_weights)
    near_total = partial[...] + times(tokens_of(tokens, far), far_weight)
    far_total = times(tokens_of(far_tokens, far), far_weight)
    for n, j in enumerate(places):
        far_total += times(tokens_of(far_tokens, j), joined(weights[2 * n : 2 * n + 2]))
    for place, total in enumerate([*near_total.reshape(-1, n_z, part, 2 * rows), far_total.reshape(n_z, part, 2 * rows)]):
        mine[:, place] = total[:, :, :rows]
        other[:, place] = total[:, :, rows:]


def near_products(weights, tokens, places):
    operands = [w for pair in weights for w in pair] + list(tokens)
    n_z, _, part, half = tokens[0].shape
    rows = weights[0][0].shape[0]
    shape = (len(tokens) * n_z * part, 2 * rows)
    return pl.pallas_call(
        functools.partial(near_kernel, places),
        out_shape=jax.ShapeDtypeStruct(shape, jnp.float32),
        in_specs=[pl.BlockSpec(memory_space=pltpu.VMEM)] * len(operands),
        out_specs=pl.BlockSpec(memory_space=pltpu.VMEM),
        compiler_params=pltpu.CompilerParams(vmem_limit_bytes=40 * 1024 * 1024),
        cost_estimate=pl.CostEstimate(
            flops=10 * shape[0] * shape[1] * len(places) * half,
            bytes_accessed=2 * sum(o.size for o in operands) + 4 * shape[0] * shape[1],
            transcendentals=0,
        ),
    )(*operands)


def all_products(weights, far_weights, tokens, far_tokens, partial, places):
    operands = [w for pair in weights for w in pair] + [*far_weights, *tokens, *far_tokens, partial]
    n_z, n_y, part, half = tokens[0].shape
    rows = far_weights[0].shape[0]
    out = jax.ShapeDtypeStruct((n_z, len(tokens) + 1, part, rows), jnp.float32)
    return pl.pallas_call(
        functools.partial(all_kernel, places, 2),
        out_shape=(out, out),
        in_specs=[pl.BlockSpec(memory_space=pltpu.VMEM)] * len(operands),
        out_specs=(pl.BlockSpec(memory_space=pltpu.VMEM),) * 2,
        compiler_params=pltpu.CompilerParams(vmem_limit_bytes=40 * 1024 * 1024),
        cost_estimate=pl.CostEstimate(
            flops=4 * (len(tokens) + n_y) * n_z * part * rows * half,
            bytes_accessed=2 * sum(o.size for o in operands),
            transcendentals=0,
        ),
    )(*operands)


def body(grad, weight, residual, row_state, col_state, out_grad):
    rows, cols = grad.shape
    tokens = out_grad.shape[0]
    n_x, n_core, n_y, n_z = (lax.axis_size(a) for a in ("x", "core", "y", "z"))
    x = lax.axis_index("x")
    all_rows, all_cols = rows * n_x * n_core, cols * n_y * n_z
    part, half = tokens // n_x, cols // n_core

    share = share_out(out_grad, n_z, n_y, part, half)
    share = lax.all_to_all(share, "z", 0, 0, tiled=True)

    grad_full = grad.astype(jnp.float32)
    squares = grad_full * grad_full + tiny_square
    col_part = jnp.sum(squares, axis=0).reshape(cols // 128, 128)
    col_total = pair_sum(col_part, "core", 1)
    col_total = col_total + shift(col_total, "x", 1) + shift(col_total, "x", 2) + shift(col_total, "x", 3)
    col_out = decay_rate * col_state + (1.0 - decay_rate) * col_total.reshape(cols) / all_rows
    master = weight.astype(jnp.float32) + residual.astype(jnp.float32)
    row_part = jnp.sum(squares, axis=1)
    scaled_part = jnp.sum(grad_full * grad_full * (1.0 / col_out)[None, :], axis=1)
    w_part = jnp.sum(master * master, axis=1)
    four = jnp.stack([row_part, scaled_part, w_part, row_state])
    two = jnp.stack([four, shift(four, "core", 1)], axis=1)
    parts = jnp.concatenate([two, shift(two, "x", 1), shift(two, "x", 2), shift(two, "x", 3)], axis=1)
    w_sum = jnp.sum(parts[2], axis=0, keepdims=True)
    sums = jnp.concatenate([parts[0], parts[1], w_sum, jnp.zeros((7, rows), jnp.float32)])
    sums = pair_sum(pair_sum(sums, "y", 1), "y", 2)
    sums = pair_sum(sums, "z", 1)
    sums, share = lax.optimization_barrier((sums, share))
    before, after = gather4(share, "x")
    sums = pair_sum(pair_sum(sums, "z", 2), "z", 4)

    new_weight, row_out, kept, given = update(
        all_rows * all_cols, all_cols, sums, parts[3], col_out[None], (grad, weight, residual), half
    )
    taken = shift(given, "core", 1)
    kept_before, taken_after = shift(kept, "y", 1), shift(taken, "y", -1)
    taken_before, kept_after = shift(taken, "y", 1), shift(kept, "y", -1)
    far_low = shift(before[: n_z // 2], "x", 1)
    far_high = shift(after[n_z // 2 :], "x", -1)
    kept_far = shift(kept_before, "y", 1)
    taken_far = shift(taken_after, "y", -1)
    kept_far, taken_far, far_low, far_high = lax.optimization_barrier((kept_far, taken_far, far_low, far_high))
    near_weights = ((kept, taken), (kept_after, taken_after), (kept_before, taken_before))
    near_tokens = (share, after, before)
    partial = near_products(near_weights, near_tokens, (0, 1, 3))
    mine, other = all_products(near_weights, (kept_far, taken_far), near_tokens, (far_low, far_high), partial, (0, 1, 3))
    total = mine + shift(other, "core", 1)
    total = lax.all_to_all(total, "z", 0, 0, tiled=True)
    summed = jnp.sum(total, axis=0)
    summed = jnp.stack([summed[0], summed[1], summed[3], summed[2]])
    summed = lax.dynamic_slice_in_dim(jnp.concatenate([summed, summed]), (n_x - x) % n_x, n_x, 0)
    input_grad = summed.reshape(tokens, rows).astype(jnp.bfloat16)
    return (new_weight, row_out.reshape(rows), col_out, input_grad)


def solution(mesh):
    fine = Mesh(mesh.devices.reshape(4, 2, 4, 8), ("x", "core", "y", "z"))
    in_specs = (P(ROW, COL), P(ROW, COL), P(ROW, COL), P(ROW), P(COL), P(COL, None))
    out_specs = (P(ROW, COL), P(ROW), P(COL), P(COL, ROW))
    return jax.shard_map(body, mesh=fine, in_specs=in_specs, out_specs=out_specs, check_vma=False)
```

time: 120 us -> 111 us (0.925)
  waiting for transfers between devices: 62.5 us -> 50.3 us
  starting transfers between devices: 46 us -> 50.7 us
    ppermute x20 -> x19, waiting for transfers between devices: 26.7 us -> 18.6 us  [shift(): return lax.ppermute(value, axis, [(i, (i + by) % n) for i in range(n)])]
    all_to_all x1, waiting for transfers between devices: 6.91 us -> 4.16 us  [body(): share = lax.all_to_all(share, 'z', 0, 0, tiled=True)]
    ppermute x20 -> x19, starting transfers between devices: 28.2 us -> 30.6 us  [shift(): return lax.ppermute(value, axis, [(i, (i + by) % n) for i in range(n)])]
    ppermute x6, starting transfers between devices: 5.3 us -> 7.55 us  [pair_sum(): return value + lax.ppermute(value, axis, [(i, i ^ bit) for i in range(n)])]
  transfers between devices with their start and end apart: 28 -> 27, of which waited for: 22 -> 19; matrix products, arithmetic and copies ran while one was open for 1% -> 1% of each run, Pallas kernels for 3% -> 2%
where the time goes in v4:
time: 111 us; the launch traced here: 110 us
  starting transfers between devices  50.7 us (46%)
  waiting for transfers between devices  50.3 us (45%)
  Pallas kernels  5.86 us (5%)
  other arithmetic  1.77 us (2%)
    ppermute x19, starting transfers between devices, shift(): return lax.ppermute(value, axis, [(i, (i + by) % n) for i in range(n)])  30.6 us
    ppermute x19, waiting for transfers between devices, shift(): return lax.ppermute(value, axis, [(i, (i + by) % n) for i in range(n)])  18.6 us
    ppermute x6, waiting for transfers between devices, pair_sum(): return value + lax.ppermute(value, axis, [(i, i ^ bit) for i in range(n)])  15.4 us
    all_to_all x1, waiting for transfers between devices, body(): total = lax.all_to_all(total, 'z', 0, 0, tiled=True)  12.2 us
    all_to_all x1, starting transfers between devices, body(): share = lax.all_to_all(share, 'z', 0, 0, tiled=True)  9.16 us
    ppermute x6, starting transfers between devices, pair_sum(): return value + lax.ppermute(value, axis, [(i, i ^ bit) for i in range(n)])  7.55 us
    all_to_all x1, waiting for transfers between devices, body(): share = lax.all_to_all(share, 'z', 0, 0, tiled=True)  4.16 us
    all_to_all x1, starting transfers between devices, body(): total = lax.all_to_all(total, 'z', 0, 0, tiled=True)  3.41 us
  transfers between devices with their start and end apart: 27, of which 19 were waited for; matrix products, arithmetic and copies ran while one was open for 1% of the time, Pallas kernels for 2%

profile of v4, /device:TPU:1, one launch (start us, length us, event | category | flops | bytes accessed | tf_op | source)
XLA Modules:
  0.0 110.5 jit_solution(8235967950655015666)
XLA Ops:
  0.6 2.6 %shard_map.93 = bf16[8,4,16,1152]{3,2,1,0:T(8,128)(2,1)} custom-call(bf16[64,73728]{1,0:T(8,128)(2,1)} %source.1), custom_call_target="tpu_custom_call" | custom-call | bytes 2359296 | tf_op jit(solution)/shard_map/pallas_call | solution.py:54
  3.3 9.2 %all-to-all-start = ((bf16[8,4,16,1152]{3,2,1,0:T(8,128)(2,1)}), bf16[8,4,16,1152]{3,2,1,0:T(8,128)(2,1)S(1)}, u32[]{:S(2)}, u32[]{:S(2)}) async-start(bf16[8,4,16,1152]{3,2,1,0:T(8,128)(2,1)} %shard_map.93), calls=%async_computation | async-start | bytes 2359296 | tf_op jit(solution)/shard_map/all_to_all | solution.py:184
  14.6 2.5 %collective-permute-start.3 = (f32[18,128]{1,0:T(8,128)S(1)}, f32[18,128]{1,0:T(8,128)S(1)}, u32[]{:S(2)}, u32[]{:S(2)}) collective-permute-start(f32[18,128]{1,0:T(8,128)S(1)} %bitcast_add_fusion.1), channel_id=1, source_target_pairs={{0,192},{64,0},{128,64},{192,128},{1,193},{65,1},{129,65},{193,129... | collective-permute-start | bytes 27656 | tf_op jit(solution)/shard_map/ppermute | solution.py:19
  18.5 2.9 %collective-permute-done.2 = f32[18,128]{1,0:T(8,128)S(1)} collective-permute-done((f32[18,128]{1,0:T(8,128)S(1)}, f32[18,128]{1,0:T(8,128)S(1)}, u32[]{:S(2)}, u32[]{:S(2)}) %collective-permute-start.2) | collective-permute-done | bytes 9248 | tf_op jit(solution)/shard_map/ppermute | solution.py:19
  21.9 1.8 %collective-permute-start.4 = (f32[4,128]{1,0:T(4,128)S(1)}, f32[4,128]{1,0:T(4,128)S(1)}, u32[]{:S(2)}, u32[]{:S(2)}) collective-permute-start(f32[4,128]{1,0:T(4,128)S(1)} %pad_maximum_fusion.1), channel_id=1, source_target_pairs={{0,32},{32,0},{1,33},{33,1},{2,34},{34,2},{3,35},{35,3},{4,36},{36... | collective-permute-start | bytes 6152 | tf_op jit(solution)/shard_map/ppermute | solution.py:19
  26.0 2.0 %collective-permute-start.7 = (f32[4,2,128]{2,1,0:T(2,128)S(1)}, f32[4,2,128]{2,1,0:T(2,128)S(1)}, u32[]{:S(2)}, u32[]{:S(2)}) collective-permute-start(f32[4,2,128]{2,1,0:T(2,128)S(1)} %pad_maximum_fusion), channel_id=1, source_target_pairs={{0,192},{64,0},{128,64},{192,128},{1,193},{65,1},{129,65},{193,129... | collective-permute-start | bytes 12296 | tf_op jit(solution)/shard_map/ppermute | solution.py:19
  30.7 1.5 %collective-permute-done.8 = f32[24,128]{1,0:T(8,128)S(1)} collective-permute-done((f32[24,128]{1,0:T(8,128)S(1)}, f32[24,128]{1,0:T(8,128)S(1)}, u32[]{:S(2)}, u32[]{:S(2)}) %collective-permute-start.8) | collective-permute-done | bytes 12320 | tf_op jit(solution)/shard_map/ppermute | solution.py:24
  32.3 2.9 %collective-permute-start.9 = (f32[24,128]{1,0:T(8,128)S(1)}, f32[24,128]{1,0:T(8,128)S(1)}, u32[]{:S(2)}, u32[]{:S(2)}) collective-permute-start(f32[24,128]{1,0:T(8,128)S(1)} %fusion.3), channel_id=1, source_target_pairs={{0,16},{8,24},{16,0},{24,8},{1,17},{9,25},{17,1},{25,9},{2,18},{10... | collective-permute-start | bytes 36872 | tf_op jit(solution)/shard_map/ppermute | solution.py:24
  36.6 1.9 %collective-permute-start.10 = (f32[24,128]{1,0:T(8,128)S(1)}, f32[24,128]{1,0:T(8,128)S(1)}, u32[]{:S(2)}, u32[]{:S(2)}) collective-permute-start(f32[24,128]{1,0:T(8,128)S(1)} %add.58), channel_id=1, source_target_pairs={{0,1},{1,0},{2,3},{3,2},{4,5},{5,4},{6,7},{7,6},{8,9},{9,8},{10,11... | collective-permute-start | bytes 36872 | tf_op jit(solution)/shard_map/ppermute | solution.py:24
  38.5 1.8 %collective-permute-done.10 = f32[24,128]{1,0:T(8,128)S(1)} collective-permute-done((f32[24,128]{1,0:T(8,128)S(1)}, f32[24,128]{1,0:T(8,128)S(1)}, u32[]{:S(2)}, u32[]{:S(2)}) %collective-permute-start.10) | collective-permute-done | bytes 12320 | tf_op jit(solution)/shard_map/ppermute | solution.py:24
  40.3 4.2 %all-to-all-done.refs_6_.refs_8_ = bf16[8,4,16,1152]{3,2,1,0:T(8,128)(2,1)S(1)} async-done(((bf16[8,4,16,1152]{3,2,1,0:T(8,128)(2,1)}), bf16[8,4,16,1152]{3,2,1,0:T(8,128)(2,1)S(1)}, u32[]{:S(2)}, u32[]{:S(2)}) %all-to-all-start) | async-done | bytes 1179680 | tf_op jit(solution)/shard_map/all_to_all | solution.py:184
  45.7 1.5 %collective-permute-start.22 = (bf16[8,4,16,1152]{3,2,1,0:T(8,128)(2,1)S(1)}, bf16[8,4,16,1152]{3,2,1,0:T(8,128)(2,1)S(1)}, u32[]{:S(2)}, u32[]{:S(2)}) collective-permute-start(bf16[8,4,16,1152]{3,2,1,0:T(8,128)(2,1)S(1)} %all-to-all-done.refs_6_.refs_8_), channel_id=1, source_target_pairs={{0,192},{64,0},{128,64},{192,128},{1,193},{65,1},{129,65},{193,129... | collective-permute-start | bytes 3538952 | tf_op jit(solution)/shard_map/ppermute | solution.py:19
  47.1 3.7 %collective-permute-done.11 = f32[24,128]{1,0:T(8,128)S(1)} collective-permute-done((f32[24,128]{1,0:T(8,128)S(1)}, f32[24,128]{1,0:T(8,128)S(1)}, u32[]{:S(2)}, u32[]{:S(2)}) %collective-permute-start.11) | collective-permute-done | bytes 12320 | tf_op jit(solution)/shard_map/ppermute | solution.py:24
  51.3 6.1 %collective-permute-done.12 = f32[24,128]{1,0:T(8,128)S(1)} collective-permute-done((f32[24,128]{1,0:T(8,128)S(1)}, f32[24,128]{1,0:T(8,128)S(1)}, u32[]{:S(2)}, u32[]{:S(2)}) %collective-permute-start.12) | collective-permute-done | bytes 12320 | tf_op jit(solution)/shard_map/ppermute | solution.py:24
  58.6 3.2 %collective-permute-start.13 = (bf16[128,1152]{1,0:T(8,128)(2,1)S(1)}, bf16[128,1152]{1,0:T(8,128)(2,1)S(1)}, u32[]{:S(2)}, u32[]{:S(2)}) collective-permute-start(bf16[128,1152]{1,0:T(8,128)(2,1)S(1)} %get-tuple-element.20), channel_id=1, source_target_pairs={{0,32},{32,0},{1,33},{33,1},{2,34},{34,2},{3,35},{35,3},{4,36},{36... | collective-permute-start | bytes 884744 | tf_op jit(solution)/shard_map/ppermute | solution.py:19
  61.8 2.7 %collective-permute-start.14 = (bf16[128,1152]{1,0:T(8,128)(2,1)S(1)}, bf16[128,1152]{1,0:T(8,128)(2,1)S(1)}, u32[]{:S(2)}, u32[]{:S(2)}) collective-permute-start(bf16[128,1152]{1,0:T(8,128)(2,1)S(1)} %get-tuple-element.19.refs_0_), channel_id=1, source_target_pairs={{0,24},{8,0},{16,8},{24,16},{1,25},{9,1},{17,9},{25,17},{2,26},{10... | collective-permute-start | bytes 884744 | tf_op jit(solution)/shard_map/ppermute | solution.py:19
  64.5 2.7 %collective-permute-start.15 = (bf16[128,1152]{1,0:T(8,128)(2,1)S(1)}, bf16[128,1152]{1,0:T(8,128)(2,1)S(1)}, u32[]{:S(2)}, u32[]{:S(2)}) collective-permute-start(bf16[128,1152]{1,0:T(8,128)(2,1)S(1)} %collective-permute-done.13.refs_1_), channel_id=1, source_target_pairs={{0,24},{8,0},{16,8},{24,16},{1,25},{9,1},{17,9},{25,17},{2,26},{10... | collective-permute-start | bytes 884744 | tf_op jit(solution)/shard_map/ppermute | solution.py:19
  67.2 5.4 %collective-permute-done.20.refs_8_.refs_10_ = bf16[8,4,16,1152]{3,2,1,0:T(8,128)(2,1)S(1)} collective-permute-done((bf16[8,4,16,1152]{3,2,1,0:T(8,128)(2,1)S(1)}, bf16[8,4,16,1152]{3,2,1,0:T(8,128)(2,1)S(1)}, u32[]{:S(2)}, u32[]{:S(2)}) %collective-permute-start.20) | collective-permute-done | bytes 1179680 | tf_op jit(solution)/shard_map/ppermute | solution.py:19
  74.1 2.7 %collective-permute-start.23 = (bf16[4,4,16,1152]{3,2,1,0:T(8,128)(2,1)S(1)}, bf16[4,4,16,1152]{3,2,1,0:T(8,128)(2,1)S(1)}, u32[]{:S(2)}, u32[]{:S(2)}) collective-permute-start(bf16[4,4,16,1152]{3,2,1,0:T(8,128)(2,1)S(1)} %slice.44), channel_id=1, source_target_pairs={{0,192},{64,0},{128,64},{192,128},{1,193},{65,1},{129,65},{193,129... | collective-permute-start | bytes 1769480 | tf_op jit(solution)/shard_map/ppermute | solution.py:19
  78.2 2.4 %collective-permute-start.19 = (bf16[128,1152]{1,0:T(8,128)(2,1)S(1)}, bf16[128,1152]{1,0:T(8,128)(2,1)S(1)}, u32[]{:S(2)}, u32[]{:S(2)}) collective-permute-start(bf16[128,1152]{1,0:T(8,128)(2,1)S(1)} %collective-permute-done.15.refs_3_), channel_id=1, source_target_pairs={{0,24},{8,0},{16,8},{24,16},{1,25},{9,1},{17,9},{25,17},{2,26},{10... | collective-permute-start | bytes 884744 | tf_op jit(solution)/shard_map/ppermute | solution.py:19
  81.9 5.4 %collective-permute-done.18.refs_6_ = bf16[128,1152]{1,0:T(8,128)(2,1)S(1)} collective-permute-done((bf16[128,1152]{1,0:T(8,128)(2,1)S(1)}, bf16[128,1152]{1,0:T(8,128)(2,1)S(1)}, u32[]{:S(2)}, u32[]{:S(2)}) %collective-permute-start.18) | collective-permute-done | bytes 294944 | tf_op jit(solution)/shard_map/ppermute | solution.py:19
  89.5 2.7 %collective-permute-start.24 = (f32[8,4,16,128]{3,2,1,0:T(8,128)S(1)}, f32[8,4,16,128]{3,2,1,0:T(8,128)S(1)}, u32[]{:S(2)}, u32[]{:S(2)}) collective-permute-start(f32[8,4,16,128]{3,2,1,0:T(8,128)S(1)} %get-tuple-element.27), channel_id=1, source_target_pairs={{0,32},{32,0},{1,33},{33,1},{2,34},{34,2},{3,35},{35,3},{4,36},{36... | collective-permute-start | bytes 786440 | tf_op jit(solution)/shard_map/ppermute | solution.py:19
  94.1 3.4 %all-to-all-start.1 = ((f32[8,4,16,128]{3,2,1,0:T(8,128)}), f32[8,4,16,128]{3,2,1,0:T(8,128)S(1)}, u32[]{:S(2)}, u32[]{:S(2)}) async-start(f32[8,4,16,128]{3,2,1,0:T(8,128)} %add.62), calls=%async_computation.1 | async-start | bytes 524288 | tf_op jit(solution)/shard_map/all_to_all | solution.py:223
  97.5 12.2 %all-to-all-done.1 = f32[8,4,16,128]{3,2,1,0:T(8,128)S(1)} async-done(((f32[8,4,16,128]{3,2,1,0:T(8,128)}), f32[8,4,16,128]{3,2,1,0:T(8,128)S(1)}, u32[]{:S(2)}, u32[]{:S(2)}) %all-to-all-start.1) | async-done | bytes 262176 | tf_op jit(solution)/shard_map/all_to_all | solution.py:223
  (75 shorter events, 22.1 us)
Async XLA Ops:
  3.3 41.2 %all-to-all-start = ((bf16[8,4,16,1152]{3,2,1,0:T(8,128)(2,1)}), bf16[8,4,16,1152]{3,2,1,0:T(8,128)(2,1)S(1)}, u32[]{:S(2)}, u32[]{:S(2)}) async-start(bf16[8,4,16,1152]{3,2,1,0:T(8,128)(2,1)} %shard_map.93), calls=%async_computation | async-start | bytes 2359296 | tf_op jit(solution)/shard_map/all_to_all | solution.py:184
  14.6 3.9 %collective-permute-start.3 = (f32[18,128]{1,0:T(8,128)S(1)}, f32[18,128]{1,0:T(8,128)S(1)}, u32[]{:S(2)}, u32[]{:S(2)}) collective-permute-start(f32[18,128]{1,0:T(8,128)S(1)} %bitcast_add_fusion.1), channel_id=1, source_target_pairs={{0,192},{64,0},{128,64},{192,128},{1,193},{65,1},{129,65},{193,129... | collective-permute-start | bytes 27656 | tf_op jit(solution)/shard_map/ppermute | solution.py:19
  17.1 4.3 %collective-permute-start.2 = (f32[18,128]{1,0:T(8,128)S(1)}, f32[18,128]{1,0:T(8,128)S(1)}, u32[]{:S(2)}, u32[]{:S(2)}) collective-permute-start(f32[18,128]{1,0:T(8,128)S(1)} %bitcast_add_fusion.1), channel_id=1, source_target_pairs={{0,128},{64,192},{128,0},{192,64},{1,129},{65,193},{129,1},{193,65... | collective-permute-start | bytes 27656 | tf_op jit(solution)/shard_map/ppermute | solution.py:19
  17.6 4.1 %collective-permute-start.1 = (f32[18,128]{1,0:T(8,128)S(1)}, f32[18,128]{1,0:T(8,128)S(1)}, u32[]{:S(2)}, u32[]{:S(2)}) collective-permute-start(f32[18,128]{1,0:T(8,128)S(1)} %bitcast_add_fusion.1), channel_id=1, source_target_pairs={{0,64},{64,128},{128,192},{192,0},{1,65},{65,129},{129,193},{193,1... | collective-permute-start | bytes 27656 | tf_op jit(solution)/shard_map/ppermute | solution.py:19
  24.6 4.0 %collective-permute-start.5 = (f32[4,2,128]{2,1,0:T(2,128)S(1)}, f32[4,2,128]{2,1,0:T(2,128)S(1)}, u32[]{:S(2)}, u32[]{:S(2)}) collective-permute-start(f32[4,2,128]{2,1,0:T(2,128)S(1)} %pad_maximum_fusion), channel_id=1, source_target_pairs={{0,64},{64,128},{128,192},{192,0},{1,65},{65,129},{129,193},{193,1... | collective-permute-start | bytes 12296 | tf_op jit(solution)/shard_map/ppermute | solution.py:19
  24.7 4.2 %collective-permute-start.6 = (f32[4,2,128]{2,1,0:T(2,128)S(1)}, f32[4,2,128]{2,1,0:T(2,128)S(1)}, u32[]{:S(2)}, u32[]{:S(2)}) collective-permute-start(f32[4,2,128]{2,1,0:T(2,128)S(1)} %pad_maximum_fusion), channel_id=1, source_target_pairs={{0,128},{64,192},{128,0},{192,64},{1,129},{65,193},{129,1},{193,65... | collective-permute-start | bytes 12296 | tf_op jit(solution)/shard_map/ppermute | solution.py:19
  26.0 3.2 %collective-permute-start.7 = (f32[4,2,128]{2,1,0:T(2,128)S(1)}, f32[4,2,128]{2,1,0:T(2,128)S(1)}, u32[]{:S(2)}, u32[]{:S(2)}) collective-permute-start(f32[4,2,128]{2,1,0:T(2,128)S(1)} %pad_maximum_fusion), channel_id=1, source_target_pairs={{0,192},{64,0},{128,64},{192,128},{1,193},{65,1},{129,65},{193,129... | collective-permute-start | bytes 12296 | tf_op jit(solution)/shard_map/ppermute | solution.py:19
  32.3 4.3 %collective-permute-start.9 = (f32[24,128]{1,0:T(8,128)S(1)}, f32[24,128]{1,0:T(8,128)S(1)}, u32[]{:S(2)}, u32[]{:S(2)}) collective-permute-start(f32[24,128]{1,0:T(8,128)S(1)} %fusion.3), channel_id=1, source_target_pairs={{0,16},{8,24},{16,0},{24,8},{1,17},{9,25},{17,1},{25,9},{2,18},{10... | collective-permute-start | bytes 36872 | tf_op jit(solution)/shard_map/ppermute | solution.py:24
  36.6 3.7 %collective-permute-start.10 = (f32[24,128]{1,0:T(8,128)S(1)}, f32[24,128]{1,0:T(8,128)S(1)}, u32[]{:S(2)}, u32[]{:S(2)}) collective-permute-start(f32[24,128]{1,0:T(8,128)S(1)} %add.58), channel_id=1, source_target_pairs={{0,1},{1,0},{2,3},{3,2},{4,5},{5,4},{6,7},{7,6},{8,9},{9,8},{10,11... | collective-permute-start | bytes 36872 | tf_op jit(solution)/shard_map/ppermute | solution.py:24
  44.5 28.1 %collective-permute-start.20 = (bf16[8,4,16,1152]{3,2,1,0:T(8,128)(2,1)S(1)}, bf16[8,4,16,1152]{3,2,1,0:T(8,128)(2,1)S(1)}, u32[]{:S(2)}, u32[]{:S(2)}) collective-permute-start(bf16[8,4,16,1152]{3,2,1,0:T(8,128)(2,1)S(1)} %all-to-all-done.refs_6_.refs_8_), channel_id=1, source_target_pairs={{0,64},{64,128},{128,192},{192,0},{1,65},{65,129},{129,193},{193,1... | collective-permute-start | bytes 3538952 | tf_op jit(solution)/shard_map/ppermute | solution.py:19
  45.7 28.3 %collective-permute-start.22 = (bf16[8,4,16,1152]{3,2,1,0:T(8,128)(2,1)S(1)}, bf16[8,4,16,1152]{3,2,1,0:T(8,128)(2,1)S(1)}, u32[]{:S(2)}, u32[]{:S(2)}) collective-permute-start(bf16[8,4,16,1152]{3,2,1,0:T(8,128)(2,1)S(1)} %all-to-all-done.refs_6_.refs_8_), channel_id=1, source_target_pairs={{0,192},{64,0},{128,64},{192,128},{1,193},{65,1},{129,65},{193,129... | collective-permute-start | bytes 3538952 | tf_op jit(solution)/shard_map/ppermute | solution.py:19
  47.1 3.7 %collective-permute-start.11 = (f32[24,128]{1,0:T(8,128)S(1)}, f32[24,128]{1,0:T(8,128)S(1)}, u32[]{:S(2)}, u32[]{:S(2)}) collective-permute-start(f32[24,128]{1,0:T(8,128)S(1)} %add.59), channel_id=1, source_target_pairs={{0,2},{1,3},{2,0},{3,1},{4,6},{5,7},{6,4},{7,5},{8,10},{9,11},{10,... | collective-permute-start | bytes 36872 | tf_op jit(solution)/shard_map/ppermute | solution.py:24
  50.9 6.5 %collective-permute-start.12 = (f32[24,128]{1,0:T(8,128)S(1)}, f32[24,128]{1,0:T(8,128)S(1)}, u32[]{:S(2)}, u32[]{:S(2)}) collective-permute-start(f32[24,128]{1,0:T(8,128)S(1)} %add.60), channel_id=1, source_target_pairs={{0,4},{1,5},{2,6},{3,7},{4,0},{5,1},{6,2},{7,3},{8,12},{9,13},{10,... | collective-permute-start | bytes 36872 | tf_op jit(solution)/shard_map/ppermute | solution.py:24
  58.6 5.9 %collective-permute-start.13 = (bf16[128,1152]{1,0:T(8,128)(2,1)S(1)}, bf16[128,1152]{1,0:T(8,128)(2,1)S(1)}, u32[]{:S(2)}, u32[]{:S(2)}) collective-permute-start(bf16[128,1152]{1,0:T(8,128)(2,1)S(1)} %get-tuple-element.20), channel_id=1, source_target_pairs={{0,32},{32,0},{1,33},{33,1},{2,34},{34,2},{3,35},{35,3},{4,36},{36... | collective-permute-start | bytes 884744 | tf_op jit(solution)/shard_map/ppermute | solution.py:19
  61.8 12.4 %collective-permute-start.14 = (bf16[128,1152]{1,0:T(8,128)(2,1)S(1)}, bf16[128,1152]{1,0:T(8,128)(2,1)S(1)}, u32[]{:S(2)}, u32[]{:S(2)}) collective-permute-start(bf16[128,1152]{1,0:T(8,128)(2,1)S(1)} %get-tuple-element.19.refs_0_), channel_id=1, source_target_pairs={{0,24},{8,0},{16,8},{24,16},{1,25},{9,1},{17,9},{25,17},{2,26},{10... | collective-permute-start | bytes 884744 | tf_op jit(solution)/shard_map/ppermute | solution.py:19
  64.5 12.4 %collective-permute-start.16 = (bf16[128,1152]{1,0:T(8,128)(2,1)S(1)}, bf16[128,1152]{1,0:T(8,128)(2,1)S(1)}, u32[]{:S(2)}, u32[]{:S(2)}) collective-permute-start(bf16[128,1152]{1,0:T(8,128)(2,1)S(1)} %get-tuple-element.19.refs_0_), channel_id=1, source_target_pairs={{0,8},{8,16},{16,24},{24,0},{1,9},{9,17},{17,25},{25,1},{2,10},{10... | collective-permute-start | bytes 884744 | tf_op jit(solution)/shard_map/ppermute | solution.py:19
  64.5 13.7 %collective-permute-start.15 = (bf16[128,1152]{1,0:T(8,128)(2,1)S(1)}, bf16[128,1152]{1,0:T(8,128)(2,1)S(1)}, u32[]{:S(2)}, u32[]{:S(2)}) collective-permute-start(bf16[128,1152]{1,0:T(8,128)(2,1)S(1)} %collective-permute-done.13.refs_1_), channel_id=1, source_target_pairs={{0,24},{8,0},{16,8},{24,16},{1,25},{9,1},{17,9},{25,17},{2,26},{10... | collective-permute-start | bytes 884744 | tf_op jit(solution)/shard_map/ppermute | solution.py:19
  72.6 8.4 %collective-permute-start.17 = (bf16[128,1152]{1,0:T(8,128)(2,1)S(1)}, bf16[128,1152]{1,0:T(8,128)(2,1)S(1)}, u32[]{:S(2)}, u32[]{:S(2)}) collective-permute-start(bf16[128,1152]{1,0:T(8,128)(2,1)S(1)} %collective-permute-done.13.refs_1_), channel_id=1, source_target_pairs={{0,8},{8,16},{16,24},{24,0},{1,9},{9,17},{17,25},{25,1},{2,10},{10... | collective-permute-start | bytes 884744 | tf_op jit(solution)/shard_map/ppermute | solution.py:19
  74.0 14.4 %collective-permute-start.21 = (bf16[4,4,16,1152]{3,2,1,0:T(8,128)(2,1)S(1)}, bf16[4,4,16,1152]{3,2,1,0:T(8,128)(2,1)S(1)}, u32[]{:S(2)}, u32[]{:S(2)}) collective-permute-start(bf16[4,4,16,1152]{3,2,1,0:T(8,128)(2,1)S(1)} %slice.43), channel_id=1, source_target_pairs={{0,64},{64,128},{128,192},{192,0},{1,65},{65,129},{129,193},{193,1... | collective-permute-start | bytes 1769480 | tf_op jit(solution)/shard_map/ppermute | solution.py:19
  74.1 14.2 %collective-permute-start.23 = (bf16[4,4,16,1152]{3,2,1,0:T(8,128)(2,1)S(1)}, bf16[4,4,16,1152]{3,2,1,0:T(8,128)(2,1)S(1)}, u32[]{:S(2)}, u32[]{:S(2)}) collective-permute-start(bf16[4,4,16,1152]{3,2,1,0:T(8,128)(2,1)S(1)} %slice.44), channel_id=1, source_target_pairs={{0,192},{64,0},{128,64},{192,128},{1,193},{65,1},{129,65},{193,129... | collective-permute-start | bytes 1769480 | tf_op jit(solution)/shard_map/ppermute | solution.py:19
  76.9 10.5 %collective-permute-start.18 = (bf16[128,1152]{1,0:T(8,128)(2,1)S(1)}, bf16[128,1152]{1,0:T(8,128)(2,1)S(1)}, u32[]{:S(2)}, u32[]{:S(2)}) collective-permute-start(bf16[128,1152]{1,0:T(8,128)(2,1)S(1)} %collective-permute-done.16.refs_4_), channel_id=1, source_target_pairs={{0,8},{8,16},{16,24},{24,0},{1,9},{9,17},{17,25},{25,1},{2,10},{10... | collective-permute-start | bytes 884744 | tf_op jit(solution)/shard_map/ppermute | solution.py:19
  78.2 9.2 %collective-permute-start.19 = (bf16[128,1152]{1,0:T(8,128)(2,1)S(1)}, bf16[128,1152]{1,0:T(8,128)(2,1)S(1)}, u32[]{:S(2)}, u32[]{:S(2)}) collective-permute-start(bf16[128,1152]{1,0:T(8,128)(2,1)S(1)} %collective-permute-done.15.refs_3_), channel_id=1, source_target_pairs={{0,24},{8,0},{16,8},{24,16},{1,25},{9,1},{17,9},{25,17},{2,26},{10... | collective-permute-start | bytes 884744 | tf_op jit(solution)/shard_map/ppermute | solution.py:19
  89.5 3.9 %collective-permute-start.24 = (f32[8,4,16,128]{3,2,1,0:T(8,128)S(1)}, f32[8,4,16,128]{3,2,1,0:T(8,128)S(1)}, u32[]{:S(2)}, u32[]{:S(2)}) collective-permute-start(f32[8,4,16,128]{3,2,1,0:T(8,128)S(1)} %get-tuple-element.27), channel_id=1, source_target_pairs={{0,32},{32,0},{1,33},{33,1},{2,34},{34,2},{3,35},{35,3},{4,36},{36... | collective-permute-start | bytes 786440 | tf_op jit(solution)/shard_map/ppermute | solution.py:19
  94.1 15.7 %all-to-all-start.1 = ((f32[8,4,16,128]{3,2,1,0:T(8,128)}), f32[8,4,16,128]{3,2,1,0:T(8,128)S(1)}, u32[]{:S(2)}, u32[]{:S(2)}) async-start(f32[8,4,16,128]{3,2,1,0:T(8,128)} %add.62), calls=%async_computation.1 | async-start | bytes 524288 | tf_op jit(solution)/shard_map/all_to_all | solution.py:223
  (9 other events, 102.2 us)

commit v5 on v4

--- a/solution.py
+++ b/solution.py
@@ -22,6 +22,10 @@
 def pair_sum(value, axis, bit):
     n = lax.axis_size(axis)
     return value + lax.ppermute(value, axis, [(i, i ^ bit) for i in range(n)])
+
+
+def swap(value, axis, bits):
+    return lax.ppermute(value, axis, [(i, i ^ bits) for i in range(lax.axis_size(axis))])
 
 
 def spread_sum(value, axis):
@@ -110,25 +114,31 @@
     return lax.dot_general(tokens, weights, (((1,), (1,)), ((), ())), preferred_element_type=jnp.float32)
 
 
-def near_kernel(places, *refs):
-    count = 2 * len(places)
-    weights, tokens, total_ref = refs[:count], refs[count:-1], refs[-1]
+def split_weights(sizes, refs):
+    weights = []
+    for size in sizes:
+        weights.append(joined(refs[:size]))
+        refs = refs[size:]
+    return weights, refs
+
+
+def near_kernel(sizes, places, *refs):
+    weights, refs = split_weights(sizes, refs)
+    tokens, total_ref = refs[:-1], refs[-1]
     total = 0.0
-    for n, j in enumerate(places):
-        total += times(tokens_of(tokens, j), joined(weights[2 * n : 2 * n + 2]))
+    for weight, j in zip(weights, places):
+        total += times(tokens_of(tokens, j), weight)
     total_ref[...] = total
 
 
-def all_kernel(places, far, *refs):
-    count = 2 * len(places)
-    weights, far_weights, refs = refs[:count], refs[count : count + 2], refs[count + 2 :]
-    tokens, far_tokens, partial, (mine, other) = refs[: len(places)], refs[len(places) : -3], refs[-3], refs[-2:]
+def all_kernel(sizes, places, far, *refs):
+    (*weights, far_weight), refs = split_weights((*sizes, 2), refs)
+    tokens, far_tokens, partial, (mine, other) = refs[:-5], refs[-5:-3], refs[-3], refs[-2:]
     n_z, _, part, rows = mine.shape
-    far_weight = joined(far_weights)
     near_total = partial[...] + times(tokens_of(tokens, far), far_weight)
     far_total = times(tokens_of(far_tokens, far), far_weight)
-    for n, j in enumerate(places):
-        far_total += times(tokens_of(far_tokens, j), joined(weights[2 * n : 2 * n + 2]))
+    for weight, j in zip(weights, places):
+        far_total += times(tokens_of(far_tokens, j), weight)
     for place, total in enumerate([*near_total.reshape(-1, n_z, part, 2 * rows), far_total.reshape(n_z, part, 2 * rows)]):
         mine[:, place] = total[:, :, :rows]
         other[:, place] = total[:, :, rows:]
@@ -140,7 +150,7 @@
     rows = weights[0][0].shape[0]
     shape = (len(tokens) * n_z * part, 2 * rows)
     return pl.pallas_call(
-        functools.partial(near_kernel, places),
+        functools.partial(near_kernel, tuple(map(len, weights)), places),
         out_shape=jax.ShapeDtypeStruct(shape, jnp.float32),
         in_specs=[pl.BlockSpec(memory_space=pltpu.VMEM)] * len(operands),
         out_specs=pl.BlockSpec(memory_space=pltpu.VMEM),
@@ -159,7 +169,7 @@
     rows = far_weights[0].shape[0]
     out = jax.ShapeDtypeStruct((n_z, len(tokens) + 1, part, rows), jnp.float32)
     return pl.pallas_call(
-        functools.partial(all_kernel, places, 2),
+        functools.partial(all_kernel, tuple(map(len, weights)), places, 2),
         out_shape=(out, out),
         in_specs=[pl.BlockSpec(memory_space=pltpu.VMEM)] * len(operands),
         out_specs=(pl.BlockSpec(memory_space=pltpu.VMEM),) * 2,
@@ -202,20 +212,20 @@
     sums = pair_sum(sums, "z", 1)
     sums, share = lax.optimization_barrier((sums, share))
     before, after = gather4(share, "x")
-    sums = pair_sum(pair_sum(sums, "z", 2), "z", 4)
+    sums = (sums + swap(sums, "z", 2)) + (swap(sums, "z", 4) + swap(sums, "z", 6))
 
     new_weight, row_out, kept, given = update(
         all_rows * all_cols, all_cols, sums, parts[3], col_out[None], (grad, weight, residual), half
     )
     taken = shift(given, "core", 1)
-    kept_before, taken_after = shift(kept, "y", 1), shift(taken, "y", -1)
-    taken_before, kept_after = shift(taken, "y", 1), shift(kept, "y", -1)
+    w_before = shift(jnp.concatenate([kept, taken]), "y", 1)
+    taken_after, kept_after = shift(taken, "y", -1), shift(kept, "y", -1)
     far_low = shift(before[: n_z // 2], "x", 1)
     far_high = shift(after[n_z // 2 :], "x", -1)
-    kept_far = shift(kept_before, "y", 1)
+    kept_far = shift(w_before[:rows], "y", 1)
     taken_far = shift(taken_after, "y", -1)
     kept_far, taken_far, far_low, far_high = lax.optimization_barrier((kept_far, taken_far, far_low, far_high))
-    near_weights = ((kept, taken), (kept_after, taken_after), (kept_before, taken_before))
+    near_weights = ((kept, taken), (kept_after, taken_after), (w_before,))
     near_tokens = (share, after, before)
     partial = near_products(near_weights, near_tokens, (0, 1, 3))
     mine, other = all_products(near_weights, (kept_far, taken_far), near_tokens, (far_low, far_high), partial, (0, 1, 3))

time: 111 us -> 110 us (level)
  waiting for transfers between devices: 50.3 us -> 46 us
  starting transfers between devices: 50.7 us -> 53.7 us
    ppermute x6 -> x4, waiting for transfers between devices: 15.4 us -> 5.57 us  [pair_sum(): return value + lax.ppermute(value, axis, [(i, i ^ bit) for i in range(n)])]
    ppermute x0 -> x3, starting transfers between devices: none -> 5.66 us  [swap(): lax.ppermute(value, axis, [(i, i ^ bits) for i in range(lax.axis_size(axi...]
    ppermute x19 -> x18, waiting for transfers between devices: 18.6 us -> 22.6 us  [shift(): return lax.ppermute(value, axis, [(i, (i + by) % n) for i in range(n)])]
    ppermute x19 -> x18, starting transfers between devices: 30.6 us -> 28.3 us  [shift(): return lax.ppermute(value, axis, [(i, (i + by) % n) for i in range(n)])]
    ppermute x0 -> x3, waiting for transfers between devices: none -> 1.37 us  [swap(): lax.ppermute(value, axis, [(i, i ^ bits) for i in range(lax.axis_size(axi...]
    ppermute x6 -> x4, starting transfers between devices: 7.55 us -> 7.17 us  [pair_sum(): return value + lax.ppermute(value, axis, [(i, i ^ bit) for i in range(n)])]
  transfers between devices with their start and end apart: 27 -> 27, of which waited for: 19 -> 20; matrix products, arithmetic and copies ran while one was open for 1% -> 1% of each run, Pallas kernels for 2% -> 2%
where the time goes in v5:
time: 110 us; the launch traced here: 109 us
  starting transfers between devices  53.7 us (49%)
  waiting for transfers between devices  46 us (42%)
  Pallas kernels  5.86 us (5%)
  other arithmetic  1.82 us (2%)
    ppermute x18, starting transfers between devices, shift(): return lax.ppermute(value, axis, [(i, (i + by) % n) for i in range(n)])  28.3 us
    ppermute x18, waiting for transfers between devices, shift(): return lax.ppermute(value, axis, [(i, (i + by) % n) for i in range(n)])  22.6 us
    all_to_all x1, waiting for transfers between devices, body(): total = lax.all_to_all(total, 'z', 0, 0, tiled=True)  12.2 us
    all_to_all x1, starting transfers between devices, body(): share = lax.all_to_all(share, 'z', 0, 0, tiled=True)  9.16 us
    ppermute x4, starting transfers between devices, pair_sum(): return value + lax.ppermute(value, axis, [(i, i ^ bit) for i in range(n)])  7.17 us
    ppermute x3, starting transfers between devices, swap(): lax.ppermute(value, axis, [(i, i ^ bits) for i in range(lax.axis_size(axi...  5.66 us
    ppermute x4, waiting for transfers between devices, pair_sum(): return value + lax.ppermute(value, axis, [(i, i ^ bit) for i in range(n)])  5.57 us
    all_to_all x1, waiting for transfers between devices, body(): share = lax.all_to_all(share, 'z', 0, 0, tiled=True)  4.16 us
  transfers between devices with their start and end apart: 27, of which 20 were waited for; matrix products, arithmetic and copies ran while one was open for 1% of the time, Pallas kernels for 2%

profile of v5, /device:TPU:1, one launch (start us, length us, event | category | flops | bytes accessed | tf_op | source)
XLA Modules:
  0.0 109.2 jit_solution(12582331025186276107)
XLA Ops:
  0.6 2.6 %shard_map.93 = bf16[8,4,16,1152]{3,2,1,0:T(8,128)(2,1)} custom-call(bf16[64,73728]{1,0:T(8,128)(2,1)} %source.1), custom_call_target="tpu_custom_call" | custom-call | bytes 2359296 | tf_op jit(solution)/shard_map/pallas_call | solution.py:58
  3.3 9.2 %all-to-all-start = ((bf16[8,4,16,1152]{3,2,1,0:T(8,128)(2,1)}), bf16[8,4,16,1152]{3,2,1,0:T(8,128)(2,1)S(1)}, u32[]{:S(2)}, u32[]{:S(2)}) async-start(bf16[8,4,16,1152]{3,2,1,0:T(8,128)(2,1)} %shard_map.93), calls=%async_computation | async-start | bytes 2359296 | tf_op jit(solution)/shard_map/all_to_all | solution.py:194
  14.6 2.5 %collective-permute-start.3 = (f32[18,128]{1,0:T(8,128)S(1)}, f32[18,128]{1,0:T(8,128)S(1)}, u32[]{:S(2)}, u32[]{:S(2)}) collective-permute-start(f32[18,128]{1,0:T(8,128)S(1)} %bitcast_add_fusion.1), channel_id=1, source_target_pairs={{0,192},{64,0},{128,64},{192,128},{1,193},{65,1},{129,65},{193,129... | collective-permute-start | bytes 27656 | tf_op jit(solution)/shard_map/ppermute | solution.py:19
  18.5 2.9 %collective-permute-done.2 = f32[18,128]{1,0:T(8,128)S(1)} collective-permute-done((f32[18,128]{1,0:T(8,128)S(1)}, f32[18,128]{1,0:T(8,128)S(1)}, u32[]{:S(2)}, u32[]{:S(2)}) %collective-permute-start.2) | collective-permute-done | bytes 9248 | tf_op jit(solution)/shard_map/ppermute | solution.py:19
  21.9 1.8 %collective-permute-start.4 = (f32[4,128]{1,0:T(4,128)S(1)}, f32[4,128]{1,0:T(4,128)S(1)}, u32[]{:S(2)}, u32[]{:S(2)}) collective-permute-start(f32[4,128]{1,0:T(4,128)S(1)} %pad_maximum_fusion.2), channel_id=1, source_target_pairs={{0,32},{32,0},{1,33},{33,1},{2,34},{34,2},{3,35},{35,3},{4,36},{36... | collective-permute-start | bytes 6152 | tf_op jit(solution)/shard_map/ppermute | solution.py:19
  26.0 2.0 %collective-permute-start.7 = (f32[4,2,128]{2,1,0:T(2,128)S(1)}, f32[4,2,128]{2,1,0:T(2,128)S(1)}, u32[]{:S(2)}, u32[]{:S(2)}) collective-permute-start(f32[4,2,128]{2,1,0:T(2,128)S(1)} %pad_maximum_fusion.1), channel_id=1, source_target_pairs={{0,192},{64,0},{128,64},{192,128},{1,193},{65,1},{129,65},{193,129... | collective-permute-start | bytes 12296 | tf_op jit(solution)/shard_map/ppermute | solution.py:19
  30.7 1.5 %collective-permute-done.8 = f32[24,128]{1,0:T(8,128)S(1)} collective-permute-done((f32[24,128]{1,0:T(8,128)S(1)}, f32[24,128]{1,0:T(8,128)S(1)}, u32[]{:S(2)}, u32[]{:S(2)}) %collective-permute-start.8) | collective-permute-done | bytes 12320 | tf_op jit(solution)/shard_map/ppermute | solution.py:24
  32.3 2.9 %collective-permute-start.9 = (f32[24,128]{1,0:T(8,128)S(1)}, f32[24,128]{1,0:T(8,128)S(1)}, u32[]{:S(2)}, u32[]{:S(2)}) collective-permute-start(f32[24,128]{1,0:T(8,128)S(1)} %fusion.3), channel_id=1, source_target_pairs={{0,16},{8,24},{16,0},{24,8},{1,17},{9,25},{17,1},{25,9},{2,18},{10... | collective-permute-start | bytes 36872 | tf_op jit(solution)/shard_map/ppermute | solution.py:24
  36.6 1.9 %collective-permute-start.10 = (f32[24,128]{1,0:T(8,128)S(1)}, f32[24,128]{1,0:T(8,128)S(1)}, u32[]{:S(2)}, u32[]{:S(2)}) collective-permute-start(f32[24,128]{1,0:T(8,128)S(1)} %add.61), channel_id=1, source_target_pairs={{0,1},{1,0},{2,3},{3,2},{4,5},{5,4},{6,7},{7,6},{8,9},{9,8},{10,11... | collective-permute-start | bytes 36872 | tf_op jit(solution)/shard_map/ppermute | solution.py:24
  38.5 1.8 %collective-permute-done.10 = f32[24,128]{1,0:T(8,128)S(1)} collective-permute-done((f32[24,128]{1,0:T(8,128)S(1)}, f32[24,128]{1,0:T(8,128)S(1)}, u32[]{:S(2)}, u32[]{:S(2)}) %collective-permute-start.10) | collective-permute-done | bytes 12320 | tf_op jit(solution)/shard_map/ppermute | solution.py:24
  40.3 4.2 %all-to-all-done.refs_5_.refs_7_ = bf16[8,4,16,1152]{3,2,1,0:T(8,128)(2,1)S(1)} async-done(((bf16[8,4,16,1152]{3,2,1,0:T(8,128)(2,1)}), bf16[8,4,16,1152]{3,2,1,0:T(8,128)(2,1)S(1)}, u32[]{:S(2)}, u32[]{:S(2)}) %all-to-all-start) | async-done | bytes 1179680 | tf_op jit(solution)/shard_map/all_to_all | solution.py:194
  45.7 1.5 %collective-permute-start.22 = (bf16[8,4,16,1152]{3,2,1,0:T(8,128)(2,1)S(1)}, bf16[8,4,16,1152]{3,2,1,0:T(8,128)(2,1)S(1)}, u32[]{:S(2)}, u32[]{:S(2)}) collective-permute-start(bf16[8,4,16,1152]{3,2,1,0:T(8,128)(2,1)S(1)} %all-to-all-done.refs_5_.refs_7_), channel_id=1, source_target_pairs={{0,192},{64,0},{128,64},{192,128},{1,193},{65,1},{129,65},{193,129... | collective-permute-start | bytes 3538952 | tf_op jit(solution)/shard_map/ppermute | solution.py:19
  48.8 4.1 %collective-permute-start.11 = (f32[24,128]{1,0:T(8,128)S(1)}, f32[24,128]{1,0:T(8,128)S(1)}, u32[]{:S(2)}, u32[]{:S(2)}) collective-permute-start(f32[24,128]{1,0:T(8,128)S(1)} %add.62), channel_id=1, source_target_pairs={{0,2},{1,3},{2,0},{3,1},{4,6},{5,7},{6,4},{7,5},{8,10},{9,11},{10,... | collective-permute-start | bytes 36872 | tf_op jit(solution)/shard_map/ppermute | solution.py:28
  55.4 4.5 %collective-permute-start.14 = (bf16[128,1152]{1,0:T(8,128)(2,1)S(1)}, bf16[128,1152]{1,0:T(8,128)(2,1)S(1)}, u32[]{:S(2)}, u32[]{:S(2)}) collective-permute-start(bf16[128,1152]{1,0:T(8,128)(2,1)S(1)} %get-tuple-element.20), channel_id=1, source_target_pairs={{0,32},{32,0},{1,33},{33,1},{2,34},{34,2},{3,35},{35,3},{4,36},{36... | collective-permute-start | bytes 884744 | tf_op jit(solution)/shard_map/ppermute | solution.py:19
  62.6 1.5 %collective-permute-start.16 = (bf16[128,1152]{1,0:T(8,128)(2,1)S(1)}, bf16[128,1152]{1,0:T(8,128)(2,1)S(1)}, u32[]{:S(2)}, u32[]{:S(2)}) collective-permute-start(bf16[128,1152]{1,0:T(8,128)(2,1)S(1)} %collective-permute-done.14.refs_1_), channel_id=1, source_target_pairs={{0,24},{8,0},{16,8},{24,16},{1,25},{9,1},{17,9},{25,17},{2,26},{10... | collective-permute-start | bytes 884744 | tf_op jit(solution)/shard_map/ppermute | solution.py:19
  65.5 7.1 %collective-permute-done.20.refs_7_.refs_9_ = bf16[8,4,16,1152]{3,2,1,0:T(8,128)(2,1)S(1)} collective-permute-done((bf16[8,4,16,1152]{3,2,1,0:T(8,128)(2,1)S(1)}, bf16[8,4,16,1152]{3,2,1,0:T(8,128)(2,1)S(1)}, u32[]{:S(2)}, u32[]{:S(2)}) %collective-permute-start.20) | collective-permute-done | bytes 1179680 | tf_op jit(solution)/shard_map/ppermute | solution.py:19
  72.8 2.7 %collective-permute-start.23 = (bf16[4,4,16,1152]{3,2,1,0:T(8,128)(2,1)S(1)}, bf16[4,4,16,1152]{3,2,1,0:T(8,128)(2,1)S(1)}, u32[]{:S(2)}, u32[]{:S(2)}) collective-permute-start(bf16[4,4,16,1152]{3,2,1,0:T(8,128)(2,1)S(1)} %slice.49), channel_id=1, source_target_pairs={{0,192},{64,0},{128,64},{192,128},{1,193},{65,1},{129,65},{193,129... | collective-permute-start | bytes 1769480 | tf_op jit(solution)/shard_map/ppermute | solution.py:19
  75.6 2.7 %collective-permute-start.19 = (bf16[128,1152]{1,0:T(8,128)(2,1)S(1)}, bf16[128,1152]{1,0:T(8,128)(2,1)S(1)}, u32[]{:S(2)}, u32[]{:S(2)}) collective-permute-start(bf16[128,1152]{1,0:T(8,128)(2,1)S(1)} %collective-permute-done.16.refs_3_), channel_id=1, source_target_pairs={{0,24},{8,0},{16,8},{24,16},{1,25},{9,1},{17,9},{25,17},{2,26},{10... | collective-permute-start | bytes 884744 | tf_op jit(solution)/shard_map/ppermute | solution.py:19
  79.4 3.2 %collective-permute-done.19.refs_6_ = bf16[128,1152]{1,0:T(8,128)(2,1)S(1)} collective-permute-done((bf16[128,1152]{1,0:T(8,128)(2,1)S(1)}, bf16[128,1152]{1,0:T(8,128)(2,1)S(1)}, u32[]{:S(2)}, u32[]{:S(2)}) %collective-permute-start.19) | collective-permute-done | bytes 294944 | tf_op jit(solution)/shard_map/ppermute | solution.py:19
  82.6 3.2 %collective-permute-done.18.refs_5_ = bf16[128,1152]{1,0:T(8,128)(2,1)S(1)} collective-permute-done((bf16[128,1152]{1,0:T(8,128)(2,1)S(1)}, bf16[128,1152]{1,0:T(8,128)(2,1)S(1)}, u32[]{:S(2)}, u32[]{:S(2)}) %collective-permute-start.18) | collective-permute-done | bytes 294944 | tf_op jit(solution)/shard_map/ppermute | solution.py:19
  85.8 1.5 %collective-permute-done.21.refs_10_ = bf16[4,4,16,1152]{3,2,1,0:T(8,128)(2,1)S(1)} collective-permute-done((bf16[4,4,16,1152]{3,2,1,0:T(8,128)(2,1)S(1)}, bf16[4,4,16,1152]{3,2,1,0:T(8,128)(2,1)S(1)}, u32[]{:S(2)}, u32[]{:S(2)}) %collective-permute-start.21) | collective-permute-done | bytes 589856 | tf_op jit(solution)/shard_map/ppermute | solution.py:19
  88.4 2.5 %collective-permute-start.24 = (f32[8,4,16,128]{3,2,1,0:T(8,128)S(1)}, f32[8,4,16,128]{3,2,1,0:T(8,128)S(1)}, u32[]{:S(2)}, u32[]{:S(2)}) collective-permute-start(f32[8,4,16,128]{3,2,1,0:T(8,128)S(1)} %get-tuple-element.27), channel_id=1, source_target_pairs={{0,32},{32,0},{1,33},{33,1},{2,34},{34,2},{3,35},{35,3},{4,36},{36... | collective-permute-start | bytes 786440 | tf_op jit(solution)/shard_map/ppermute | solution.py:19
  92.8 3.4 %all-to-all-start.1 = ((f32[8,4,16,128]{3,2,1,0:T(8,128)}), f32[8,4,16,128]{3,2,1,0:T(8,128)S(1)}, u32[]{:S(2)}, u32[]{:S(2)}) async-start(f32[8,4,16,128]{3,2,1,0:T(8,128)} %add.66), calls=%async_computation.1 | async-start | bytes 524288 | tf_op jit(solution)/shard_map/all_to_all | solution.py:233
  96.2 12.2 %all-to-all-done.1 = f32[8,4,16,128]{3,2,1,0:T(8,128)S(1)} async-done(((f32[8,4,16,128]{3,2,1,0:T(8,128)}), f32[8,4,16,128]{3,2,1,0:T(8,128)S(1)}, u32[]{:S(2)}, u32[]{:S(2)}) %all-to-all-start.1) | async-done | bytes 262176 | tf_op jit(solution)/shard_map/all_to_all | solution.py:233
  (76 shorter events, 24.8 us)
Async XLA Ops:
  3.3 41.2 %all-to-all-start = ((bf16[8,4,16,1152]{3,2,1,0:T(8,128)(2,1)}), bf16[8,4,16,1152]{3,2,1,0:T(8,128)(2,1)S(1)}, u32[]{:S(2)}, u32[]{:S(2)}) async-start(bf16[8,4,16,1152]{3,2,1,0:T(8,128)(2,1)} %shard_map.93), calls=%async_computation | async-start | bytes 2359296 | tf_op jit(solution)/shard_map/all_to_all | solution.py:194
  14.6 3.9 %collective-permute-start.3 = (f32[18,128]{1,0:T(8,128)S(1)}, f32[18,128]{1,0:T(8,128)S(1)}, u32[]{:S(2)}, u32[]{:S(2)}) collective-permute-start(f32[18,128]{1,0:T(8,128)S(1)} %bitcast_add_fusion.1), channel_id=1, source_target_pairs={{0,192},{64,0},{128,64},{192,128},{1,193},{65,1},{129,65},{193,129... | collective-permute-start | bytes 27656 | tf_op jit(solution)/shard_map/ppermute | solution.py:19
  17.1 4.3 %collective-permute-start.2 = (f32[18,128]{1,0:T(8,128)S(1)}, f32[18,128]{1,0:T(8,128)S(1)}, u32[]{:S(2)}, u32[]{:S(2)}) collective-permute-start(f32[18,128]{1,0:T(8,128)S(1)} %bitcast_add_fusion.1), channel_id=1, source_target_pairs={{0,128},{64,192},{128,0},{192,64},{1,129},{65,193},{129,1},{193,65... | collective-permute-start | bytes 27656 | tf_op jit(solution)/shard_map/ppermute | solution.py:19
  17.6 4.1 %collective-permute-start.1 = (f32[18,128]{1,0:T(8,128)S(1)}, f32[18,128]{1,0:T(8,128)S(1)}, u32[]{:S(2)}, u32[]{:S(2)}) collective-permute-start(f32[18,128]{1,0:T(8,128)S(1)} %bitcast_add_fusion.1), channel_id=1, source_target_pairs={{0,64},{64,128},{128,192},{192,0},{1,65},{65,129},{129,193},{193,1... | collective-permute-start | bytes 27656 | tf_op jit(solution)/shard_map/ppermute | solution.py:19
  24.6 4.0 %collective-permute-start.5 = (f32[4,2,128]{2,1,0:T(2,128)S(1)}, f32[4,2,128]{2,1,0:T(2,128)S(1)}, u32[]{:S(2)}, u32[]{:S(2)}) collective-permute-start(f32[4,2,128]{2,1,0:T(2,128)S(1)} %pad_maximum_fusion.1), channel_id=1, source_target_pairs={{0,64},{64,128},{128,192},{192,0},{1,65},{65,129},{129,193},{193,1... | collective-permute-start | bytes 12296 | tf_op jit(solution)/shard_map/ppermute | solution.py:19
  24.7 4.2 %collective-permute-start.6 = (f32[4,2,128]{2,1,0:T(2,128)S(1)}, f32[4,2,128]{2,1,0:T(2,128)S(1)}, u32[]{:S(2)}, u32[]{:S(2)}) collective-permute-start(f32[4,2,128]{2,1,0:T(2,128)S(1)} %pad_maximum_fusion.1), channel_id=1, source_target_pairs={{0,128},{64,192},{128,0},{192,64},{1,129},{65,193},{129,1},{193,65... | collective-permute-start | bytes 12296 | tf_op jit(solution)/shard_map/ppermute | solution.py:19
  26.0 3.2 %collective-permute-start.7 = (f32[4,2,128]{2,1,0:T(2,128)S(1)}, f32[4,2,128]{2,1,0:T(2,128)S(1)}, u32[]{:S(2)}, u32[]{:S(2)}) collective-permute-start(f32[4,2,128]{2,1,0:T(2,128)S(1)} %pad_maximum_fusion.1), channel_id=1, source_target_pairs={{0,192},{64,0},{128,64},{192,128},{1,193},{65,1},{129,65},{193,129... | collective-permute-start | bytes 12296 | tf_op jit(solution)/shard_map/ppermute | solution.py:19
  32.3 4.3 %collective-permute-start.9 = (f32[24,128]{1,0:T(8,128)S(1)}, f32[24,128]{1,0:T(8,128)S(1)}, u32[]{:S(2)}, u32[]{:S(2)}) collective-permute-start(f32[24,128]{1,0:T(8,128)S(1)} %fusion.3), channel_id=1, source_target_pairs={{0,16},{8,24},{16,0},{24,8},{1,17},{9,25},{17,1},{25,9},{2,18},{10... | collective-permute-start | bytes 36872 | tf_op jit(solution)/shard_map/ppermute | solution.py:24
  36.6 3.7 %collective-permute-start.10 = (f32[24,128]{1,0:T(8,128)S(1)}, f32[24,128]{1,0:T(8,128)S(1)}, u32[]{:S(2)}, u32[]{:S(2)}) collective-permute-start(f32[24,128]{1,0:T(8,128)S(1)} %add.61), channel_id=1, source_target_pairs={{0,1},{1,0},{2,3},{3,2},{4,5},{5,4},{6,7},{7,6},{8,9},{9,8},{10,11... | collective-permute-start | bytes 36872 | tf_op jit(solution)/shard_map/ppermute | solution.py:24
  44.5 28.1 %collective-permute-start.20 = (bf16[8,4,16,1152]{3,2,1,0:T(8,128)(2,1)S(1)}, bf16[8,4,16,1152]{3,2,1,0:T(8,128)(2,1)S(1)}, u32[]{:S(2)}, u32[]{:S(2)}) collective-permute-start(bf16[8,4,16,1152]{3,2,1,0:T(8,128)(2,1)S(1)} %all-to-all-done.refs_5_.refs_7_), channel_id=1, source_target_pairs={{0,64},{64,128},{128,192},{192,0},{1,65},{65,129},{129,193},{193,1... | collective-permute-start | bytes 3538952 | tf_op jit(solution)/shard_map/ppermute | solution.py:19
  45.7 27.1 %collective-permute-start.22 = (bf16[8,4,16,1152]{3,2,1,0:T(8,128)(2,1)S(1)}, bf16[8,4,16,1152]{3,2,1,0:T(8,128)(2,1)S(1)}, u32[]{:S(2)}, u32[]{:S(2)}) collective-permute-start(bf16[8,4,16,1152]{3,2,1,0:T(8,128)(2,1)S(1)} %all-to-all-done.refs_5_.refs_7_), channel_id=1, source_target_pairs={{0,192},{64,0},{128,64},{192,128},{1,193},{65,1},{129,65},{193,129... | collective-permute-start | bytes 3538952 | tf_op jit(solution)/shard_map/ppermute | solution.py:19
  47.1 6.5 %collective-permute-start.12 = (f32[24,128]{1,0:T(8,128)S(1)}, f32[24,128]{1,0:T(8,128)S(1)}, u32[]{:S(2)}, u32[]{:S(2)}) collective-permute-start(f32[24,128]{1,0:T(8,128)S(1)} %add.62), channel_id=1, source_target_pairs={{0,4},{1,5},{2,6},{3,7},{4,0},{5,1},{6,2},{7,3},{8,12},{9,13},{10,... | collective-permute-start | bytes 36872 | tf_op jit(solution)/shard_map/ppermute | solution.py:28
  47.8 5.8 %collective-permute-start.13 = (f32[24,128]{1,0:T(8,128)S(1)}, f32[24,128]{1,0:T(8,128)S(1)}, u32[]{:S(2)}, u32[]{:S(2)}) collective-permute-start(f32[24,128]{1,0:T(8,128)S(1)} %add.62), channel_id=1, source_target_pairs={{0,6},{1,7},{2,4},{3,5},{4,2},{5,3},{6,0},{7,1},{8,14},{9,15},{10,... | collective-permute-start | bytes 36872 | tf_op jit(solution)/shard_map/ppermute | solution.py:28
  48.8 5.4 %collective-permute-start.11 = (f32[24,128]{1,0:T(8,128)S(1)}, f32[24,128]{1,0:T(8,128)S(1)}, u32[]{:S(2)}, u32[]{:S(2)}) collective-permute-start(f32[24,128]{1,0:T(8,128)S(1)} %add.62), channel_id=1, source_target_pairs={{0,2},{1,3},{2,0},{3,1},{4,6},{5,7},{6,4},{7,5},{8,10},{9,11},{10,... | collective-permute-start | bytes 36872 | tf_op jit(solution)/shard_map/ppermute | solution.py:28
  55.4 5.7 %collective-permute-start.14 = (bf16[128,1152]{1,0:T(8,128)(2,1)S(1)}, bf16[128,1152]{1,0:T(8,128)(2,1)S(1)}, u32[]{:S(2)}, u32[]{:S(2)}) collective-permute-start(bf16[128,1152]{1,0:T(8,128)(2,1)S(1)} %get-tuple-element.20), channel_id=1, source_target_pairs={{0,32},{32,0},{1,33},{33,1},{2,34},{34,2},{3,35},{35,3},{4,36},{36... | collective-permute-start | bytes 884744 | tf_op jit(solution)/shard_map/ppermute | solution.py:19
  61.2 17.1 %collective-permute-start.17 = (bf16[256,1152]{1,0:T(8,128)(2,1)S(1)}, bf16[256,1152]{1,0:T(8,128)(2,1)S(1)}, u32[]{:S(2)}, u32[]{:S(2)}) collective-permute-start(bf16[256,1152]{1,0:T(8,128)(2,1)S(1)} %pad_maximum_fusion), channel_id=1, source_target_pairs={{0,8},{8,16},{16,24},{24,0},{1,9},{9,17},{17,25},{25,1},{2,10},{10... | collective-permute-start | bytes 1769480 | tf_op jit(solution)/shard_map/ppermute | solution.py:19
  62.6 13.0 %collective-permute-start.16 = (bf16[128,1152]{1,0:T(8,128)(2,1)S(1)}, bf16[128,1152]{1,0:T(8,128)(2,1)S(1)}, u32[]{:S(2)}, u32[]{:S(2)}) collective-permute-start(bf16[128,1152]{1,0:T(8,128)(2,1)S(1)} %collective-permute-done.14.refs_1_), channel_id=1, source_target_pairs={{0,24},{8,0},{16,8},{24,16},{1,25},{9,1},{17,9},{25,17},{2,26},{10... | collective-permute-start | bytes 884744 | tf_op jit(solution)/shard_map/ppermute | solution.py:19
  64.1 14.3 %collective-permute-start.15 = (bf16[128,1152]{1,0:T(8,128)(2,1)S(1)}, bf16[128,1152]{1,0:T(8,128)(2,1)S(1)}, u32[]{:S(2)}, u32[]{:S(2)}) collective-permute-start(bf16[128,1152]{1,0:T(8,128)(2,1)S(1)} %get-tuple-element.19.refs_0_), channel_id=1, source_target_pairs={{0,24},{8,0},{16,8},{24,16},{1,25},{9,1},{17,9},{25,17},{2,26},{10... | collective-permute-start | bytes 884744 | tf_op jit(solution)/shard_map/ppermute | solution.py:19
  72.7 14.7 %collective-permute-start.21 = (bf16[4,4,16,1152]{3,2,1,0:T(8,128)(2,1)S(1)}, bf16[4,4,16,1152]{3,2,1,0:T(8,128)(2,1)S(1)}, u32[]{:S(2)}, u32[]{:S(2)}) collective-permute-start(bf16[4,4,16,1152]{3,2,1,0:T(8,128)(2,1)S(1)} %slice.48), channel_id=1, source_target_pairs={{0,64},{64,128},{128,192},{192,0},{1,65},{65,129},{129,193},{193,1... | collective-permute-start | bytes 1769480 | tf_op jit(solution)/shard_map/ppermute | solution.py:19
  72.8 14.5 %collective-permute-start.23 = (bf16[4,4,16,1152]{3,2,1,0:T(8,128)(2,1)S(1)}, bf16[4,4,16,1152]{3,2,1,0:T(8,128)(2,1)S(1)}, u32[]{:S(2)}, u32[]{:S(2)}) collective-permute-start(bf16[4,4,16,1152]{3,2,1,0:T(8,128)(2,1)S(1)} %slice.49), channel_id=1, source_target_pairs={{0,192},{64,0},{128,64},{192,128},{1,193},{65,1},{129,65},{193,129... | collective-permute-start | bytes 1769480 | tf_op jit(solution)/shard_map/ppermute | solution.py:19
  75.6 7.0 %collective-permute-start.19 = (bf16[128,1152]{1,0:T(8,128)(2,1)S(1)}, bf16[128,1152]{1,0:T(8,128)(2,1)S(1)}, u32[]{:S(2)}, u32[]{:S(2)}) collective-permute-start(bf16[128,1152]{1,0:T(8,128)(2,1)S(1)} %collective-permute-done.16.refs_3_), channel_id=1, source_target_pairs={{0,24},{8,0},{16,8},{24,16},{1,25},{9,1},{17,9},{25,17},{2,26},{10... | collective-permute-start | bytes 884744 | tf_op jit(solution)/shard_map/ppermute | solution.py:19
  78.3 7.5 %collective-permute-start.18 = (bf16[128,1152]{1,0:T(8,128)(2,1)S(1)}, bf16[128,1152]{1,0:T(8,128)(2,1)S(1)}, u32[]{:S(2)}, u32[]{:S(2)}) collective-permute-start(bf16[128,1152]{1,0:T(8,128)(2,1)S(1)} %slice.47), channel_id=1, source_target_pairs={{0,8},{8,16},{16,24},{24,0},{1,9},{9,17},{17,25},{25,1},{2,10},{10... | collective-permute-start | bytes 884744 | tf_op jit(solution)/shard_map/ppermute | solution.py:19
  88.4 3.6 %collective-permute-start.24 = (f32[8,4,16,128]{3,2,1,0:T(8,128)S(1)}, f32[8,4,16,128]{3,2,1,0:T(8,128)S(1)}, u32[]{:S(2)}, u32[]{:S(2)}) collective-permute-start(f32[8,4,16,128]{3,2,1,0:T(8,128)S(1)} %get-tuple-element.27), channel_id=1, source_target_pairs={{0,32},{32,0},{1,33},{33,1},{2,34},{34,2},{3,35},{35,3},{4,36},{36... | collective-permute-start | bytes 786440 | tf_op jit(solution)/shard_map/ppermute | solution.py:19
  92.8 15.7 %all-to-all-start.1 = ((f32[8,4,16,128]{3,2,1,0:T(8,128)}), f32[8,4,16,128]{3,2,1,0:T(8,128)S(1)}, u32[]{:S(2)}, u32[]{:S(2)}) async-start(f32[8,4,16,128]{3,2,1,0:T(8,128)} %add.66), calls=%async_computation.1 | async-start | bytes 524288 | tf_op jit(solution)/shard_map/all_to_all | solution.py:233
  (9 other events, 99.0 us)

commit v6 on v5

--- a/solution.py
+++ b/solution.py
@@ -37,20 +37,27 @@
     return shift(value, axis, 1), shift(value, axis, -1)
 
 
-def share_kernel(source, target, done):
+def share_kernel(source, target, held, done, sent):
     n_z, n_y, part, half = target.shape
     n_core = lax.axis_size("core")
     x, core, y = lax.axis_index("x"), lax.axis_index("core"), lax.axis_index("y")
     top = pl.multiple_of(x * part, part)
     copies = []
-    for j in range(n_y):
-        for i in range(n_z):
+    for i in range(n_z):
+        for j in range(n_y):
             block = (y + j) % n_y * n_z + i
             left = pl.multiple_of((block * n_core + core) * half, 128)
-            copy = pltpu.make_async_copy(source.at[pl.ds(top, part), pl.ds(left, half)], target.at[i, j], done.at[i, j])
+            copy = pltpu.make_async_copy(source.at[pl.ds(top, part), pl.ds(left, half)], held.at[i, j], done.at[i, j])
             copy.start()
             copies.append(copy)
-    for copy in copies:
+    out = []
+    for i in range(n_z):
+        for copy in copies[i * n_y : (i + 1) * n_y]:
+            copy.wait()
+        copy = pltpu.make_async_copy(held.at[i], target.at[i], sent.at[i])
+        copy.start()
+        out.append(copy)
+    for copy in out:
         copy.wait()
 
 
@@ -59,8 +66,12 @@
         share_kernel,
         out_shape=jax.ShapeDtypeStruct((n_z, n_y, part, half), out_grad.dtype),
         in_specs=[pl.BlockSpec(memory_space=pltpu.HBM)],
-        out_specs=pl.BlockSpec(memory_space=pltpu.VMEM),
-        scratch_shapes=[pltpu.SemaphoreType.DMA((n_z, n_y))],
+        out_specs=pl.BlockSpec(memory_space=pl.ANY),
+        scratch_shapes=[
+            pltpu.VMEM((n_z, n_y, part, half), out_grad.dtype),
+            pltpu.SemaphoreType.DMA((n_z, n_y)),
+            pltpu.SemaphoreType.DMA((n_z,)),
+        ],
         compiler_params=pltpu.CompilerParams(vmem_limit_bytes=56 * 1024 * 1024),
         cost_estimate=pl.CostEstimate(flops=0, bytes_accessed=4 * n_z * n_y * part * half, transcendentals=0),
     )(out_grad)

time: 110 us -> 109 us (level)
  no operation moved by 1% of the time
where the time goes in v6:
time: 109 us
  starting transfers between devices  53.7 us (49%)
  waiting for transfers between devices  46 us (42%)
  Pallas kernels  5.58 us (5%)
  other arithmetic  1.82 us (2%)
    ppermute x18, starting transfers between devices, shift(): return lax.ppermute(value, axis, [(i, (i + by) % n) for i in range(n)])  28.3 us
    ppermute x18, waiting for transfers between devices, shift(): return lax.ppermute(value, axis, [(i, (i + by) % n) for i in range(n)])  22.6 us
    all_to_all x1, waiting for transfers between devices, body(): total = lax.all_to_all(total, 'z', 0, 0, tiled=True)  12.2 us
    all_to_all x1, starting transfers between devices, body(): share = lax.all_to_all(share, 'z', 0, 0, tiled=True)  9.16 us
    ppermute x4, starting transfers between devices, pair_sum(): return value + lax.ppermute(value, axis, [(i, i ^ bit) for i in range(n)])  7.17 us
    ppermute x3, starting transfers between devices, swap(): lax.ppermute(value, axis, [(i, i ^ bits) for i in range(lax.axis_size(axi...  5.66 us
    ppermute x4, waiting for transfers between devices, pair_sum(): return value + lax.ppermute(value, axis, [(i, i ^ bit) for i in range(n)])  5.56 us
    all_to_all x1, waiting for transfers between devices, body(): share = lax.all_to_all(share, 'z', 0, 0, tiled=True)  4.16 us
  transfers between devices with their start and end apart: 27, of which 20 were waited for; matrix products, arithmetic and copies ran while one was open for 1% of the time, Pallas kernels for 2%

profile of v6, /device:TPU:1, one launch (start us, length us, event | category | flops | bytes accessed | tf_op | source)
XLA Modules:
  0.0 108.9 jit_solution(15857539861289987187)
XLA Ops:
  0.6 2.3 %shard_map.93 = bf16[8,4,16,1152]{3,2,1,0:T(8,128)(2,1)} custom-call(bf16[64,73728]{1,0:T(8,128)(2,1)} %source.1), custom_call_target="tpu_custom_call" | custom-call | bytes 2359296 | tf_op jit(solution)/shard_map/pallas_call | solution.py:65
  3.0 9.2 %all-to-all-start = ((bf16[8,4,16,1152]{3,2,1,0:T(8,128)(2,1)}), bf16[8,4,16,1152]{3,2,1,0:T(8,128)(2,1)S(1)}, u32[]{:S(2)}, u32[]{:S(2)}) async-start(bf16[8,4,16,1152]{3,2,1,0:T(8,128)(2,1)} %shard_map.93), calls=%async_computation | async-start | bytes 2359296 | tf_op jit(solution)/shard_map/all_to_all | solution.py:205
  14.3 2.5 %collective-permute-start.3 = (f32[18,128]{1,0:T(8,128)S(1)}, f32[18,128]{1,0:T(8,128)S(1)}, u32[]{:S(2)}, u32[]{:S(2)}) collective-permute-start(f32[18,128]{1,0:T(8,128)S(1)} %bitcast_add_fusion.1), channel_id=1, source_target_pairs={{0,192},{64,0},{128,64},{192,128},{1,193},{65,1},{129,65},{193,129... | collective-permute-start | bytes 27656 | tf_op jit(solution)/shard_map/ppermute | solution.py:19
  18.2 2.9 %collective-permute-done.2 = f32[18,128]{1,0:T(8,128)S(1)} collective-permute-done((f32[18,128]{1,0:T(8,128)S(1)}, f32[18,128]{1,0:T(8,128)S(1)}, u32[]{:S(2)}, u32[]{:S(2)}) %collective-permute-start.2) | collective-permute-done | bytes 9248 | tf_op jit(solution)/shard_map/ppermute | solution.py:19
  21.7 1.8 %collective-permute-start.4 = (f32[4,128]{1,0:T(4,128)S(1)}, f32[4,128]{1,0:T(4,128)S(1)}, u32[]{:S(2)}, u32[]{:S(2)}) collective-permute-start(f32[4,128]{1,0:T(4,128)S(1)} %pad_maximum_fusion.2), channel_id=1, source_target_pairs={{0,32},{32,0},{1,33},{33,1},{2,34},{34,2},{3,35},{35,3},{4,36},{36... | collective-permute-start | bytes 6152 | tf_op jit(solution)/shard_map/ppermute | solution.py:19
  25.7 2.0 %collective-permute-start.7 = (f32[4,2,128]{2,1,0:T(2,128)S(1)}, f32[4,2,128]{2,1,0:T(2,128)S(1)}, u32[]{:S(2)}, u32[]{:S(2)}) collective-permute-start(f32[4,2,128]{2,1,0:T(2,128)S(1)} %pad_maximum_fusion.1), channel_id=1, source_target_pairs={{0,192},{64,0},{128,64},{192,128},{1,193},{65,1},{129,65},{193,129... | collective-permute-start | bytes 12296 | tf_op jit(solution)/shard_map/ppermute | solution.py:19
  30.4 1.5 %collective-permute-done.8 = f32[24,128]{1,0:T(8,128)S(1)} collective-permute-done((f32[24,128]{1,0:T(8,128)S(1)}, f32[24,128]{1,0:T(8,128)S(1)}, u32[]{:S(2)}, u32[]{:S(2)}) %collective-permute-start.8) | collective-permute-done | bytes 12320 | tf_op jit(solution)/shard_map/ppermute | solution.py:24
  32.0 2.9 %collective-permute-start.9 = (f32[24,128]{1,0:T(8,128)S(1)}, f32[24,128]{1,0:T(8,128)S(1)}, u32[]{:S(2)}, u32[]{:S(2)}) collective-permute-start(f32[24,128]{1,0:T(8,128)S(1)} %fusion.3), channel_id=1, source_target_pairs={{0,16},{8,24},{16,0},{24,8},{1,17},{9,25},{17,1},{25,9},{2,18},{10... | collective-permute-start | bytes 36872 | tf_op jit(solution)/shard_map/ppermute | solution.py:24
  36.4 1.9 %collective-permute-start.10 = (f32[24,128]{1,0:T(8,128)S(1)}, f32[24,128]{1,0:T(8,128)S(1)}, u32[]{:S(2)}, u32[]{:S(2)}) collective-permute-start(f32[24,128]{1,0:T(8,128)S(1)} %add.61), channel_id=1, source_target_pairs={{0,1},{1,0},{2,3},{3,2},{4,5},{5,4},{6,7},{7,6},{8,9},{9,8},{10,11... | collective-permute-start | bytes 36872 | tf_op jit(solution)/shard_map/ppermute | solution.py:24
  38.2 1.8 %collective-permute-done.10 = f32[24,128]{1,0:T(8,128)S(1)} collective-permute-done((f32[24,128]{1,0:T(8,128)S(1)}, f32[24,128]{1,0:T(8,128)S(1)}, u32[]{:S(2)}, u32[]{:S(2)}) %collective-permute-start.10) | collective-permute-done | bytes 12320 | tf_op jit(solution)/shard_map/ppermute | solution.py:24
  40.0 4.2 %all-to-all-done.refs_5_.refs_7_ = bf16[8,4,16,1152]{3,2,1,0:T(8,128)(2,1)S(1)} async-done(((bf16[8,4,16,1152]{3,2,1,0:T(8,128)(2,1)}), bf16[8,4,16,1152]{3,2,1,0:T(8,128)(2,1)S(1)}, u32[]{:S(2)}, u32[]{:S(2)}) %all-to-all-start) | async-done | bytes 1179680 | tf_op jit(solution)/shard_map/all_to_all | solution.py:205
  45.4 1.5 %collective-permute-start.22 = (bf16[8,4,16,1152]{3,2,1,0:T(8,128)(2,1)S(1)}, bf16[8,4,16,1152]{3,2,1,0:T(8,128)(2,1)S(1)}, u32[]{:S(2)}, u32[]{:S(2)}) collective-permute-start(bf16[8,4,16,1152]{3,2,1,0:T(8,128)(2,1)S(1)} %all-to-all-done.refs_5_.refs_7_), channel_id=1, source_target_pairs={{0,192},{64,0},{128,64},{192,128},{1,193},{65,1},{129,65},{193,129... | collective-permute-start | bytes 3538952 | tf_op jit(solution)/shard_map/ppermute | solution.py:19
  48.5 4.1 %collective-permute-start.11 = (f32[24,128]{1,0:T(8,128)S(1)}, f32[24,128]{1,0:T(8,128)S(1)}, u32[]{:S(2)}, u32[]{:S(2)}) collective-permute-start(f32[24,128]{1,0:T(8,128)S(1)} %add.62), channel_id=1, source_target_pairs={{0,2},{1,3},{2,0},{3,1},{4,6},{5,7},{6,4},{7,5},{8,10},{9,11},{10,... | collective-permute-start | bytes 36872 | tf_op jit(solution)/shard_map/ppermute | solution.py:28
  55.2 4.5 %collective-permute-start.14 = (bf16[128,1152]{1,0:T(8,128)(2,1)S(1)}, bf16[128,1152]{1,0:T(8,128)(2,1)S(1)}, u32[]{:S(2)}, u32[]{:S(2)}) collective-permute-start(bf16[128,1152]{1,0:T(8,128)(2,1)S(1)} %get-tuple-element.20), channel_id=1, source_target_pairs={{0,32},{32,0},{1,33},{33,1},{2,34},{34,2},{3,35},{35,3},{4,36},{36... | collective-permute-start | bytes 884744 | tf_op jit(solution)/shard_map/ppermute | solution.py:19
  62.3 1.5 %collective-permute-start.16 = (bf16[128,1152]{1,0:T(8,128)(2,1)S(1)}, bf16[128,1152]{1,0:T(8,128)(2,1)S(1)}, u32[]{:S(2)}, u32[]{:S(2)}) collective-permute-start(bf16[128,1152]{1,0:T(8,128)(2,1)S(1)} %collective-permute-done.14.refs_1_), channel_id=1, source_target_pairs={{0,24},{8,0},{16,8},{24,16},{1,25},{9,1},{17,9},{25,17},{2,26},{10... | collective-permute-start | bytes 884744 | tf_op jit(solution)/shard_map/ppermute | solution.py:19
  65.2 7.1 %collective-permute-done.20.refs_7_.refs_9_ = bf16[8,4,16,1152]{3,2,1,0:T(8,128)(2,1)S(1)} collective-permute-done((bf16[8,4,16,1152]{3,2,1,0:T(8,128)(2,1)S(1)}, bf16[8,4,16,1152]{3,2,1,0:T(8,128)(2,1)S(1)}, u32[]{:S(2)}, u32[]{:S(2)}) %collective-permute-start.20) | collective-permute-done | bytes 1179680 | tf_op jit(solution)/shard_map/ppermute | solution.py:19
  72.5 2.7 %collective-permute-start.23 = (bf16[4,4,16,1152]{3,2,1,0:T(8,128)(2,1)S(1)}, bf16[4,4,16,1152]{3,2,1,0:T(8,128)(2,1)S(1)}, u32[]{:S(2)}, u32[]{:S(2)}) collective-permute-start(bf16[4,4,16,1152]{3,2,1,0:T(8,128)(2,1)S(1)} %slice.49), channel_id=1, source_target_pairs={{0,192},{64,0},{128,64},{192,128},{1,193},{65,1},{129,65},{193,129... | collective-permute-start | bytes 1769480 | tf_op jit(solution)/shard_map/ppermute | solution.py:19
  75.3 2.7 %collective-permute-start.19 = (bf16[128,1152]{1,0:T(8,128)(2,1)S(1)}, bf16[128,1152]{1,0:T(8,128)(2,1)S(1)}, u32[]{:S(2)}, u32[]{:S(2)}) collective-permute-start(bf16[128,1152]{1,0:T(8,128)(2,1)S(1)} %collective-permute-done.16.refs_3_), channel_id=1, source_target_pairs={{0,24},{8,0},{16,8},{24,16},{1,25},{9,1},{17,9},{25,17},{2,26},{10... | collective-permute-start | bytes 884744 | tf_op jit(solution)/shard_map/ppermute | solution.py:19
  79.1 3.2 %collective-permute-done.19.refs_6_ = bf16[128,1152]{1,0:T(8,128)(2,1)S(1)} collective-permute-done((bf16[128,1152]{1,0:T(8,128)(2,1)S(1)}, bf16[128,1152]{1,0:T(8,128)(2,1)S(1)}, u32[]{:S(2)}, u32[]{:S(2)}) %collective-permute-start.19) | collective-permute-done | bytes 294944 | tf_op jit(solution)/shard_map/ppermute | solution.py:19
  82.3 3.2 %collective-permute-done.18.refs_5_ = bf16[128,1152]{1,0:T(8,128)(2,1)S(1)} collective-permute-done((bf16[128,1152]{1,0:T(8,128)(2,1)S(1)}, bf16[128,1152]{1,0:T(8,128)(2,1)S(1)}, u32[]{:S(2)}, u32[]{:S(2)}) %collective-permute-start.18) | collective-permute-done | bytes 294944 | tf_op jit(solution)/shard_map/ppermute | solution.py:19
  85.5 1.5 %collective-permute-done.21.refs_10_ = bf16[4,4,16,1152]{3,2,1,0:T(8,128)(2,1)S(1)} collective-permute-done((bf16[4,4,16,1152]{3,2,1,0:T(8,128)(2,1)S(1)}, bf16[4,4,16,1152]{3,2,1,0:T(8,128)(2,1)S(1)}, u32[]{:S(2)}, u32[]{:S(2)}) %collective-permute-start.21) | collective-permute-done | bytes 589856 | tf_op jit(solution)/shard_map/ppermute | solution.py:19
  88.2 2.5 %collective-permute-start.24 = (f32[8,4,16,128]{3,2,1,0:T(8,128)S(1)}, f32[8,4,16,128]{3,2,1,0:T(8,128)S(1)}, u32[]{:S(2)}, u32[]{:S(2)}) collective-permute-start(f32[8,4,16,128]{3,2,1,0:T(8,128)S(1)} %get-tuple-element.27), channel_id=1, source_target_pairs={{0,32},{32,0},{1,33},{33,1},{2,34},{34,2},{3,35},{35,3},{4,36},{36... | collective-permute-start | bytes 786440 | tf_op jit(solution)/shard_map/ppermute | solution.py:19
  92.5 3.4 %all-to-all-start.1 = ((f32[8,4,16,128]{3,2,1,0:T(8,128)}), f32[8,4,16,128]{3,2,1,0:T(8,128)S(1)}, u32[]{:S(2)}, u32[]{:S(2)}) async-start(f32[8,4,16,128]{3,2,1,0:T(8,128)} %add.66), calls=%async_computation.1 | async-start | bytes 524288 | tf_op jit(solution)/shard_map/all_to_all | solution.py:244
  95.9 12.2 %all-to-all-done.1 = f32[8,4,16,128]{3,2,1,0:T(8,128)S(1)} async-done(((f32[8,4,16,128]{3,2,1,0:T(8,128)}), f32[8,4,16,128]{3,2,1,0:T(8,128)S(1)}, u32[]{:S(2)}, u32[]{:S(2)}) %all-to-all-start.1) | async-done | bytes 262176 | tf_op jit(solution)/shard_map/all_to_all | solution.py:244
  (76 shorter events, 24.8 us)
Async XLA Ops:
  3.0 41.2 %all-to-all-start = ((bf16[8,4,16,1152]{3,2,1,0:T(8,128)(2,1)}), bf16[8,4,16,1152]{3,2,1,0:T(8,128)(2,1)S(1)}, u32[]{:S(2)}, u32[]{:S(2)}) async-start(bf16[8,4,16,1152]{3,2,1,0:T(8,128)(2,1)} %shard_map.93), calls=%async_computation | async-start | bytes 2359296 | tf_op jit(solution)/shard_map/all_to_all | solution.py:205
  14.3 3.9 %collective-permute-start.3 = (f32[18,128]{1,0:T(8,128)S(1)}, f32[18,128]{1,0:T(8,128)S(1)}, u32[]{:S(2)}, u32[]{:S(2)}) collective-permute-start(f32[18,128]{1,0:T(8,128)S(1)} %bitcast_add_fusion.1), channel_id=1, source_target_pairs={{0,192},{64,0},{128,64},{192,128},{1,193},{65,1},{129,65},{193,129... | collective-permute-start | bytes 27656 | tf_op jit(solution)/shard_map/ppermute | solution.py:19
  16.8 4.3 %collective-permute-start.2 = (f32[18,128]{1,0:T(8,128)S(1)}, f32[18,128]{1,0:T(8,128)S(1)}, u32[]{:S(2)}, u32[]{:S(2)}) collective-permute-start(f32[18,128]{1,0:T(8,128)S(1)} %bitcast_add_fusion.1), channel_id=1, source_target_pairs={{0,128},{64,192},{128,0},{192,64},{1,129},{65,193},{129,1},{193,65... | collective-permute-start | bytes 27656 | tf_op jit(solution)/shard_map/ppermute | solution.py:19
  17.3 4.1 %collective-permute-start.1 = (f32[18,128]{1,0:T(8,128)S(1)}, f32[18,128]{1,0:T(8,128)S(1)}, u32[]{:S(2)}, u32[]{:S(2)}) collective-permute-start(f32[18,128]{1,0:T(8,128)S(1)} %bitcast_add_fusion.1), channel_id=1, source_target_pairs={{0,64},{64,128},{128,192},{192,0},{1,65},{65,129},{129,193},{193,1... | collective-permute-start | bytes 27656 | tf_op jit(solution)/shard_map/ppermute | solution.py:19
  24.3 4.0 %collective-permute-start.5 = (f32[4,2,128]{2,1,0:T(2,128)S(1)}, f32[4,2,128]{2,1,0:T(2,128)S(1)}, u32[]{:S(2)}, u32[]{:S(2)}) collective-permute-start(f32[4,2,128]{2,1,0:T(2,128)S(1)} %pad_maximum_fusion.1), channel_id=1, source_target_pairs={{0,64},{64,128},{128,192},{192,0},{1,65},{65,129},{129,193},{193,1... | collective-permute-start | bytes 12296 | tf_op jit(solution)/shard_map/ppermute | solution.py:19
  24.4 4.2 %collective-permute-start.6 = (f32[4,2,128]{2,1,0:T(2,128)S(1)}, f32[4,2,128]{2,1,0:T(2,128)S(1)}, u32[]{:S(2)}, u32[]{:S(2)}) collective-permute-start(f32[4,2,128]{2,1,0:T(2,128)S(1)} %pad_maximum_fusion.1), channel_id=1, source_target_pairs={{0,128},{64,192},{128,0},{192,64},{1,129},{65,193},{129,1},{193,65... | collective-permute-start | bytes 12296 | tf_op jit(solution)/shard_map/ppermute | solution.py:19
  25.7 3.2 %collective-permute-start.7 = (f32[4,2,128]{2,1,0:T(2,128)S(1)}, f32[4,2,128]{2,1,0:T(2,128)S(1)}, u32[]{:S(2)}, u32[]{:S(2)}) collective-permute-start(f32[4,2,128]{2,1,0:T(2,128)S(1)} %pad_maximum_fusion.1), channel_id=1, source_target_pairs={{0,192},{64,0},{128,64},{192,128},{1,193},{65,1},{129,65},{193,129... | collective-permute-start | bytes 12296 | tf_op jit(solution)/shard_map/ppermute | solution.py:19
  32.0 4.3 %collective-permute-start.9 = (f32[24,128]{1,0:T(8,128)S(1)}, f32[24,128]{1,0:T(8,128)S(1)}, u32[]{:S(2)}, u32[]{:S(2)}) collective-permute-start(f32[24,128]{1,0:T(8,128)S(1)} %fusion.3), channel_id=1, source_target_pairs={{0,16},{8,24},{16,0},{24,8},{1,17},{9,25},{17,1},{25,9},{2,18},{10... | collective-permute-start | bytes 36872 | tf_op jit(solution)/shard_map/ppermute | solution.py:24
  36.4 3.7 %collective-permute-start.10 = (f32[24,128]{1,0:T(8,128)S(1)}, f32[24,128]{1,0:T(8,128)S(1)}, u32[]{:S(2)}, u32[]{:S(2)}) collective-permute-start(f32[24,128]{1,0:T(8,128)S(1)} %add.61), channel_id=1, source_target_pairs={{0,1},{1,0},{2,3},{3,2},{4,5},{5,4},{6,7},{7,6},{8,9},{9,8},{10,11... | collective-permute-start | bytes 36872 | tf_op jit(solution)/shard_map/ppermute | solution.py:24
  44.2 28.1 %collective-permute-start.20 = (bf16[8,4,16,1152]{3,2,1,0:T(8,128)(2,1)S(1)}, bf16[8,4,16,1152]{3,2,1,0:T(8,128)(2,1)S(1)}, u32[]{:S(2)}, u32[]{:S(2)}) collective-permute-start(bf16[8,4,16,1152]{3,2,1,0:T(8,128)(2,1)S(1)} %all-to-all-done.refs_5_.refs_7_), channel_id=1, source_target_pairs={{0,64},{64,128},{128,192},{192,0},{1,65},{65,129},{129,193},{193,1... | collective-permute-start | bytes 3538952 | tf_op jit(solution)/shard_map/ppermute | solution.py:19
  45.4 27.1 %collective-permute-start.22 = (bf16[8,4,16,1152]{3,2,1,0:T(8,128)(2,1)S(1)}, bf16[8,4,16,1152]{3,2,1,0:T(8,128)(2,1)S(1)}, u32[]{:S(2)}, u32[]{:S(2)}) collective-permute-start(bf16[8,4,16,1152]{3,2,1,0:T(8,128)(2,1)S(1)} %all-to-all-done.refs_5_.refs_7_), channel_id=1, source_target_pairs={{0,192},{64,0},{128,64},{192,128},{1,193},{65,1},{129,65},{193,129... | collective-permute-start | bytes 3538952 | tf_op jit(solution)/shard_map/ppermute | solution.py:19
  46.9 6.5 %collective-permute-start.12 = (f32[24,128]{1,0:T(8,128)S(1)}, f32[24,128]{1,0:T(8,128)S(1)}, u32[]{:S(2)}, u32[]{:S(2)}) collective-permute-start(f32[24,128]{1,0:T(8,128)S(1)} %add.62), channel_id=1, source_target_pairs={{0,4},{1,5},{2,6},{3,7},{4,0},{5,1},{6,2},{7,3},{8,12},{9,13},{10,... | collective-permute-start | bytes 36872 | tf_op jit(solution)/shard_map/ppermute | solution.py:28
  47.5 5.8 %collective-permute-start.13 = (f32[24,128]{1,0:T(8,128)S(1)}, f32[24,128]{1,0:T(8,128)S(1)}, u32[]{:S(2)}, u32[]{:S(2)}) collective-permute-start(f32[24,128]{1,0:T(8,128)S(1)} %add.62), channel_id=1, source_target_pairs={{0,6},{1,7},{2,4},{3,5},{4,2},{5,3},{6,0},{7,1},{8,14},{9,15},{10,... | collective-permute-start | bytes 36872 | tf_op jit(solution)/shard_map/ppermute | solution.py:28
  48.5 5.4 %collective-permute-start.11 = (f32[24,128]{1,0:T(8,128)S(1)}, f32[24,128]{1,0:T(8,128)S(1)}, u32[]{:S(2)}, u32[]{:S(2)}) collective-permute-start(f32[24,128]{1,0:T(8,128)S(1)} %add.62), channel_id=1, source_target_pairs={{0,2},{1,3},{2,0},{3,1},{4,6},{5,7},{6,4},{7,5},{8,10},{9,11},{10,... | collective-permute-start | bytes 36872 | tf_op jit(solution)/shard_map/ppermute | solution.py:28
  55.2 5.7 %collective-permute-start.14 = (bf16[128,1152]{1,0:T(8,128)(2,1)S(1)}, bf16[128,1152]{1,0:T(8,128)(2,1)S(1)}, u32[]{:S(2)}, u32[]{:S(2)}) collective-permute-start(bf16[128,1152]{1,0:T(8,128)(2,1)S(1)} %get-tuple-element.20), channel_id=1, source_target_pairs={{0,32},{32,0},{1,33},{33,1},{2,34},{34,2},{3,35},{35,3},{4,36},{36... | collective-permute-start | bytes 884744 | tf_op jit(solution)/shard_map/ppermute | solution.py:19
  60.9 17.1 %collective-permute-start.17 = (bf16[256,1152]{1,0:T(8,128)(2,1)S(1)}, bf16[256,1152]{1,0:T(8,128)(2,1)S(1)}, u32[]{:S(2)}, u32[]{:S(2)}) collective-permute-start(bf16[256,1152]{1,0:T(8,128)(2,1)S(1)} %pad_maximum_fusion), channel_id=1, source_target_pairs={{0,8},{8,16},{16,24},{24,0},{1,9},{9,17},{17,25},{25,1},{2,10},{10... | collective-permute-start | bytes 1769480 | tf_op jit(solution)/shard_map/ppermute | solution.py:19
  62.3 13.0 %collective-permute-start.16 = (bf16[128,1152]{1,0:T(8,128)(2,1)S(1)}, bf16[128,1152]{1,0:T(8,128)(2,1)S(1)}, u32[]{:S(2)}, u32[]{:S(2)}) collective-permute-start(bf16[128,1152]{1,0:T(8,128)(2,1)S(1)} %collective-permute-done.14.refs_1_), channel_id=1, source_target_pairs={{0,24},{8,0},{16,8},{24,16},{1,25},{9,1},{17,9},{25,17},{2,26},{10... | collective-permute-start | bytes 884744 | tf_op jit(solution)/shard_map/ppermute | solution.py:19
  63.8 14.3 %collective-permute-start.15 = (bf16[128,1152]{1,0:T(8,128)(2,1)S(1)}, bf16[128,1152]{1,0:T(8,128)(2,1)S(1)}, u32[]{:S(2)}, u32[]{:S(2)}) collective-permute-start(bf16[128,1152]{1,0:T(8,128)(2,1)S(1)} %get-tuple-element.19.refs_0_), channel_id=1, source_target_pairs={{0,24},{8,0},{16,8},{24,16},{1,25},{9,1},{17,9},{25,17},{2,26},{10... | collective-permute-start | bytes 884744 | tf_op jit(solution)/shard_map/ppermute | solution.py:19
  72.4 14.7 %collective-permute-start.21 = (bf16[4,4,16,1152]{3,2,1,0:T(8,128)(2,1)S(1)}, bf16[4,4,16,1152]{3,2,1,0:T(8,128)(2,1)S(1)}, u32[]{:S(2)}, u32[]{:S(2)}) collective-permute-start(bf16[4,4,16,1152]{3,2,1,0:T(8,128)(2,1)S(1)} %slice.48), channel_id=1, source_target_pairs={{0,64},{64,128},{128,192},{192,0},{1,65},{65,129},{129,193},{193,1... | collective-permute-start | bytes 1769480 | tf_op jit(solution)/shard_map/ppermute | solution.py:19
  72.5 14.5 %collective-permute-start.23 = (bf16[4,4,16,1152]{3,2,1,0:T(8,128)(2,1)S(1)}, bf16[4,4,16,1152]{3,2,1,0:T(8,128)(2,1)S(1)}, u32[]{:S(2)}, u32[]{:S(2)}) collective-permute-start(bf16[4,4,16,1152]{3,2,1,0:T(8,128)(2,1)S(1)} %slice.49), channel_id=1, source_target_pairs={{0,192},{64,0},{128,64},{192,128},{1,193},{65,1},{129,65},{193,129... | collective-permute-start | bytes 1769480 | tf_op jit(solution)/shard_map/ppermute | solution.py:19
  75.3 7.0 %collective-permute-start.19 = (bf16[128,1152]{1,0:T(8,128)(2,1)S(1)}, bf16[128,1152]{1,0:T(8,128)(2,1)S(1)}, u32[]{:S(2)}, u32[]{:S(2)}) collective-permute-start(bf16[128,1152]{1,0:T(8,128)(2,1)S(1)} %collective-permute-done.16.refs_3_), channel_id=1, source_target_pairs={{0,24},{8,0},{16,8},{24,16},{1,25},{9,1},{17,9},{25,17},{2,26},{10... | collective-permute-start | bytes 884744 | tf_op jit(solution)/shard_map/ppermute | solution.py:19
  78.0 7.5 %collective-permute-start.18 = (bf16[128,1152]{1,0:T(8,128)(2,1)S(1)}, bf16[128,1152]{1,0:T(8,128)(2,1)S(1)}, u32[]{:S(2)}, u32[]{:S(2)}) collective-permute-start(bf16[128,1152]{1,0:T(8,128)(2,1)S(1)} %slice.47), channel_id=1, source_target_pairs={{0,8},{8,16},{16,24},{24,0},{1,9},{9,17},{17,25},{25,1},{2,10},{10... | collective-permute-start | bytes 884744 | tf_op jit(solution)/shard_map/ppermute | solution.py:19
  88.2 3.6 %collective-permute-start.24 = (f32[8,4,16,128]{3,2,1,0:T(8,128)S(1)}, f32[8,4,16,128]{3,2,1,0:T(8,128)S(1)}, u32[]{:S(2)}, u32[]{:S(2)}) collective-permute-start(f32[8,4,16,128]{3,2,1,0:T(8,128)S(1)} %get-tuple-element.27), channel_id=1, source_target_pairs={{0,32},{32,0},{1,33},{33,1},{2,34},{34,2},{3,35},{35,3},{4,36},{36... | collective-permute-start | bytes 786440 | tf_op jit(solution)/shard_map/ppermute | solution.py:19
  92.5 15.7 %all-to-all-start.1 = ((f32[8,4,16,128]{3,2,1,0:T(8,128)}), f32[8,4,16,128]{3,2,1,0:T(8,128)S(1)}, u32[]{:S(2)}, u32[]{:S(2)}) async-start(f32[8,4,16,128]{3,2,1,0:T(8,128)} %add.66), calls=%async_computation.1 | async-start | bytes 524288 | tf_op jit(solution)/shard_map/all_to_all | solution.py:244
  (9 other events, 99.0 us)

commit v7 on v6

--- a/solution.py
+++ b/solution.py
@@ -110,6 +110,7 @@
         in_specs=[vmem] * 6,
         out_specs=(vmem,) * 4,
         compiler_params=pltpu.CompilerParams(vmem_limit_bytes=16 * 1024 * 1024),
+        cost_estimate=pl.CostEstimate(flops=rows * cols, bytes_accessed=rows * cols, transcendentals=0),
     )(sums, state, col_out, *arrays)
 
 
@@ -142,17 +143,24 @@
     total_ref[...] = total
 
 
-def all_kernel(sizes, places, far, *refs):
+def far_kernel(sizes, places, far, *refs):
     (*weights, far_weight), refs = split_weights((*sizes, 2), refs)
-    tokens, far_tokens, partial, (mine, other) = refs[:-5], refs[-5:-3], refs[-3], refs[-2:]
+    tokens, (mine, other) = refs[:2], refs[2:]
+    n_z, part, rows = mine.shape
+    total = times(tokens_of(tokens, far), far_weight)
+    for weight, j in zip(weights, places):
+        total += times(tokens_of(tokens, j), weight)
+    total = total.reshape(n_z, part, 2 * rows)
+    mine[...], other[...] = total[:, :, :rows], total[:, :, rows:]
+
+
+def rest_kernel(far, *refs):
+    weight, tokens, partial, (mine, other) = joined(refs[:2]), refs[2:-3], refs[-3], refs[-2:]
     n_z, _, part, rows = mine.shape
-    near_total = partial[...] + times(tokens_of(tokens, far), far_weight)
-    far_total = times(tokens_of(far_tokens, far), far_weight)
-    for weight, j in zip(weights, places):
-        far_total += times(tokens_of(far_tokens, j), weight)
-    for place, total in enumerate([*near_total.reshape(-1, n_z, part, 2 * rows), far_total.reshape(n_z, part, 2 * rows)]):
-        mine[:, place] = total[:, :, :rows]
-        other[:, place] = total[:, :, rows:]
+    total = (partial[...] + times(tokens_of(tokens, far), weight)).reshape(-1, n_z, part, 2 * rows)
+    for place in range(total.shape[0]):
+        mine[:, place] = total[place, :, :, :rows]
+        other[:, place] = total[place, :, :, rows:]
 
 
 def near_products(weights, tokens, places):
@@ -174,21 +182,16 @@
     )(*operands)
 
 
-def all_products(weights, far_weights, tokens, far_tokens, partial, places):
-    operands = [w for pair in weights for w in pair] + [*far_weights, *tokens, *far_tokens, partial]
-    n_z, n_y, part, half = tokens[0].shape
-    rows = far_weights[0].shape[0]
-    out = jax.ShapeDtypeStruct((n_z, len(tokens) + 1, part, rows), jnp.float32)
-    return pl.pallas_call(
-        functools.partial(all_kernel, tuple(map(len, weights)), places, 2),
+def pair_call(kernel, shape, flops, operands):
+    out = jax.ShapeDtypeStruct(shape, jnp.float32)
+    return pl.pallas_call(
+        kernel,
         out_shape=(out, out),
         in_specs=[pl.BlockSpec(memory_space=pltpu.VMEM)] * len(operands),
         out_specs=(pl.BlockSpec(memory_space=pltpu.VMEM),) * 2,
         compiler_params=pltpu.CompilerParams(vmem_limit_bytes=40 * 1024 * 1024),
         cost_estimate=pl.CostEstimate(
-            flops=4 * (len(tokens) + n_y) * n_z * part * rows * half,
-            bytes_accessed=2 * sum(o.size for o in operands),
-            transcendentals=0,
+            flops=flops, bytes_accessed=2 * sum(o.size for o in operands), transcendentals=0
         ),
     )(*operands)
 
@@ -229,18 +232,29 @@
         all_rows * all_cols, all_cols, sums, parts[3], col_out[None], (grad, weight, residual), half
     )
     taken = shift(given, "core", 1)
-    w_before = shift(jnp.concatenate([kept, taken]), "y", 1)
-    taken_after, kept_after = shift(taken, "y", -1), shift(kept, "y", -1)
+    w_before, w_after = gather4(jnp.concatenate([kept, taken]), "y")
     far_low = shift(before[: n_z // 2], "x", 1)
     far_high = shift(after[n_z // 2 :], "x", -1)
     kept_far = shift(w_before[:rows], "y", 1)
-    taken_far = shift(taken_after, "y", -1)
+    taken_far = shift(w_after[rows:], "y", -1)
     kept_far, taken_far, far_low, far_high = lax.optimization_barrier((kept_far, taken_far, far_low, far_high))
-    near_weights = ((kept, taken), (kept_after, taken_after), (w_before,))
+    near_weights = ((kept, taken), (w_after,), (w_before,))
     near_tokens = (share, after, before)
     partial = near_products(near_weights, near_tokens, (0, 1, 3))
-    mine, other = all_products(near_weights, (kept_far, taken_far), near_tokens, (far_low, far_high), partial, (0, 1, 3))
-    total = mine + shift(other, "core", 1)
+    shape = (n_z, 3, part, rows)
+    work = 4 * n_z * part * rows * half
+    rest = pair_call(functools.partial(rest_kernel, 2), shape, 3 * work, [kept_far, taken_far, *near_tokens, partial])
+    sizes = tuple(map(len, near_weights))
+    flat = [w for group in near_weights for w in group]
+    last = pair_call(
+        functools.partial(far_kernel, sizes, (0, 1, 3), 2),
+        (n_z, part, rows),
+        n_y * work,
+        [*flat, kept_far, taken_far, far_low, far_high],
+    )
+    rest = rest[0] + shift(rest[1], "core", 1)
+    last = last[0] + shift(last[1], "core", 1)
+    total = jnp.concatenate([rest, last[:, None]], axis=1)
     total = lax.all_to_all(total, "z", 0, 0, tiled=True)
     summed = jnp.sum(total, axis=0)
     summed = jnp.stack([summed[0], summed[1], summed[3], summed[2]])

time: 109 us -> 111 us (1.018)
  waiting for transfers between devices: 46 us -> 48.5 us
  starting transfers between devices: 53.7 us -> 52.4 us
    ppermute x18, waiting for transfers between devices: 22.6 us -> 25.2 us  [shift(): return lax.ppermute(value, axis, [(i, (i + by) % n) for i in range(n)])]
    ppermute x18, starting transfers between devices: 28.3 us -> 27.1 us  [shift(): return lax.ppermute(value, axis, [(i, (i + by) % n) for i in range(n)])]
where the time goes in v7:
time: 111 us; the launch traced here: 110 us
  starting transfers between devices  52.4 us (47%)
  waiting for transfers between devices  48.5 us (44%)
  Pallas kernels  5.76 us (5%)
  other arithmetic  1.79 us (2%)
    ppermute x18, starting transfers between devices, shift(): return lax.ppermute(value, axis, [(i, (i + by) % n) for i in range(n)])  27.1 us
    ppermute x18, waiting for transfers between devices, shift(): return lax.ppermute(value, axis, [(i, (i + by) % n) for i in range(n)])  25.2 us
    all_to_all x1, waiting for transfers between devices, body(): total = lax.all_to_all(total, 'z', 0, 0, tiled=True)  12.3 us
    all_to_all x1, starting transfers between devices, body(): share = lax.all_to_all(share, 'z', 0, 0, tiled=True)  9.16 us
    ppermute x4, starting transfers between devices, pair_sum(): return value + lax.ppermute(value, axis, [(i, i ^ bit) for i in range(n)])  7.17 us
    ppermute x3, starting transfers between devices, swap(): lax.ppermute(value, axis, [(i, i ^ bits) for i in range(lax.axis_size(axi...  5.66 us
    ppermute x4, waiting for transfers between devices, pair_sum(): return value + lax.ppermute(value, axis, [(i, i ^ bit) for i in range(n)])  5.56 us
    all_to_all x1, waiting for transfers between devices, body(): share = lax.all_to_all(share, 'z', 0, 0, tiled=True)  4.16 us
  transfers between devices with their start and end apart: 27, of which 20 were waited for; matrix products, arithmetic and copies ran while one was open for 1% of the time, Pallas kernels for 2%

profile of v7, /device:TPU:1, one launch (start us, length us, event | category | flops | bytes accessed | tf_op | source)
XLA Modules:
  0.0 110.4 jit_solution(6663147175252971973)
XLA Ops:
  0.6 2.3 %shard_map.93 = bf16[8,4,16,1152]{3,2,1,0:T(8,128)(2,1)} custom-call(bf16[64,73728]{1,0:T(8,128)(2,1)} %source.1), custom_call_target="tpu_custom_call" | custom-call | bytes 2359296 | tf_op jit(solution)/shard_map/pallas_call | solution.py:65
  3.0 9.2 %all-to-all-start = ((bf16[8,4,16,1152]{3,2,1,0:T(8,128)(2,1)}), bf16[8,4,16,1152]{3,2,1,0:T(8,128)(2,1)S(1)}, u32[]{:S(2)}, u32[]{:S(2)}) async-start(bf16[8,4,16,1152]{3,2,1,0:T(8,128)(2,1)} %shard_map.93), calls=%async_computation | async-start | bytes 2359296 | tf_op jit(solution)/shard_map/all_to_all | solution.py:208
  14.3 2.5 %collective-permute-start.3 = (f32[18,128]{1,0:T(8,128)S(1)}, f32[18,128]{1,0:T(8,128)S(1)}, u32[]{:S(2)}, u32[]{:S(2)}) collective-permute-start(f32[18,128]{1,0:T(8,128)S(1)} %bitcast_add_fusion.1), channel_id=1, source_target_pairs={{0,192},{64,0},{128,64},{192,128},{1,193},{65,1},{129,65},{193,129... | collective-permute-start | bytes 27656 | tf_op jit(solution)/shard_map/ppermute | solution.py:19
  18.2 2.9 %collective-permute-done.2 = f32[18,128]{1,0:T(8,128)S(1)} collective-permute-done((f32[18,128]{1,0:T(8,128)S(1)}, f32[18,128]{1,0:T(8,128)S(1)}, u32[]{:S(2)}, u32[]{:S(2)}) %collective-permute-start.2) | collective-permute-done | bytes 9248 | tf_op jit(solution)/shard_map/ppermute | solution.py:19
  21.7 1.8 %collective-permute-start.4 = (f32[4,128]{1,0:T(4,128)S(1)}, f32[4,128]{1,0:T(4,128)S(1)}, u32[]{:S(2)}, u32[]{:S(2)}) collective-permute-start(f32[4,128]{1,0:T(4,128)S(1)} %pad_maximum_fusion.2), channel_id=1, source_target_pairs={{0,32},{32,0},{1,33},{33,1},{2,34},{34,2},{3,35},{35,3},{4,36},{36... | collective-permute-start | bytes 6152 | tf_op jit(solution)/shard_map/ppermute | solution.py:19
  25.7 2.0 %collective-permute-start.7 = (f32[4,2,128]{2,1,0:T(2,128)S(1)}, f32[4,2,128]{2,1,0:T(2,128)S(1)}, u32[]{:S(2)}, u32[]{:S(2)}) collective-permute-start(f32[4,2,128]{2,1,0:T(2,128)S(1)} %pad_maximum_fusion.1), channel_id=1, source_target_pairs={{0,192},{64,0},{128,64},{192,128},{1,193},{65,1},{129,65},{193,129... | collective-permute-start | bytes 12296 | tf_op jit(solution)/shard_map/ppermute | solution.py:19
  30.4 1.5 %collective-permute-done.8 = f32[24,128]{1,0:T(8,128)S(1)} collective-permute-done((f32[24,128]{1,0:T(8,128)S(1)}, f32[24,128]{1,0:T(8,128)S(1)}, u32[]{:S(2)}, u32[]{:S(2)}) %collective-permute-start.8) | collective-permute-done | bytes 12320 | tf_op jit(solution)/shard_map/ppermute | solution.py:24
  32.0 2.9 %collective-permute-start.9 = (f32[24,128]{1,0:T(8,128)S(1)}, f32[24,128]{1,0:T(8,128)S(1)}, u32[]{:S(2)}, u32[]{:S(2)}) collective-permute-start(f32[24,128]{1,0:T(8,128)S(1)} %fusion.3), channel_id=1, source_target_pairs={{0,16},{8,24},{16,0},{24,8},{1,17},{9,25},{17,1},{25,9},{2,18},{10... | collective-permute-start | bytes 36872 | tf_op jit(solution)/shard_map/ppermute | solution.py:24
  36.4 1.9 %collective-permute-start.10 = (f32[24,128]{1,0:T(8,128)S(1)}, f32[24,128]{1,0:T(8,128)S(1)}, u32[]{:S(2)}, u32[]{:S(2)}) collective-permute-start(f32[24,128]{1,0:T(8,128)S(1)} %add.64), channel_id=1, source_target_pairs={{0,1},{1,0},{2,3},{3,2},{4,5},{5,4},{6,7},{7,6},{8,9},{9,8},{10,11... | collective-permute-start | bytes 36872 | tf_op jit(solution)/shard_map/ppermute | solution.py:24
  38.2 1.8 %collective-permute-done.10 = f32[24,128]{1,0:T(8,128)S(1)} collective-permute-done((f32[24,128]{1,0:T(8,128)S(1)}, f32[24,128]{1,0:T(8,128)S(1)}, u32[]{:S(2)}, u32[]{:S(2)}) %collective-permute-start.10) | collective-permute-done | bytes 12320 | tf_op jit(solution)/shard_map/ppermute | solution.py:24
  40.0 4.2 %all-to-all-done.refs_4_.refs_2_ = bf16[8,4,16,1152]{3,2,1,0:T(8,128)(2,1)S(1)} async-done(((bf16[8,4,16,1152]{3,2,1,0:T(8,128)(2,1)}), bf16[8,4,16,1152]{3,2,1,0:T(8,128)(2,1)S(1)}, u32[]{:S(2)}, u32[]{:S(2)}) %all-to-all-start) | async-done | bytes 1179680 | tf_op jit(solution)/shard_map/all_to_all | solution.py:208
  45.4 1.5 %collective-permute-start.21 = (bf16[8,4,16,1152]{3,2,1,0:T(8,128)(2,1)S(1)}, bf16[8,4,16,1152]{3,2,1,0:T(8,128)(2,1)S(1)}, u32[]{:S(2)}, u32[]{:S(2)}) collective-permute-start(bf16[8,4,16,1152]{3,2,1,0:T(8,128)(2,1)S(1)} %all-to-all-done.refs_4_.refs_2_), channel_id=1, source_target_pairs={{0,192},{64,0},{128,64},{192,128},{1,193},{65,1},{129,65},{193,129... | collective-permute-start | bytes 3538952 | tf_op jit(solution)/shard_map/ppermute | solution.py:19
  48.5 4.1 %collective-permute-start.11 = (f32[24,128]{1,0:T(8,128)S(1)}, f32[24,128]{1,0:T(8,128)S(1)}, u32[]{:S(2)}, u32[]{:S(2)}) collective-permute-start(f32[24,128]{1,0:T(8,128)S(1)} %add.65), channel_id=1, source_target_pairs={{0,2},{1,3},{2,0},{3,1},{4,6},{5,7},{6,4},{7,5},{8,10},{9,11},{10,... | collective-permute-start | bytes 36872 | tf_op jit(solution)/shard_map/ppermute | solution.py:28
  55.2 4.5 %collective-permute-start.14 = (bf16[128,1152]{1,0:T(8,128)(2,1)S(1)}, bf16[128,1152]{1,0:T(8,128)(2,1)S(1)}, u32[]{:S(2)}, u32[]{:S(2)}) collective-permute-start(bf16[128,1152]{1,0:T(8,128)(2,1)S(1)} %get-tuple-element.22), channel_id=1, source_target_pairs={{0,32},{32,0},{1,33},{33,1},{2,34},{34,2},{3,35},{35,3},{4,36},{36... | collective-permute-start | bytes 884744 | tf_op jit(solution)/shard_map/ppermute | solution.py:19
  62.3 1.5 %collective-permute-start.17 = (bf16[256,1152]{1,0:T(8,128)(2,1)S(1)}, bf16[256,1152]{1,0:T(8,128)(2,1)S(1)}, u32[]{:S(2)}, u32[]{:S(2)}) collective-permute-start(bf16[256,1152]{1,0:T(8,128)(2,1)S(1)} %constant_dynamic-update-slice_fusion), channel_id=1, source_target_pairs={{0,24},{8,0},{16,8},{24,16},{1,25},{9,1},{17,9},{25,17},{2,26},{10... | collective-permute-start | bytes 1769480 | tf_op jit(solution)/shard_map/ppermute | solution.py:19
  63.8 8.5 %collective-permute-done.19.refs_6_.refs_4_ = bf16[8,4,16,1152]{3,2,1,0:T(8,128)(2,1)S(1)} collective-permute-done((bf16[8,4,16,1152]{3,2,1,0:T(8,128)(2,1)S(1)}, bf16[8,4,16,1152]{3,2,1,0:T(8,128)(2,1)S(1)}, u32[]{:S(2)}, u32[]{:S(2)}) %collective-permute-start.19) | collective-permute-done | bytes 1179680 | tf_op jit(solution)/shard_map/ppermute | solution.py:19
  72.6 2.7 %collective-permute-start.22 = (bf16[4,4,16,1152]{3,2,1,0:T(8,128)(2,1)S(1)}, bf16[4,4,16,1152]{3,2,1,0:T(8,128)(2,1)S(1)}, u32[]{:S(2)}, u32[]{:S(2)}) collective-permute-start(bf16[4,4,16,1152]{3,2,1,0:T(8,128)(2,1)S(1)} %slice.54), channel_id=1, source_target_pairs={{0,192},{64,0},{128,64},{192,128},{1,193},{65,1},{129,65},{193,129... | collective-permute-start | bytes 1769480 | tf_op jit(solution)/shard_map/ppermute | solution.py:19
  75.3 1.6 %collective-permute-done.15.refs_3_ = bf16[256,1152]{1,0:T(8,128)(2,1)S(1)} collective-permute-done((bf16[256,1152]{1,0:T(8,128)(2,1)S(1)}, bf16[256,1152]{1,0:T(8,128)(2,1)S(1)}, u32[]{:S(2)}, u32[]{:S(2)}) %collective-permute-start.15) | collective-permute-done | bytes 589856 | tf_op jit(solution)/shard_map/ppermute | solution.py:19
  77.1 2.7 %collective-permute-start.18 = (bf16[128,1152]{1,0:T(8,128)(2,1)S(1)}, bf16[128,1152]{1,0:T(8,128)(2,1)S(1)}, u32[]{:S(2)}, u32[]{:S(2)}) collective-permute-start(bf16[128,1152]{1,0:T(8,128)(2,1)S(1)} %slice.52), channel_id=1, source_target_pairs={{0,24},{8,0},{16,8},{24,16},{1,25},{9,1},{17,9},{25,17},{2,26},{10... | collective-permute-start | bytes 884744 | tf_op jit(solution)/shard_map/ppermute | solution.py:19
  79.8 5.8 %collective-permute-done.16.refs_0_.refs_4_ = bf16[128,1152]{1,0:T(8,128)(2,1)S(1)} collective-permute-done((bf16[128,1152]{1,0:T(8,128)(2,1)S(1)}, bf16[128,1152]{1,0:T(8,128)(2,1)S(1)}, u32[]{:S(2)}, u32[]{:S(2)}) %collective-permute-start.16) | collective-permute-done | bytes 294944 | tf_op jit(solution)/shard_map/ppermute | solution.py:19
  85.6 1.5 %collective-permute-done.20.refs_6_ = bf16[4,4,16,1152]{3,2,1,0:T(8,128)(2,1)S(1)} collective-permute-done((bf16[4,4,16,1152]{3,2,1,0:T(8,128)(2,1)S(1)}, bf16[4,4,16,1152]{3,2,1,0:T(8,128)(2,1)S(1)}, u32[]{:S(2)}, u32[]{:S(2)}) %collective-permute-start.20) | collective-permute-done | bytes 589856 | tf_op jit(solution)/shard_map/ppermute | solution.py:19
  87.9 2.5 %collective-permute-start.24 = (f32[8,16,128]{2,1,0:T(8,128)S(1)}, f32[8,16,128]{2,1,0:T(8,128)S(1)}, u32[]{:S(2)}, u32[]{:S(2)}) collective-permute-start(f32[8,16,128]{2,1,0:T(8,128)S(1)} %get-tuple-element.31), channel_id=1, source_target_pairs={{0,32},{32,0},{1,33},{33,1},{2,34},{34,2},{3,35},{35,3},{4,36},{36... | collective-permute-start | bytes 196616 | tf_op jit(solution)/shard_map/ppermute | solution.py:19
  94.0 3.4 %all-to-all-start.1 = ((f32[8,4,16,128]{3,2,1,0:T(8,128)}), f32[8,4,16,128]{3,2,1,0:T(8,128)S(1)}, u32[]{:S(2)}, u32[]{:S(2)}) async-start(f32[8,4,16,128]{3,2,1,0:T(8,128)} %pad_maximum_fusion), calls=%async_computation.1 | async-start | bytes 524288 | tf_op jit(solution)/shard_map/all_to_all | solution.py:258
  97.5 12.3 %all-to-all-done.1 = f32[8,4,16,128]{3,2,1,0:T(8,128)S(1)} async-done(((f32[8,4,16,128]{3,2,1,0:T(8,128)}), f32[8,4,16,128]{3,2,1,0:T(8,128)S(1)}, u32[]{:S(2)}, u32[]{:S(2)}) %all-to-all-start.1) | async-done | bytes 262176 | tf_op jit(solution)/shard_map/all_to_all | solution.py:258
  (81 shorter events, 24.0 us)
Async XLA Ops:
  3.0 41.2 %all-to-all-start = ((bf16[8,4,16,1152]{3,2,1,0:T(8,128)(2,1)}), bf16[8,4,16,1152]{3,2,1,0:T(8,128)(2,1)S(1)}, u32[]{:S(2)}, u32[]{:S(2)}) async-start(bf16[8,4,16,1152]{3,2,1,0:T(8,128)(2,1)} %shard_map.93), calls=%async_computation | async-start | bytes 2359296 | tf_op jit(solution)/shard_map/all_to_all | solution.py:208
  14.3 3.9 %collective-permute-start.3 = (f32[18,128]{1,0:T(8,128)S(1)}, f32[18,128]{1,0:T(8,128)S(1)}, u32[]{:S(2)}, u32[]{:S(2)}) collective-permute-start(f32[18,128]{1,0:T(8,128)S(1)} %bitcast_add_fusion.1), channel_id=1, source_target_pairs={{0,192},{64,0},{128,64},{192,128},{1,193},{65,1},{129,65},{193,129... | collective-permute-start | bytes 27656 | tf_op jit(solution)/shard_map/ppermute | solution.py:19
  16.8 4.3 %collective-permute-start.2 = (f32[18,128]{1,0:T(8,128)S(1)}, f32[18,128]{1,0:T(8,128)S(1)}, u32[]{:S(2)}, u32[]{:S(2)}) collective-permute-start(f32[18,128]{1,0:T(8,128)S(1)} %bitcast_add_fusion.1), channel_id=1, source_target_pairs={{0,128},{64,192},{128,0},{192,64},{1,129},{65,193},{129,1},{193,65... | collective-permute-start | bytes 27656 | tf_op jit(solution)/shard_map/ppermute | solution.py:19
  17.3 4.1 %collective-permute-start.1 = (f32[18,128]{1,0:T(8,128)S(1)}, f32[18,128]{1,0:T(8,128)S(1)}, u32[]{:S(2)}, u32[]{:S(2)}) collective-permute-start(f32[18,128]{1,0:T(8,128)S(1)} %bitcast_add_fusion.1), channel_id=1, source_target_pairs={{0,64},{64,128},{128,192},{192,0},{1,65},{65,129},{129,193},{193,1... | collective-permute-start | bytes 27656 | tf_op jit(solution)/shard_map/ppermute | solution.py:19
  24.3 4.0 %collective-permute-start.5 = (f32[4,2,128]{2,1,0:T(2,128)S(1)}, f32[4,2,128]{2,1,0:T(2,128)S(1)}, u32[]{:S(2)}, u32[]{:S(2)}) collective-permute-start(f32[4,2,128]{2,1,0:T(2,128)S(1)} %pad_maximum_fusion.1), channel_id=1, source_target_pairs={{0,64},{64,128},{128,192},{192,0},{1,65},{65,129},{129,193},{193,1... | collective-permute-start | bytes 12296 | tf_op jit(solution)/shard_map/ppermute | solution.py:19
  24.4 4.2 %collective-permute-start.6 = (f32[4,2,128]{2,1,0:T(2,128)S(1)}, f32[4,2,128]{2,1,0:T(2,128)S(1)}, u32[]{:S(2)}, u32[]{:S(2)}) collective-permute-start(f32[4,2,128]{2,1,0:T(2,128)S(1)} %pad_maximum_fusion.1), channel_id=1, source_target_pairs={{0,128},{64,192},{128,0},{192,64},{1,129},{65,193},{129,1},{193,65... | collective-permute-start | bytes 12296 | tf_op jit(solution)/shard_map/ppermute | solution.py:19
  25.7 3.2 %collective-permute-start.7 = (f32[4,2,128]{2,1,0:T(2,128)S(1)}, f32[4,2,128]{2,1,0:T(2,128)S(1)}, u32[]{:S(2)}, u32[]{:S(2)}) collective-permute-start(f32[4,2,128]{2,1,0:T(2,128)S(1)} %pad_maximum_fusion.1), channel_id=1, source_target_pairs={{0,192},{64,0},{128,64},{192,128},{1,193},{65,1},{129,65},{193,129... | collective-permute-start | bytes 12296 | tf_op jit(solution)/shard_map/ppermute | solution.py:19
  29.1 2.9 %collective-permute-start.8 = (f32[24,128]{1,0:T(8,128)S(1)}, f32[24,128]{1,0:T(8,128)S(1)}, u32[]{:S(2)}, u32[]{:S(2)}) collective-permute-start(f32[24,128]{1,0:T(8,128)S(1)} %maximum_maximum_fusion), channel_id=1, source_target_pairs={{0,8},{8,0},{16,24},{24,16},{1,9},{9,1},{17,25},{25,17},{2,10},{10... | collective-permute-start | bytes 36872 | tf_op jit(solution)/shard_map/ppermute | solution.py:24
  32.0 4.3 %collective-permute-start.9 = (f32[24,128]{1,0:T(8,128)S(1)}, f32[24,128]{1,0:T(8,128)S(1)}, u32[]{:S(2)}, u32[]{:S(2)}) collective-permute-start(f32[24,128]{1,0:T(8,128)S(1)} %fusion.3), channel_id=1, source_target_pairs={{0,16},{8,24},{16,0},{24,8},{1,17},{9,25},{17,1},{25,9},{2,18},{10... | collective-permute-start | bytes 36872 | tf_op jit(solution)/shard_map/ppermute | solution.py:24
  36.4 3.7 %collective-permute-start.10 = (f32[24,128]{1,0:T(8,128)S(1)}, f32[24,128]{1,0:T(8,128)S(1)}, u32[]{:S(2)}, u32[]{:S(2)}) collective-permute-start(f32[24,128]{1,0:T(8,128)S(1)} %add.64), channel_id=1, source_target_pairs={{0,1},{1,0},{2,3},{3,2},{4,5},{5,4},{6,7},{7,6},{8,9},{9,8},{10,11... | collective-permute-start | bytes 36872 | tf_op jit(solution)/shard_map/ppermute | solution.py:24
  44.2 28.1 %collective-permute-start.19 = (bf16[8,4,16,1152]{3,2,1,0:T(8,128)(2,1)S(1)}, bf16[8,4,16,1152]{3,2,1,0:T(8,128)(2,1)S(1)}, u32[]{:S(2)}, u32[]{:S(2)}) collective-permute-start(bf16[8,4,16,1152]{3,2,1,0:T(8,128)(2,1)S(1)} %all-to-all-done.refs_4_.refs_2_), channel_id=1, source_target_pairs={{0,64},{64,128},{128,192},{192,0},{1,65},{65,129},{129,193},{193,1... | collective-permute-start | bytes 3538952 | tf_op jit(solution)/shard_map/ppermute | solution.py:19
  45.4 27.1 %collective-permute-start.21 = (bf16[8,4,16,1152]{3,2,1,0:T(8,128)(2,1)S(1)}, bf16[8,4,16,1152]{3,2,1,0:T(8,128)(2,1)S(1)}, u32[]{:S(2)}, u32[]{:S(2)}) collective-permute-start(bf16[8,4,16,1152]{3,2,1,0:T(8,128)(2,1)S(1)} %all-to-all-done.refs_4_.refs_2_), channel_id=1, source_target_pairs={{0,192},{64,0},{128,64},{192,128},{1,193},{65,1},{129,65},{193,129... | collective-permute-start | bytes 3538952 | tf_op jit(solution)/shard_map/ppermute | solution.py:19
  46.9 6.5 %collective-permute-start.12 = (f32[24,128]{1,0:T(8,128)S(1)}, f32[24,128]{1,0:T(8,128)S(1)}, u32[]{:S(2)}, u32[]{:S(2)}) collective-permute-start(f32[24,128]{1,0:T(8,128)S(1)} %add.65), channel_id=1, source_target_pairs={{0,4},{1,5},{2,6},{3,7},{4,0},{5,1},{6,2},{7,3},{8,12},{9,13},{10,... | collective-permute-start | bytes 36872 | tf_op jit(solution)/shard_map/ppermute | solution.py:28
  47.6 5.8 %collective-permute-start.13 = (f32[24,128]{1,0:T(8,128)S(1)}, f32[24,128]{1,0:T(8,128)S(1)}, u32[]{:S(2)}, u32[]{:S(2)}) collective-permute-start(f32[24,128]{1,0:T(8,128)S(1)} %add.65), channel_id=1, source_target_pairs={{0,6},{1,7},{2,4},{3,5},{4,2},{5,3},{6,0},{7,1},{8,14},{9,15},{10,... | collective-permute-start | bytes 36872 | tf_op jit(solution)/shard_map/ppermute | solution.py:28
  48.5 5.4 %collective-permute-start.11 = (f32[24,128]{1,0:T(8,128)S(1)}, f32[24,128]{1,0:T(8,128)S(1)}, u32[]{:S(2)}, u32[]{:S(2)}) collective-permute-start(f32[24,128]{1,0:T(8,128)S(1)} %add.65), channel_id=1, source_target_pairs={{0,2},{1,3},{2,0},{3,1},{4,6},{5,7},{6,4},{7,5},{8,10},{9,11},{10,... | collective-permute-start | bytes 36872 | tf_op jit(solution)/shard_map/ppermute | solution.py:28
  55.2 5.7 %collective-permute-start.14 = (bf16[128,1152]{1,0:T(8,128)(2,1)S(1)}, bf16[128,1152]{1,0:T(8,128)(2,1)S(1)}, u32[]{:S(2)}, u32[]{:S(2)}) collective-permute-start(bf16[128,1152]{1,0:T(8,128)(2,1)S(1)} %get-tuple-element.22), channel_id=1, source_target_pairs={{0,32},{32,0},{1,33},{33,1},{2,34},{34,2},{3,35},{35,3},{4,36},{36... | collective-permute-start | bytes 884744 | tf_op jit(solution)/shard_map/ppermute | solution.py:19
  60.9 16.0 %collective-permute-start.15 = (bf16[256,1152]{1,0:T(8,128)(2,1)S(1)}, bf16[256,1152]{1,0:T(8,128)(2,1)S(1)}, u32[]{:S(2)}, u32[]{:S(2)}) collective-permute-start(bf16[256,1152]{1,0:T(8,128)(2,1)S(1)} %constant_dynamic-update-slice_fusion), channel_id=1, source_target_pairs={{0,8},{8,16},{16,24},{24,0},{1,9},{9,17},{17,25},{25,1},{2,10},{10... | collective-permute-start | bytes 1769480 | tf_op jit(solution)/shard_map/ppermute | solution.py:19
  62.3 14.7 %collective-permute-start.17 = (bf16[256,1152]{1,0:T(8,128)(2,1)S(1)}, bf16[256,1152]{1,0:T(8,128)(2,1)S(1)}, u32[]{:S(2)}, u32[]{:S(2)}) collective-permute-start(bf16[256,1152]{1,0:T(8,128)(2,1)S(1)} %constant_dynamic-update-slice_fusion), channel_id=1, source_target_pairs={{0,24},{8,0},{16,8},{24,16},{1,25},{9,1},{17,9},{25,17},{2,26},{10... | collective-permute-start | bytes 1769480 | tf_op jit(solution)/shard_map/ppermute | solution.py:19
  72.4 14.7 %collective-permute-start.20 = (bf16[4,4,16,1152]{3,2,1,0:T(8,128)(2,1)S(1)}, bf16[4,4,16,1152]{3,2,1,0:T(8,128)(2,1)S(1)}, u32[]{:S(2)}, u32[]{:S(2)}) collective-permute-start(bf16[4,4,16,1152]{3,2,1,0:T(8,128)(2,1)S(1)} %slice.53), channel_id=1, source_target_pairs={{0,64},{64,128},{128,192},{192,0},{1,65},{65,129},{129,193},{193,1... | collective-permute-start | bytes 1769480 | tf_op jit(solution)/shard_map/ppermute | solution.py:19
  72.6 14.5 %collective-permute-start.22 = (bf16[4,4,16,1152]{3,2,1,0:T(8,128)(2,1)S(1)}, bf16[4,4,16,1152]{3,2,1,0:T(8,128)(2,1)S(1)}, u32[]{:S(2)}, u32[]{:S(2)}) collective-permute-start(bf16[4,4,16,1152]{3,2,1,0:T(8,128)(2,1)S(1)} %slice.54), channel_id=1, source_target_pairs={{0,192},{64,0},{128,64},{192,128},{1,193},{65,1},{129,65},{193,129... | collective-permute-start | bytes 1769480 | tf_op jit(solution)/shard_map/ppermute | solution.py:19
  76.9 8.7 %collective-permute-start.16 = (bf16[128,1152]{1,0:T(8,128)(2,1)S(1)}, bf16[128,1152]{1,0:T(8,128)(2,1)S(1)}, u32[]{:S(2)}, u32[]{:S(2)}) collective-permute-start(bf16[128,1152]{1,0:T(8,128)(2,1)S(1)} %slice.51), channel_id=1, source_target_pairs={{0,8},{8,16},{16,24},{24,0},{1,9},{9,17},{17,25},{25,1},{2,10},{10... | collective-permute-start | bytes 884744 | tf_op jit(solution)/shard_map/ppermute | solution.py:19
  77.1 8.5 %collective-permute-start.18 = (bf16[128,1152]{1,0:T(8,128)(2,1)S(1)}, bf16[128,1152]{1,0:T(8,128)(2,1)S(1)}, u32[]{:S(2)}, u32[]{:S(2)}) collective-permute-start(bf16[128,1152]{1,0:T(8,128)(2,1)S(1)} %slice.52), channel_id=1, source_target_pairs={{0,24},{8,0},{16,8},{24,16},{1,25},{9,1},{17,9},{25,17},{2,26},{10... | collective-permute-start | bytes 884744 | tf_op jit(solution)/shard_map/ppermute | solution.py:19
  87.9 4.0 %collective-permute-start.24 = (f32[8,16,128]{2,1,0:T(8,128)S(1)}, f32[8,16,128]{2,1,0:T(8,128)S(1)}, u32[]{:S(2)}, u32[]{:S(2)}) collective-permute-start(f32[8,16,128]{2,1,0:T(8,128)S(1)} %get-tuple-element.31), channel_id=1, source_target_pairs={{0,32},{32,0},{1,33},{33,1},{2,34},{34,2},{3,35},{35,3},{4,36},{36... | collective-permute-start | bytes 196616 | tf_op jit(solution)/shard_map/ppermute | solution.py:19
  94.0 15.7 %all-to-all-start.1 = ((f32[8,4,16,128]{3,2,1,0:T(8,128)}), f32[8,4,16,128]{3,2,1,0:T(8,128)S(1)}, u32[]{:S(2)}, u32[]{:S(2)}) async-start(f32[8,4,16,128]{3,2,1,0:T(8,128)} %pad_maximum_fusion), calls=%async_computation.1 | async-start | bytes 524288 | tf_op jit(solution)/shard_map/all_to_all | solution.py:258
  (9 other events, 97.7 us)
